TPU v7x, 128 devices: a whole 4x4x4 slice. The times are simulated.
128 devices in a mesh: gx: 8 (over z, x_hi), gy: 8 (over y, core), gz: 2 (over x_lo).
Axes of the slice: x: 4 (x_hi: 2, x_lo: 2; x = x_hi * 2 + x_lo), y: 4, z: 4, core: 2. Of those that a mesh axis runs over, the one named last changes fastest.
Arguments:
- populations: float32 [27, 32, 64, 512], P(None, 'gx', 'gy', 'gz'), may hold values from 0 to 1, as said below
- blockage: float32 [32, 64, 512], P('gx', 'gy', 'gz'), may hold values from 0.02 to 0.4
- solid_mask: int32 [32, 64, 512], P('gx', 'gy', 'gz'), may hold values 0 or 1
- cotangent: float32 [27, 32, 64, 512], P(None, 'gx', 'gy', 'gz'), may hold values from -6 to 6
Outputs:
- adjoint_start: float32 [27, 32, 64, 512], P(None, 'gx', 'gy', 'gz')
- grad_blockage: float32 [32, 64, 512], P('gx', 'gy', 'gz')
Inputs may be any that keep to these rules, and one draw needn't show every extreme that they name: `populations`: every population is positive.
All inputs are finite; a program needn't handle non-finite values. No bound on the sum of `solid_mask` on one device may be relied on, other than what follows from the above.
Results may differ from a plain program's by a relative error of at most 0.0003.
Values sent between devices are 32-bit elements; how exact they have to be, the bound alone decides.
No kernel may reach another device: no remote copies, remote signals or barrier semaphores. Data moves between devices by JAX's collectives and lax.ppermute only.
A program may use at most 128 MiB of HBM per device.

v0:
```python
import functools
import jax
import jax.numpy as jnp
from jax import lax
from jax.experimental import pallas as pl
from jax.experimental.pallas import tpu as pltpu
from jax.sharding import PartitionSpec as P

DIRS = [(a, b, d) for a in (-1, 0, 1) for b in (-1, 0, 1) for d in (-1, 0, 1)]
WEIGHTS = [(8.0 / 27.0, 2.0 / 27.0, 1.0 / 54.0, 1.0 / 216.0)[abs(a) + abs(b) + abs(d)] for a, b, d in DIRS]
OMEGA = 1.25
NT = 17
ROWS = NT * 8
MINI = pl.ds(128, 8)
F32 = jnp.float32


def tile(n):
    return pl.ds(n * 8, 8) if isinstance(n, int) else pl.ds(pl.multiple_of(n * 8, 8), 8)


def lanes():
    return lax.broadcasted_iota(jnp.int32, (8, 128), 1)


def subs():
    return lax.broadcasted_iota(jnp.int32, (8, 128), 0)


def roll_l(v, k):
    return pltpu.roll(v, k, 1)


def roll_s(v, k):
    return pltpu.roll(v, k, 0)


def mod128(k):
    return lax.rem(k + 256, 128)


def sides(axis):
    parity = lax.rem(lax.axis_index(axis), 2)
    return (1 - 2 * parity, 2 * parity - 1)


def moments(f):
    rho = f[13]
    mom = [None, None, None]
    for i in range(13):
        plus, minus = f[i] + f[26 - i], f[26 - i] - f[i]
        rho = rho + plus
        for k in range(3):
            c = DIRS[26 - i][k]
            if c:
                term = minus if c > 0 else -minus
                mom[k] = term if mom[k] is None else (mom[k] + minus if c > 0 else mom[k] - minus)
    inv = 1.0 / rho
    return rho, [m * inv for m in mom]


def dot_c(vec, comps):
    out = None
    for c, v in zip(vec, comps):
        if c:
            if out is None:
                out = v if c > 0 else -v
            else:
                out = out + v if c > 0 else out - v
    return out


def collide(f, solid, rho, u):
    fluid = 1.0 - solid
    own = (1.0 - OMEGA) * fluid
    base = OMEGA * fluid * rho
    rest = base * (1.0 - 1.5 * (u[0] * u[0] + u[1] * u[1] + u[2] * u[2]))
    out = [None] * 27
    for i in range(13):
        j = 26 - i
        w = WEIGHTS[i]
        cu = dot_c(DIRS[j], u)
        bc = base * cu
        even = w * (rest + 4.5 * (bc * cu))
        odd = (3.0 * w) * bc
        out[j] = own * f[j] + solid * f[i] + (even + odd)
        out[i] = own * f[i] + solid * f[j] + (even - odd)
    out[13] = (own + solid) * f[13] + WEIGHTS[13] * rest
    return out


def pull_back(p, solid, u, f=None, rho=None):
    w0 = WEIGHTS[13] * p[13]
    w1 = [None] * 3
    w2 = {}
    add = lambda x, y: y if x is None else x + y
    by_class = {}
    for i in range(13):
        j = 26 - i
        plus, minus = WEIGHTS[i] * (p[j] + p[i]), WEIGHTS[i] * (p[j] - p[i])
        w0 = w0 + plus
        c = DIRS[j]
        for k in range(3):
            if c[k]:
                w1[k] = add(w1[k], minus if c[k] > 0 else -minus)
            for m in range(k, 3):
                cc = c[k] * c[m]
                if cc:
                    w2[(k, m)] = add(w2.get((k, m)), plus if cc > 0 else -plus)
    at = lambda k, m: w2[(min(k, m), max(k, m))]
    w2u = [at(k, 0) * u[0] + at(k, 1) * u[1] + at(k, 2) * u[2] for k in range(3)]
    uwu = u[0] * w2u[0] + u[1] * w2u[1] + u[2] * w2u[2]
    uu = u[0] * u[0] + u[1] * u[1] + u[2] * u[2]
    fluid = 1.0 - solid
    own = (1.0 - OMEGA) * fluid
    gain = OMEGA * fluid
    g_rho = gain * (w0 * (1.0 + 1.5 * uu) - 4.5 * uwu)
    g_mom = [gain * (3.0 * w1[k] + 9.0 * w2u[k] - 3.0 * (u[k] * w0)) for k in range(3)]
    out = [None] * 27
    for i in range(13):
        j = 26 - i
        odd = dot_c(DIRS[j], g_mom)
        out[j] = own * p[j] + solid * p[i] + (g_rho + odd)
        out[i] = own * p[i] + solid * p[j] + (g_rho - odd)
    out[13] = (own + solid) * p[13] + g_rho
    if f is None:
        return out, None
    blame = OMEGA * (p[13] * f[13])
    for i in range(13):
        j = 26 - i
        blame = blame + (p[i] * (f[j] - (1.0 - OMEGA) * f[i]) + p[j] * (f[i] - (1.0 - OMEGA) * f[j]))
    w1u = w1[0] * u[0] + w1[1] * u[1] + w1[2] * u[2]
    blame = blame - (OMEGA * rho) * (w0 * (1.0 - 1.5 * uu) + 3.0 * w1u + 4.5 * uwu)
    return out, blame


def stream_main(own, yh, out_own, out_yh, orient, gz, low, high, put):
    lane, sub = lanes(), subs()
    floor = (lane == 0) & (gz == 0)
    roof = (lane == 127) & (gz == 1)

    def body(x, carry):
        for a in (-1, 0, 1):
            for b in (-1, 0, 1):
                xs = x - orient * a
                bp = orient * b
                both = out_yh is not None
                need = both or bp != 0
                into = 9 * (a + 1) + 3 * (b + 1) + 1 + orient * (2 * gz - 1)
                shift = 127 - 2 * gz - 4 * xs
                ins_own = roll_l(own[into, MINI, :], shift)
                ins_yh = roll_l(yh[into, MINI, :], shift) if need else None
                for d in (-1, 0, 1):
                    i = 9 * (a + 1) + 3 * (b + 1) + d + 1
                    dp = orient * d

                    def shifted(ref, ins):
                        t0, t1 = ref[i, tile(2 * xs), :], ref[i, tile(2 * xs + 1), :]
                        if dp == 1:
                            return (jnp.where(lane == 0, ins, roll_l(t0, 1)), roll_l(jnp.where(lane == 127, t0, t1), 1))
                        if dp == -1:
                            return (roll_l(jnp.where(lane == 0, t1, t0), 127), jnp.where(lane == 127, ins, roll_l(t1, 127)))
                        return t0, t1

                    mine = shifted(own, ins_own)
                    halo = shifted(yh, ins_yh) if need else (None, None)
                    for half in (0, 1):
                        vo, vy = mine[half], halo[half]
                        ny = vy
                        if bp == 1:
                            no = roll_s(jnp.where(sub == 7, vy, vo), 1)
                            if both:
                                ny = roll_s(jnp.where(sub == 7, vo, vy), 1)
                        elif bp == -1:
                            no = roll_s(jnp.where(sub == 0, vy, vo), 7)
                            if both:
                                ny = roll_s(jnp.where(sub == 0, vo, vy), 7)
                        else:
                            no = vo
                        wall = floor if (dp == 1 and half == 0) else roof if (dp == -1 and half == 1) else None
                        here = tile(2 * x + half)
                        if wall is not None:
                            no = jnp.where(wall, own[26 - i, here, :], no)
                            if both:
                                ny = jnp.where(wall, yh[26 - i, here, :], ny)
                        put(out_own, i, x, half, no)
                        if both:
                            out_yh[i, here, :] = ny
        return carry

    lax.fori_loop(low, high, body, 0)


def put_tile(ref, i, x, half, value):
    ref[i, tile(2 * x + half), :] = value


def stream_mini(own, yh, out_own, out_yh, orient, gz):
    lane, sub = lanes(), subs()
    slot = lax.rem(lane, 4)
    edge = 1 - gz
    for a in (-1, 0, 1):
        for b in (-1, 0, 1):
            bp = orient * b
            both = out_yh is not None
            need = both or bp != 0
            outof = 9 * (a + 1) + 3 * (b + 1) + 1 + orient * (1 - 2 * gz)

            def rim(ref):
                acc = jnp.zeros((8, 128), F32)
                for xe in range(8):
                    src = ref[outof, tile(2 * xe + edge), :]
                    acc = jnp.where(lane == 4 * xe + 3 * gz, roll_l(src, 4 * xe + 1 + 2 * gz), acc)
                return acc

            rim_own = rim(own)
            rim_yh = rim(yh) if need else None
            for d in (-1, 0, 1):
                i = 9 * (a + 1) + 3 * (b + 1) + d + 1
                dp = orient * d
                ap = orient * a

                def shifted(ref, edge_values):
                    v = ref[i, MINI, :]
                    if dp == 1:
                        v = jnp.where(slot == 0, edge_values, roll_l(v, 1))
                    if dp == -1:
                        v = jnp.where(slot == 3, edge_values, roll_l(v, 127))
                    if ap:
                        v = roll_l(v, (4 * ap) % 128)
                    return v

                vo = shifted(own, rim_own)
                vy = shifted(yh, rim_yh) if need else None
                ny = vy
                if bp == 1:
                    no = roll_s(jnp.where(sub == 7, vy, vo), 1)
                    if both:
                        ny = roll_s(jnp.where(sub == 7, vo, vy), 1)
                elif bp == -1:
                    no = roll_s(jnp.where(sub == 0, vy, vo), 7)
                    if both:
                        ny = roll_s(jnp.where(sub == 0, vo, vy), 7)
                else:
                    no = vo
                out_own[i, MINI, :] = no
                if both:
                    out_yh[i, MINI, :] = ny


def entries(e, orient, stride):
    others = [(r // 3) * 3 + r % 3 if stride == 9 else (r // 3) * 9 + r % 3 for r in range(9)]
    inward, outward = stride * (orient * e + 1), stride * (1 - orient * e)
    out = [(inward + c, 1, None, 0) for c in others]
    out += [(stride + c, 1, None, 0) for c in others]
    out += [(inward + c, 2, outward + c, orient * (r % 3 - 1)) for r, c in enumerate(others)]
    return out


def wall_masks(gz, by_half):
    lane, half = lanes(), lax.rem(subs(), 2)
    floor, roof = (lane == 0) & (gz == 0), (lane == 127) & (gz == 1)
    if by_half:
        return {-1: floor & (half == 0), 1: roof & (half == 1)}
    return {-1: floor, 1: roof}


def pack_x(msg, e, orient, gz, pops, adj=None, solid=None):
    near = 2 + 3 * ((e + 1) // 2)
    walls = wall_masks(gz, False)
    lane = lanes()
    items = [(pops, i, near if layer == 1 else near - e, st, dp) for i, layer, st, dp in entries(e, orient, 9)]
    if adj is not None:
        items += [(adj, 9 * (1 - e) + c, near, None, 0) for c in range(9)]
        items += [(solid, 0, near, None, 0)]
    strip = [jnp.zeros((8, 128), F32) for _ in range((len(items) + 31) // 32)]
    for k, (ref, i, plane, stash, dp) in enumerate(items):
        for half in (0, 1):
            v = ref[i, tile(2 * plane + half), :]
            if stash is not None and ((dp == -1 and half == 0) or (dp == 1 and half == 1)):
                v = jnp.where(walls[dp], ref[stash, tile(2 * near + half), :], v)
            msg[(2 * k + half) * 8 : (2 * k + half) * 8 + 8, :] = v
        s = 4 * (k % 32)
        moved = roll_l(ref[i, MINI, :], mod128(s - 4 * plane))
        strip[k // 32] = jnp.where((lane >= s) & (lane < s + 4), moved, strip[k // 32])
    for n, v in enumerate(strip):
        r = (2 * len(items) + n) * 8
        msg[r : r + 8, :] = v


def unpack_x(msg, s, orient, pops, adj=None, solid=None):
    near = 2 + 3 * ((s + 1) // 2) + s
    e = -s
    lane = lanes()
    plane_of = lax.div(lane, 4)
    outward = 9 * (1 - orient * e)
    items = [(pops, i, near if layer == 1 else near + s, st) for i, layer, st, _ in entries(e, orient, 9)]
    if adj is not None:
        items += [(adj, 9 * (1 - e) + c, near, None) for c in range(9)]
        items += [(solid, 0, near, None)]
    for k, (ref, i, plane, stash) in enumerate(items):
        for half in (0, 1):
            v = msg[(2 * k + half) * 8 : (2 * k + half) * 8 + 8, :]
            ref[i, tile(2 * plane + half), :] = v
            if stash is not None:
                ref[stash, tile(2 * near + half), :] = v
        r = (2 * len(items) + k // 32) * 8
        moved = roll_l(msg[r : r + 8, :], mod128(4 * plane - 4 * (k % 32)))
        ref[i, MINI, :] = jnp.where(plane_of == plane, moved, ref[i, MINI, :])


def pack_y(msg, e, orient, gz, pops, adj=None, solid=None):
    near = 7 * ((e + 1) // 2)
    walls = wall_masks(gz, True)
    items = [(pops, i, near if layer == 1 else near - e, st, dp) for i, layer, st, dp in entries(e, orient, 3)]
    if adj is not None:
        items += [(adj, 3 * (1 - e) + c, near, None, 0) for c in Y_OTHERS]
        items += [(solid, 0, near, None, 0)]
    for k, (ref, i, row, stash, dp) in enumerate(items):
        for part in (0, 1):
            v = ref[i, pl.ds(64 * part + row, 8, stride=8), :]
            if dp:
                v = jnp.where(walls[dp], ref[stash, pl.ds(64 * part + near, 8, stride=8), :], v)
            msg[(2 * k + part) * 8 : (2 * k + part) * 8 + 8, :] = v
        msg[16 * len(items) + k : 16 * len(items) + k + 1, :] = ref[i, pl.ds(128 + row, 1), :]


Y_OTHERS = [(r // 3) * 9 + r % 3 for r in range(9)]


def unpack_y(msg, s, orient, pops, adj=None, solid=None):
    near = 7 * ((1 - s) // 2)
    e = -s
    items = [(pops, i, near if layer == 1 else near + s, st) for i, layer, st, _ in entries(e, orient, 3)]
    if adj is not None:
        items += [(adj, 3 * (1 - e) + c, near, None) for c in Y_OTHERS]
        items += [(solid, 0, near, None)]
    for k, (ref, i, row, stash) in enumerate(items):
        for part in (0, 1):
            v = msg[(2 * k + part) * 8 : (2 * k + part) * 8 + 8, :]
            ref[i, pl.ds(64 * part + row, 8, stride=8), :] = v
            if stash is not None:
                ref[stash, pl.ds(64 * part + near, 8, stride=8), :] = v
        ref[i, pl.ds(128 + row, 1), :] = msg[16 * len(items) + k : 16 * len(items) + k + 1, :]


def solid_of(blockage, mask):
    m = mask.astype(F32)
    return blockage * (1.0 - m) + m


def cut_kernel(pops, block, mask, cot, msg):
    gz = lax.axis_index("gz")
    lane = lanes()
    top = gz == 0
    for n in range(7):
        acc = jnp.zeros((8, 128), F32)
        for j in range(8):
            slot = 8 * n + j
            if slot > 54:
                break
            for x in range(4):
                if slot == 54:
                    hi = solid_of(block[x, :, 128:256], mask[x, :, 128:256])
                    lo = solid_of(block[x, :, 0:128], mask[x, :, 0:128])
                else:
                    ref, i = (pops, slot) if slot < 27 else (cot, slot - 27)
                    hi, lo = ref[i, x, :, 128:256], ref[i, x, :, 0:128]
                at = 16 * j + 4 * x
                moved = roll_l(jnp.where(top, hi, lo), mod128(at + 4 - 4 * gz))
                acc = jnp.where((lane >= at) & (lane < at + 4), moved, acc)
        msg[8 * n : 8 * n + 8, :] = acc


def first_kernel(pops, block, mask, cot, cut, tx, ax, sx, msg0, msg1):
    gz = lax.axis_index("gz")

    def body(x, carry):
        for half in (0, 1):
            z = pl.ds(128 * half, 128)
            here = tile(2 * (x + 2) + half)
            s = solid_of(block[x, :, z], mask[x, :, z])
            sx[0, here, :] = s
            f = [pops[i, x, :, z] for i in range(27)]
            rho, u = moments(f)
            out = collide(f, s, rho, u)
            for i in range(27):
                tx[i, here, :] = out[i]
                ax[i, here, :] = cot[i, x, :, z]
        return carry

    lax.fori_loop(0, 4, body, 0)

    def slot(n):
        return roll_l(cut[8 * (n // 8) : 8 * (n // 8) + 8, :], (8 - 16 * (n % 8)) % 128)

    s = slot(54)
    sx[0, MINI, :] = s
    f = [slot(i) for i in range(27)]
    rho, u = moments(f)
    out = collide(f, s, rho, u)
    for i in range(27):
        tx[i, MINI, :] = out[i]
        ax[i, MINI, :] = slot(27 + i)
    for msg, e in zip((msg0, msg1), sides("gx")):
        pack_x(msg, e, 1, gz, tx, ax, sx)


def carry_over(pairs):
    def body(k, carry):
        here = tile(jnp.where(k == 8, 16, k + 4))
        for src, dst in pairs:
            for i in range(src.shape[0]):
                dst[i, here, :] = src[i, here, :]
        return carry

    lax.fori_loop(0, 9, body, 0)


def span_kernel(tx_in, ax_in, sx_in, got0, got1, tx, ax, sx, msg0, msg1):
    gz = lax.axis_index("gz")
    carry_over(((tx_in, tx), (ax_in, ax), (sx_in, sx)))
    for msg, s in zip((got0, got1), sides("gx")):
        unpack_x(msg, s, 1, tx, ax, sx)
    for msg, e in zip((msg0, msg1), sides("gy")):
        pack_y(msg, e, 1, gz, tx, ax, sx)


def span_kernel_2(tx_in, got0, got1, tx, msg0, msg1):
    gz = lax.axis_index("gz")
    carry_over(((tx_in, tx),))
    for msg, s in zip((got0, got1), sides("gx")):
        unpack_x(msg, s, -1, tx)
    for msg, e in zip((msg0, msg1), sides("gy")):
        pack_y(msg, e, -1, gz, tx)


def put_own(ref, i, x, half, value):
    ref[i, tile(2 * (x - 2) + half), :] = value


def middle_kernel(tx, ax, sx, got0, got1, a2, f1, u_own, u_yh, sy, q2, msg0, msg1, ty, ay, f_own, f_yh, c_own, c_yh, p_own):
    gz = lax.axis_index("gz")
    for msg, s in zip((got0, got1), sides("gy")):
        unpack_y(msg, s, 1, ty, ay, sy)
    stream_main(tx, ty, f_own, f_yh, 1, gz, 1, 7, put_tile)
    stream_mini(tx, ty, f_own, f_yh, 1, gz)

    def again(k, carry):
        n = jnp.where(k == 12, 16, k + 2)
        here = tile(n)
        for src, sol, dst, us in ((f_own, sx, c_own, u_own), (f_yh, sy, c_yh, u_yh)):
            f = [src[i, here, :] for i in range(27)]
            rho, u = moments(f)
            us[0, here, :] = rho
            for c in range(3):
                us[c + 1, here, :] = u[c]
            out = collide(f, sol[0, here, :], rho, u)
            for i in range(27):
                dst[i, here, :] = out[i]
        return carry

    lax.fori_loop(0, 13, again, 0)

    def keep(n, carry):
        for i in range(27):
            f1[i, tile(n), :] = f_own[i, tile(n + 4), :]
        return carry

    lax.fori_loop(0, 8, keep, 0)
    stream_main(c_own, c_yh, f_own, None, 1, gz, 2, 6, put_tile)
    stream_mini(c_own, c_yh, f_own, None, 1, gz)
    stream_main(ax, ay, p_own, None, -1, gz, 2, 6, put_tile)
    stream_mini(ax, ay, p_own, None, -1, gz)

    def back(k, carry):
        n = jnp.where(k == 8, 16, k + 4)
        here = tile(n)
        f = [f_own[i, here, :] for i in range(27)]
        p = [p_own[i, here, :] for i in range(27)]
        rho, u = moments(f)
        out, blame = pull_back(p, sx[0, here, :], u, f, rho)
        for i in range(27):
            a2[i, here, :] = out[i]
        q2[tile(k), :] = blame
        return carry

    lax.fori_loop(0, 9, back, 0)
    for msg, e in zip((msg0, msg1), sides("gx")):
        pack_x(msg, e, -1, gz, a2)


def last_kernel(a2, pops, block, mask, f1, u_own, u_yh, sx, sy, q2, got0, got1, adjoint, grad, ty, p_own, p_yh, c_own, c_yh):
    gz = lax.axis_index("gz")
    for msg, s in zip((got0, got1), sides("gy")):
        unpack_y(msg, s, -1, ty)
    stream_main(a2, ty, p_own, p_yh, -1, gz, 1, 7, put_tile)
    stream_mini(a2, ty, p_own, p_yh, -1, gz)

    def again(k, carry):
        n = jnp.where(k == 12, 16, k + 2)
        here = tile(n)
        for src, sol, dst, us in ((p_own, sx, c_own, u_own), (p_yh, sy, c_yh, u_yh)):
            out, _ = pull_back([src[i, here, :] for i in range(27)], sol[0, here, :], [us[c, here, :] for c in (1, 2, 3)])
            for i in range(27):
                dst[i, here, :] = out[i]
        return carry

    lax.fori_loop(0, 13, again, 0)

    def first_blame(x, carry):
        for half in (0, 1):
            here = tile(2 * x + 4 + half)
            there = tile(2 * x + half)
            u = [u_own[c, here, :] for c in (1, 2, 3)]
            _, blame = pull_back([p_own[i, here, :] for i in range(27)], sx[0, here, :], u, [f1[i, there, :] for i in range(27)], u_own[0, here, :])
            grad[x, :, pl.ds(128 * half, 128)] = blame + q2[there, :]
        return carry

    lax.fori_loop(0, 4, first_blame, 0)
    stream_main(c_own, c_yh, p_own, None, -1, gz, 2, 6, put_tile)

    def back(x, carry):
        for half in (0, 1):
            z = pl.ds(128 * half, 128)
            here = tile(2 * x + 4 + half)
            f = [pops[i, x, :, z] for i in range(27)]
            rho, u = moments(f)
            out, blame = pull_back([p_own[i, here, :] for i in range(27)], sx[0, here, :], u, f, rho)
            for i in range(27):
                adjoint[i, x, :, z] = out[i]
            grad[x, :, z] = (1.0 - mask[x, :, z].astype(F32)) * (grad[x, :, z] + blame)
        return carry

    lax.fori_loop(0, 4, back, 0)


def call(kernel, outs, scratch=(), name=None):
    return pl.pallas_call(
        kernel,
        out_shape=[jax.ShapeDtypeStruct(s, F32) for s in outs],
        scratch_shapes=[pltpu.VMEM(s, F32) for s in scratch],
        compiler_params=pltpu.CompilerParams(vmem_limit_bytes=48 * 1024 * 1024),
        name=name,
    )


def swap(x, axis, odd):
    n = lax.axis_size(axis)
    pairs = [(i, (i ^ 1) if not odd else ((i + 1) % n if i % 2 else (i - 1) % n)) for i in range(n)]
    return lax.ppermute(x, axis, pairs)


BIG = (27, ROWS, 128)
ONE = (1, ROWS, 128)
X1 = ((2 * 37 + 2) * 8, 128)
Y1 = (37 * 16 + 40, 128)
X2 = ((2 * 27 + 1) * 8, 128)
Y2 = (27 * 16 + 32, 128)


def body(populations, blockage, solid_mask, cotangent):
    (cut,) = call(cut_kernel, [(56, 128)], name="cut")(populations, blockage, solid_mask, cotangent)
    cut = lax.ppermute(cut, "gz", [(0, 1), (1, 0)])
    tx, ax, sx, m0, m1 = call(first_kernel, [BIG, BIG, ONE, X1, X1], name="first")(populations, blockage, solid_mask, cotangent, cut)
    m0, m1 = swap(m0, "gx", False), swap(m1, "gx", True)
    tx, ax, sx, m0, m1 = call(span_kernel, [BIG, BIG, ONE, Y1, Y1], name="span")(tx, ax, sx, m0, m1)
    m0, m1 = swap(m0, "gy", False), swap(m1, "gy", True)
    a2, f1, u_own, u_yh, sy, q2, m0, m1 = call(
        middle_kernel,
        [BIG, (27, 64, 128), (4, ROWS, 128), (4, ROWS, 128), ONE, (72, 128), X2, X2],
        scratch=[BIG] * 7,
        name="middle",
    )(tx, ax, sx, m0, m1)
    m0, m1 = swap(m0, "gx", False), swap(m1, "gx", True)
    a2, m0, m1 = call(span_kernel_2, [BIG, Y2, Y2], name="span2")(a2, m0, m1)
    m0, m1 = swap(m0, "gy", False), swap(m1, "gy", True)
    adjoint, grad = call(last_kernel, [(27, 4, 8, 256), (4, 8, 256)], scratch=[BIG] * 5, name="last")(
        a2, populations, blockage, solid_mask, f1, u_own, u_yh, sx, sy, q2, m0, m1
    )
    return adjoint, grad


def solution(mesh):
    placed = (P(None, "gx", "gy", "gz"), P("gx", "gy", "gz"), P("gx", "gy", "gz"), P(None, "gx", "gy", "gz"))
    return jax.shard_map(
        body, mesh=mesh, in_specs=placed, out_specs=(P(None, "gx", "gy", "gz"), P("gx", "gy", "gz")), check_vma=False
    )
```

profile of v0, /device:TPU:0, one launch (start us, length us, event | category | flops | bytes accessed | tf_op | source)
XLA Modules:
  0.0 78.7 jit_solution(14875127043419354306)
XLA Ops:
  0.6 0.0 copy-start
  0.6 1.2 %copy-done = f32[27,4,8,256]{3,2,1,0:T(8,128)S(1)} copy-done((f32[27,4,8,256]{3,2,1,0:T(8,128)S(1)}, f32[27,4,8,256]{3,2,1,0:T(8,128)}, u32[]{:S(2)}) %copy-start) | copy-done | bytes 884760
  1.8 0.0 copy-start.2
  1.8 1.2 %copy-done.2 = f32[27,4,8,256]{3,2,1,0:T(8,128)S(1)} copy-done((f32[27,4,8,256]{3,2,1,0:T(8,128)S(1)}, f32[27,4,8,256]{3,2,1,0:T(8,128)}, u32[]{:S(2)}) %copy-start.2) | copy-done | bytes 884760
  3.0 0.0 copy-start.6
  3.0 0.8 copy-done.6
  3.7 0.0 copy-start.8
  3.7 0.8 copy-done.8
  4.5 0.3 cut.1
  4.8 1.7 %collective-permute-start = (f32[56,128]{1,0:T(8,128)S(1)}, f32[56,128]{1,0:T(8,128)S(1)}, u32[]{:S(2)}, u32[]{:S(2)}) collective-permute-start(f32[56,128]{1,0:T(8,128)S(1)} %cut.1), channel_id=1, source_target_pairs={{0,1},{1,0},{2,3},{3,2},{4,5},{5,4},{6,7},{7,6},{8,9},{9,8},{10,11... | collective-permute-start | bytes 86024 | tf_op jit(solution)/shard_map/ppermute | solution.py:564
  6.5 2.3 %collective-permute-done.cut = f32[56,128]{1,0:T(8,128)S(1)} collective-permute-done((f32[56,128]{1,0:T(8,128)S(1)}, f32[56,128]{1,0:T(8,128)S(1)}, u32[]{:S(2)}, u32[]{:S(2)}) %collective-permute-start) | collective-permute-done | bytes 28704 | tf_op jit(solution)/shard_map/ppermute | solution.py:564
  8.8 2.0 %first.1 = (f32[27,136,128]{2,1,0:T(8,128)S(1)}, f32[27,136,128]{2,1,0:T(8,128)}, f32[1,136,128]{2,1,0:T(8,128)S(1)}, f32[608,128]{1,0:T(8,128)S(1)}, f32[608,128]{1,0:T(8,128)S(1)}) custom-call(f32[27,4,8,256]{3,2,1,0:T(8,128)S(1)} %copy-done, f32[4,8,256]{2,1,0:T(8,128)S(1)} %copy-done.6, s32[4,8,256]{2,1,0:T(8,128)S(1)} %copy-done.8, ...), custom_call_target="tpu_custom_call" | custom-call | tf_op jit(solution)/shard_map/first/pallas_call | solution.py:565
  10.7 0.0 copy-start.5
  10.7 1.2 %copy-done.5 = f32[27,136,128]{2,1,0:T(8,128)} copy-done((f32[27,136,128]{2,1,0:T(8,128)}, f32[27,136,128]{2,1,0:T(8,128)S(1)}, u32[]{:S(2)}) %copy-start.5) | copy-done | bytes 1880088
  12.0 3.1 %collective-permute-start.1 = (f32[608,128]{1,0:T(8,128)S(1)}, f32[608,128]{1,0:T(8,128)S(1)}, u32[]{:S(2)}, u32[]{:S(2)}) collective-permute-start(f32[608,128]{1,0:T(8,128)S(1)} %get-tuple-element.26), channel_id=1, source_target_pairs={{0,16},{16,0},{32,48},{48,32},{64,80},{80,64},{96,112},{112,96},{1... | collective-permute-start | bytes 933896 | tf_op jit(solution)/shard_map/ppermute | solution.py:551
  15.1 4.0 %collective-permute-start.2 = (f32[608,128]{1,0:T(8,128)S(1)}, f32[608,128]{1,0:T(8,128)S(1)}, u32[]{:S(2)}, u32[]{:S(2)}) collective-permute-start(f32[608,128]{1,0:T(8,128)S(1)} %get-tuple-element.27), channel_id=1, source_target_pairs={{0,112},{16,32},{32,16},{48,64},{64,48},{80,96},{96,80},{112,0},{1... | collective-permute-start | bytes 933896 | tf_op jit(solution)/shard_map/ppermute | solution.py:551
  19.1 4.5 %collective-permute-done.1.got0 = f32[608,128]{1,0:T(8,128)S(1)} collective-permute-done((f32[608,128]{1,0:T(8,128)S(1)}, f32[608,128]{1,0:T(8,128)S(1)}, u32[]{:S(2)}, u32[]{:S(2)}) %collective-permute-start.1) | collective-permute-done | bytes 311328 | tf_op jit(solution)/shard_map/ppermute | solution.py:551
  23.6 8.1 %collective-permute-done.2.got1 = f32[608,128]{1,0:T(8,128)S(1)} collective-permute-done((f32[608,128]{1,0:T(8,128)S(1)}, f32[608,128]{1,0:T(8,128)S(1)}, u32[]{:S(2)}, u32[]{:S(2)}) %collective-permute-start.2) | collective-permute-done | bytes 311328 | tf_op jit(solution)/shard_map/ppermute | solution.py:551
  31.6 2.8 %span.1 = (f32[27,136,128]{2,1,0:T(8,128)S(1)}, f32[27,136,128]{2,1,0:T(8,128)S(1)}, f32[1,136,128]{2,1,0:T(8,128)S(1)}, f32[632,128]{1,0:T(8,128)S(1)}, f32[632,128]{1,0:T(8,128)S(1)}) custom-call(f32[27,136,128]{2,1,0:T(8,128)} %copy-done.5, f32[27,136,128]{2,1,0:T(8,128)} %get-tuple-element.24.ax_in, f32[1,136,128]{2,1,0:T(8,128)S(1)} %get-tuple-element.25.sx_in, ...), custom_call_target="tpu_custom_call" | custom-call | tf_op jit(solution)/shard_map/span/pallas_call | solution.py:567
  34.4 0.0 copy-start.3
  34.4 1.3 %copy-done.3 = f32[27,136,128]{2,1,0:T(8,128)} copy-done((f32[27,136,128]{2,1,0:T(8,128)}, f32[27,136,128]{2,1,0:T(8,128)S(1)}, u32[]{:S(2)}) %copy-start.3) | copy-done | bytes 1880088
  35.7 0.0 copy-start.4
  35.7 1.2 %copy-done.4 = f32[27,136,128]{2,1,0:T(8,128)} copy-done((f32[27,136,128]{2,1,0:T(8,128)}, f32[27,136,128]{2,1,0:T(8,128)S(1)}, u32[]{:S(2)}) %copy-start.4) | copy-done | bytes 1880088
  36.9 0.0 collective-permute-start.3
  36.9 3.1 %collective-permute-start.4 = (f32[632,128]{1,0:T(8,128)S(1)}, f32[632,128]{1,0:T(8,128)S(1)}, u32[]{:S(2)}, u32[]{:S(2)}) collective-permute-start(f32[632,128]{1,0:T(8,128)S(1)} %get-tuple-element.32), channel_id=1, source_target_pairs={{0,14},{2,4},{4,2},{6,8},{8,6},{10,12},{12,10},{14,0},{1,15},{3,5}... | collective-permute-start | bytes 970760 | tf_op jit(solution)/shard_map/ppermute | solution.py:551
  40.0 0.0 collective-permute-done.3.got0
  40.0 4.7 %collective-permute-done.4.got1 = f32[632,128]{1,0:T(8,128)S(1)} collective-permute-done((f32[632,128]{1,0:T(8,128)S(1)}, f32[632,128]{1,0:T(8,128)S(1)}, u32[]{:S(2)}, u32[]{:S(2)}) %collective-permute-start.4) | collective-permute-done | bytes 323616 | tf_op jit(solution)/shard_map/ppermute | solution.py:551
  44.8 8.0 %middle.1 = (f32[27,136,128]{2,1,0:T(8,128)S(1)}, f32[27,64,128]{2,1,0:T(8,128)S(1)}, f32[4,136,128]{2,1,0:T(8,128)S(1)}, f32[4,136,128]{2,1,0:T(8,128)S(1)}, f3...) custom-call(f32[27,136,128]{2,1,0:T(8,128)} %copy-done.3, ...), custom_call_target="tpu_custom_call" | custom-call | tf_op jit(solution)/shard_map/middle/pallas_call | solution.py:569
  52.7 0.0 copy-start.1
  52.7 0.0 copy-start.7
  52.8 0.0 copy-start.9
  52.8 1.0 %collective-permute-start.5 = (f32[440,128]{1,0:T(8,128)S(1)}, f32[440,128]{1,0:T(8,128)S(1)}, u32[]{:S(2)}, u32[]{:S(2)}) collective-permute-start(f32[440,128]{1,0:T(8,128)S(1)} %get-tuple-element.34), channel_id=1, source_target_pairs={{0,16},{16,0},{32,48},{48,32},{64,80},{80,64},{96,112},{112,96},{1... | collective-permute-start | bytes 675848 | tf_op jit(solution)/shard_map/ppermute | solution.py:551
  53.8 2.5 %collective-permute-start.6 = (f32[440,128]{1,0:T(8,128)S(1)}, f32[440,128]{1,0:T(8,128)S(1)}, u32[]{:S(2)}, u32[]{:S(2)}) collective-permute-start(f32[440,128]{1,0:T(8,128)S(1)} %get-tuple-element.35), channel_id=1, source_target_pairs={{0,112},{16,32},{32,16},{48,64},{64,48},{80,96},{96,80},{112,0},{1... | collective-permute-start | bytes 675848 | tf_op jit(solution)/shard_map/ppermute | solution.py:551
  56.2 6.6 %collective-permute-done.5.got0 = f32[440,128]{1,0:T(8,128)S(1)} collective-permute-done((f32[440,128]{1,0:T(8,128)S(1)}, f32[440,128]{1,0:T(8,128)S(1)}, u32[]{:S(2)}, u32[]{:S(2)}) %collective-permute-start.5) | collective-permute-done | bytes 225312 | tf_op jit(solution)/shard_map/ppermute | solution.py:551
  62.8 3.1 %collective-permute-done.6.got1 = f32[440,128]{1,0:T(8,128)S(1)} collective-permute-done((f32[440,128]{1,0:T(8,128)S(1)}, f32[440,128]{1,0:T(8,128)S(1)}, u32[]{:S(2)}, u32[]{:S(2)}) %collective-permute-start.6) | collective-permute-done | bytes 225312 | tf_op jit(solution)/shard_map/ppermute | solution.py:551
  65.9 0.6 span2.1
  66.4 0.1 collective-permute-start.7
  66.5 2.7 %collective-permute-start.8 = (f32[464,128]{1,0:T(8,128)S(1)}, f32[464,128]{1,0:T(8,128)S(1)}, u32[]{:S(2)}, u32[]{:S(2)}) collective-permute-start(f32[464,128]{1,0:T(8,128)S(1)} %get-tuple-element.43), channel_id=1, source_target_pairs={{0,14},{2,4},{4,2},{6,8},{8,6},{10,12},{12,10},{14,0},{1,15},{3,5}... | collective-permute-start | bytes 712712 | tf_op jit(solution)/shard_map/ppermute | solution.py:551
  69.2 0.0 collective-permute-done.7.got0
  69.2 4.1 %collective-permute-done.8.got1 = f32[464,128]{1,0:T(8,128)S(1)} collective-permute-done((f32[464,128]{1,0:T(8,128)S(1)}, f32[464,128]{1,0:T(8,128)S(1)}, u32[]{:S(2)}, u32[]{:S(2)}) %collective-permute-start.8) | collective-permute-done | bytes 237600 | tf_op jit(solution)/shard_map/ppermute | solution.py:551
  73.3 0.0 copy-done.1
  73.3 0.0 copy-done.7
  73.3 0.0 copy-done.9
  73.3 5.4 %last.1 = (f32[27,4,8,256]{3,2,1,0:T(8,128)}, f32[4,8,256]{2,1,0:T(8,128)}) custom-call(f32[27,136,128]{2,1,0:T(8,128)S(1)} %get-tuple-element.36.a2, f32[27,4,8,256]{3,2,1,0:T(8,128)S(1)} %copy-done.1, f32[4,8,256]{2,1,0:T(8,128)S(1)} %copy-done.7, s32[4,8,256]{2,1,0:T(8,128)S(1)} %copy-done.9, f32[27,64,128]{2,1,0:T(8,128)S(1)} %get-tuple-element.37.f1, ...), custom_call_target="tpu_custom_call" | custom-call | tf_op jit(solution)/shard_map/last/pallas_call | solution.py:578
Async XLA Ops:
  0.6 1.2 %copy-start = (f32[27,4,8,256]{3,2,1,0:T(8,128)S(1)}, f32[27,4,8,256]{3,2,1,0:T(8,128)}, u32[]{:S(2)}) copy-start(f32[27,4,8,256]{3,2,1,0:T(8,128)} %pops.5) | copy-start | bytes 2654212
  1.8 1.2 %copy-start.2 = (f32[27,4,8,256]{3,2,1,0:T(8,128)S(1)}, f32[27,4,8,256]{3,2,1,0:T(8,128)}, u32[]{:S(2)}) copy-start(f32[27,4,8,256]{3,2,1,0:T(8,128)} %cot.3) | copy-start | bytes 2654212
  3.0 0.8 copy-start.6
  3.7 0.8 copy-start.8
  4.8 4.0 %collective-permute-start = (f32[56,128]{1,0:T(8,128)S(1)}, f32[56,128]{1,0:T(8,128)S(1)}, u32[]{:S(2)}, u32[]{:S(2)}) collective-permute-start(f32[56,128]{1,0:T(8,128)S(1)} %cut.1), channel_id=1, source_target_pairs={{0,1},{1,0},{2,3},{3,2},{4,5},{5,4},{6,7},{7,6},{8,9},{9,8},{10,11... | collective-permute-start | bytes 86024 | tf_op jit(solution)/shard_map/ppermute | solution.py:564
  10.7 1.2 %copy-start.5 = (f32[27,136,128]{2,1,0:T(8,128)}, f32[27,136,128]{2,1,0:T(8,128)S(1)}, u32[]{:S(2)}) copy-start(f32[27,136,128]{2,1,0:T(8,128)S(1)} %get-tuple-element.23.tx_in) | copy-start | bytes 5640196
  12.0 11.6 %collective-permute-start.1 = (f32[608,128]{1,0:T(8,128)S(1)}, f32[608,128]{1,0:T(8,128)S(1)}, u32[]{:S(2)}, u32[]{:S(2)}) collective-permute-start(f32[608,128]{1,0:T(8,128)S(1)} %get-tuple-element.26), channel_id=1, source_target_pairs={{0,16},{16,0},{32,48},{48,32},{64,80},{80,64},{96,112},{112,96},{1... | collective-permute-start | bytes 933896 | tf_op jit(solution)/shard_map/ppermute | solution.py:551
  15.1 16.6 %collective-permute-start.2 = (f32[608,128]{1,0:T(8,128)S(1)}, f32[608,128]{1,0:T(8,128)S(1)}, u32[]{:S(2)}, u32[]{:S(2)}) collective-permute-start(f32[608,128]{1,0:T(8,128)S(1)} %get-tuple-element.27), channel_id=1, source_target_pairs={{0,112},{16,32},{32,16},{48,64},{64,48},{80,96},{96,80},{112,0},{1... | collective-permute-start | bytes 933896 | tf_op jit(solution)/shard_map/ppermute | solution.py:551
  34.4 1.3 %copy-start.3 = (f32[27,136,128]{2,1,0:T(8,128)}, f32[27,136,128]{2,1,0:T(8,128)S(1)}, u32[]{:S(2)}) copy-start(f32[27,136,128]{2,1,0:T(8,128)S(1)} %get-tuple-element.28.tx) | copy-start | bytes 5640196
  35.7 1.2 %copy-start.4 = (f32[27,136,128]{2,1,0:T(8,128)}, f32[27,136,128]{2,1,0:T(8,128)S(1)}, u32[]{:S(2)}) copy-start(f32[27,136,128]{2,1,0:T(8,128)S(1)} %get-tuple-element.29.ax) | copy-start | bytes 5640196
  36.9 3.1 %collective-permute-start.3 = (f32[632,128]{1,0:T(8,128)S(1)}, f32[632,128]{1,0:T(8,128)S(1)}, u32[]{:S(2)}, u32[]{:S(2)}) collective-permute-start(f32[632,128]{1,0:T(8,128)S(1)} %get-tuple-element.31), channel_id=1, source_target_pairs={{0,2},{2,0},{4,6},{6,4},{8,10},{10,8},{12,14},{14,12},{1,3},{3,1},... | collective-permute-start | bytes 970760 | tf_op jit(solution)/shard_map/ppermute | solution.py:551
  36.9 7.8 %collective-permute-start.4 = (f32[632,128]{1,0:T(8,128)S(1)}, f32[632,128]{1,0:T(8,128)S(1)}, u32[]{:S(2)}, u32[]{:S(2)}) collective-permute-start(f32[632,128]{1,0:T(8,128)S(1)} %get-tuple-element.32), channel_id=1, source_target_pairs={{0,14},{2,4},{4,2},{6,8},{8,6},{10,12},{12,10},{14,0},{1,15},{3,5}... | collective-permute-start | bytes 970760 | tf_op jit(solution)/shard_map/ppermute | solution.py:551
  52.7 20.6 %copy-start.1 = (f32[27,4,8,256]{3,2,1,0:T(8,128)S(1)}, f32[27,4,8,256]{3,2,1,0:T(8,128)}, u32[]{:S(2)}) copy-start(f32[27,4,8,256]{3,2,1,0:T(8,128)} %pops.5) | copy-start | bytes 2654212
  52.7 20.6 %copy-start.7 = (f32[4,8,256]{2,1,0:T(8,128)S(1)}, f32[4,8,256]{2,1,0:T(8,128)}, u32[]{:S(2)}) copy-start(f32[4,8,256]{2,1,0:T(8,128)} %block.5) | copy-start | bytes 98308
  52.8 20.6 %copy-start.9 = (s32[4,8,256]{2,1,0:T(8,128)S(1)}, s32[4,8,256]{2,1,0:T(8,128)}, u32[]{:S(2)}) copy-start(s32[4,8,256]{2,1,0:T(8,128)} %mask.5) | copy-start | bytes 98308
  52.8 10.0 %collective-permute-start.5 = (f32[440,128]{1,0:T(8,128)S(1)}, f32[440,128]{1,0:T(8,128)S(1)}, u32[]{:S(2)}, u32[]{:S(2)}) collective-permute-start(f32[440,128]{1,0:T(8,128)S(1)} %get-tuple-element.34), channel_id=1, source_target_pairs={{0,16},{16,0},{32,48},{48,32},{64,80},{80,64},{96,112},{112,96},{1... | collective-permute-start | bytes 675848 | tf_op jit(solution)/shard_map/ppermute | solution.py:551
  53.8 12.1 %collective-permute-start.6 = (f32[440,128]{1,0:T(8,128)S(1)}, f32[440,128]{1,0:T(8,128)S(1)}, u32[]{:S(2)}, u32[]{:S(2)}) collective-permute-start(f32[440,128]{1,0:T(8,128)S(1)} %get-tuple-element.35), channel_id=1, source_target_pairs={{0,112},{16,32},{32,16},{48,64},{64,48},{80,96},{96,80},{112,0},{1... | collective-permute-start | bytes 675848 | tf_op jit(solution)/shard_map/ppermute | solution.py:551
  66.4 2.8 %collective-permute-start.7 = (f32[464,128]{1,0:T(8,128)S(1)}, f32[464,128]{1,0:T(8,128)S(1)}, u32[]{:S(2)}, u32[]{:S(2)}) collective-permute-start(f32[464,128]{1,0:T(8,128)S(1)} %get-tuple-element.42), channel_id=1, source_target_pairs={{0,2},{2,0},{4,6},{6,4},{8,10},{10,8},{12,14},{14,12},{1,3},{3,1},... | collective-permute-start | bytes 712712 | tf_op jit(solution)/shard_map/ppermute | solution.py:551
  66.5 6.8 %collective-permute-start.8 = (f32[464,128]{1,0:T(8,128)S(1)}, f32[464,128]{1,0:T(8,128)S(1)}, u32[]{:S(2)}, u32[]{:S(2)}) collective-permute-start(f32[464,128]{1,0:T(8,128)S(1)} %get-tuple-element.43), channel_id=1, source_target_pairs={{0,14},{2,4},{4,2},{6,8},{8,6},{10,12},{12,10},{14,0},{1,15},{3,5}... | collective-permute-start | bytes 712712 | tf_op jit(solution)/shard_map/ppermute | solution.py:551
where the time goes:
time: 79.5 us; the launch traced here: 78.7 us
  waiting for transfers between devices  33.4 us (42%)
  Pallas kernels  19 us (24%)
  starting transfers between devices  18.1 us (23%)
  local copies, waits for them, and re-layouts  7.58 us (10%)
    ppermute x8, waiting for transfers between devices, swap(): return lax.ppermute(x, axis, pairs)  31.1 us
    ppermute x8, starting transfers between devices, swap(): return lax.ppermute(x, axis, pairs)  16.4 us
    pallas_call x1, Pallas kernels, body(): call(middle_kernel, [BIG, (27, 64, 128), (4, ROWS, 128), (4, ROWS, 128),...  7.97 us
    unnamed x20, local copies, waits for them, and re-layouts  7.58 us
    pallas_call x1, Pallas kernels, body(): call(last_kernel, [(27, 4, 8, 256), (4, 8, 256)], scratch=[BIG] * 5, name...  5.4 us
    pallas_call x1, Pallas kernels, body(): call(span_kernel, [BIG, BIG, ONE, Y1, Y1], name='span')(tx, ax, sx, m0, m1)  2.76 us
    ppermute x1, waiting for transfers between devices, body(): cut = lax.ppermute(cut, 'gz', [(0, 1), (1, 0)])  2.3 us
    pallas_call x1, Pallas kernels, body(): call(first_kernel, [BIG, BIG, ONE, X1, X1], name='first')  1.99 us
  transfers between devices with their start and end apart: 9, of which 7 were waited for; matrix products, arithmetic and copies ran while one was open for 0% of the time, Pallas kernels for 0%

commit v1 on v0

--- a/solution.py
+++ b/solution.py
@@ -349,10 +349,19 @@
     return blockage * (1.0 - m) + m
 
 
-def cut_kernel(pops, block, mask, cot, msg):
+def cut_kernel(pops_hbm, block_hbm, mask_hbm, cot_hbm, msg, pops, block, mask, cot, sems):
     gz = lax.axis_index("gz")
     lane = lanes()
-    top = gz == 0
+    z = pl.ds(pl.multiple_of(128 * (1 - gz), 128), 128)
+    copies = []
+    for n, (src, dst) in enumerate(((pops_hbm, pops), (cot_hbm, cot))):
+        copies.append(pltpu.make_async_copy(src.at[:, :, :, z], dst, sems.at[n]))
+    for n, (src, dst) in enumerate(((block_hbm, block), (mask_hbm, mask))):
+        copies.append(pltpu.make_async_copy(src.at[:, :, z], dst, sems.at[n + 2]))
+    for copy in copies:
+        copy.start()
+    for copy in copies:
+        copy.wait()
     for n in range(7):
         acc = jnp.zeros((8, 128), F32)
         for j in range(8):
@@ -361,13 +370,12 @@
                 break
             for x in range(4):
                 if slot == 54:
-                    hi = solid_of(block[x, :, 128:256], mask[x, :, 128:256])
-                    lo = solid_of(block[x, :, 0:128], mask[x, :, 0:128])
+                    edge = solid_of(block[x], mask[x])
                 else:
                     ref, i = (pops, slot) if slot < 27 else (cot, slot - 27)
-                    hi, lo = ref[i, x, :, 128:256], ref[i, x, :, 0:128]
+                    edge = ref[i, x]
                 at = 16 * j + 4 * x
-                moved = roll_l(jnp.where(top, hi, lo), mod128(at + 4 - 4 * gz))
+                moved = roll_l(edge, mod128(at + 4 - 4 * gz))
                 acc = jnp.where((lane >= at) & (lane < at + 4), moved, acc)
         msg[8 * n : 8 * n + 8, :] = acc
 
@@ -435,21 +443,17 @@
         pack_y(msg, e, -1, gz, tx)
 
 
-def put_own(ref, i, x, half, value):
-    ref[i, tile(2 * (x - 2) + half), :] = value
-
-
-def middle_kernel(tx, ax, sx, got0, got1, a2, f1, u_own, u_yh, sy, q2, msg0, msg1, ty, ay, f_own, f_yh, c_own, c_yh, p_own):
+def middle_kernel(tx, ax, sx, got0, got1, a2, f1, u_own, u_yh, sy, q2, msg0, msg1, ty, ay, f2, f_yh, c_own, c_yh, p_own):
     gz = lax.axis_index("gz")
     for msg, s in zip((got0, got1), sides("gy")):
         unpack_y(msg, s, 1, ty, ay, sy)
-    stream_main(tx, ty, f_own, f_yh, 1, gz, 1, 7, put_tile)
-    stream_mini(tx, ty, f_own, f_yh, 1, gz)
+    stream_main(tx, ty, f1, f_yh, 1, gz, 1, 7, put_tile)
+    stream_mini(tx, ty, f1, f_yh, 1, gz)
 
     def again(k, carry):
         n = jnp.where(k == 12, 16, k + 2)
         here = tile(n)
-        for src, sol, dst, us in ((f_own, sx, c_own, u_own), (f_yh, sy, c_yh, u_yh)):
+        for src, sol, dst, us in ((f1, sx, c_own, u_own), (f_yh, sy, c_yh, u_yh)):
             f = [src[i, here, :] for i in range(27)]
             rho, u = moments(f)
             us[0, here, :] = rho
@@ -462,21 +466,15 @@
 
     lax.fori_loop(0, 13, again, 0)
 
-    def keep(n, carry):
-        for i in range(27):
-            f1[i, tile(n), :] = f_own[i, tile(n + 4), :]
-        return carry
-
-    lax.fori_loop(0, 8, keep, 0)
-    stream_main(c_own, c_yh, f_own, None, 1, gz, 2, 6, put_tile)
-    stream_mini(c_own, c_yh, f_own, None, 1, gz)
+    stream_main(c_own, c_yh, f2, None, 1, gz, 2, 6, put_tile)
+    stream_mini(c_own, c_yh, f2, None, 1, gz)
     stream_main(ax, ay, p_own, None, -1, gz, 2, 6, put_tile)
     stream_mini(ax, ay, p_own, None, -1, gz)
 
     def back(k, carry):
         n = jnp.where(k == 8, 16, k + 4)
         here = tile(n)
-        f = [f_own[i, here, :] for i in range(27)]
+        f = [f2[i, here, :] for i in range(27)]
         p = [p_own[i, here, :] for i in range(27)]
         rho, u = moments(f)
         out, blame = pull_back(p, sx[0, here, :], u, f, rho)
@@ -490,7 +488,7 @@
         pack_x(msg, e, -1, gz, a2)
 
 
-def last_kernel(a2, pops, block, mask, f1, u_own, u_yh, sx, sy, q2, got0, got1, adjoint, grad, ty, p_own, p_yh, c_own, c_yh):
+def last_kernel(a2, pops, block, mask, f1, u_own, u_yh, sx, sy, q2, got0, got1, adjoint, grad, ty, p_own, p_yh, c_own, c_yh, q1):
     gz = lax.axis_index("gz")
     for msg, s in zip((got0, got1), sides("gy")):
         unpack_y(msg, s, -1, ty)
@@ -501,23 +499,17 @@
         n = jnp.where(k == 12, 16, k + 2)
         here = tile(n)
         for src, sol, dst, us in ((p_own, sx, c_own, u_own), (p_yh, sy, c_yh, u_yh)):
-            out, _ = pull_back([src[i, here, :] for i in range(27)], sol[0, here, :], [us[c, here, :] for c in (1, 2, 3)])
+            p = [src[i, here, :] for i in range(27)]
+            u = [us[c, here, :] for c in (1, 2, 3)]
+            f = None if src is p_yh else [f1[i, here, :] for i in range(27)]
+            out, blame = pull_back(p, sol[0, here, :], u, f, us[0, here, :])
             for i in range(27):
                 dst[i, here, :] = out[i]
+            if f is not None:
+                q1[here, :] = blame
         return carry
 
     lax.fori_loop(0, 13, again, 0)
-
-    def first_blame(x, carry):
-        for half in (0, 1):
-            here = tile(2 * x + 4 + half)
-            there = tile(2 * x + half)
-            u = [u_own[c, here, :] for c in (1, 2, 3)]
-            _, blame = pull_back([p_own[i, here, :] for i in range(27)], sx[0, here, :], u, [f1[i, there, :] for i in range(27)], u_own[0, here, :])
-            grad[x, :, pl.ds(128 * half, 128)] = blame + q2[there, :]
-        return carry
-
-    lax.fori_loop(0, 4, first_blame, 0)
     stream_main(c_own, c_yh, p_own, None, -1, gz, 2, 6, put_tile)
 
     def back(x, carry):
@@ -529,18 +521,19 @@
             out, blame = pull_back([p_own[i, here, :] for i in range(27)], sx[0, here, :], u, f, rho)
             for i in range(27):
                 adjoint[i, x, :, z] = out[i]
-            grad[x, :, z] = (1.0 - mask[x, :, z].astype(F32)) * (grad[x, :, z] + blame)
+            grad[x, :, z] = (1.0 - mask[x, :, z].astype(F32)) * (q1[here, :] + q2[tile(2 * x + half), :] + blame)
         return carry
 
     lax.fori_loop(0, 4, back, 0)
 
 
-def call(kernel, outs, scratch=(), name=None):
+def call(kernel, outs, scratch=(), name=None, mib=8, in_specs=None):
     return pl.pallas_call(
         kernel,
         out_shape=[jax.ShapeDtypeStruct(s, F32) for s in outs],
-        scratch_shapes=[pltpu.VMEM(s, F32) for s in scratch],
-        compiler_params=pltpu.CompilerParams(vmem_limit_bytes=48 * 1024 * 1024),
+        scratch_shapes=[pltpu.VMEM(s, F32) if isinstance(s, tuple) else s for s in scratch],
+        **({} if in_specs is None else {"in_specs": in_specs}),
+        compiler_params=pltpu.CompilerParams(vmem_limit_bytes=mib * 1024 * 1024),
         name=name,
     )
 
@@ -560,7 +553,9 @@
 
 
 def body(populations, blockage, solid_mask, cotangent):
-    (cut,) = call(cut_kernel, [(56, 128)], name="cut")(populations, blockage, solid_mask, cotangent)
+    halves = [pltpu.VMEM((27, 4, 8, 128), F32), pltpu.VMEM((4, 8, 128), F32), pltpu.VMEM((4, 8, 128), jnp.int32), pltpu.VMEM((27, 4, 8, 128), F32)]
+    anywhere = [pl.BlockSpec(memory_space=pltpu.HBM)] * 4
+    (cut,) = call(cut_kernel, [(56, 128)], scratch=halves + [pltpu.SemaphoreType.DMA((4,))], name="cut", mib=60, in_specs=anywhere)(populations, blockage, solid_mask, cotangent)
     cut = lax.ppermute(cut, "gz", [(0, 1), (1, 0)])
     tx, ax, sx, m0, m1 = call(first_kernel, [BIG, BIG, ONE, X1, X1], name="first")(populations, blockage, solid_mask, cotangent, cut)
     m0, m1 = swap(m0, "gx", False), swap(m1, "gx", True)
@@ -568,14 +563,15 @@
     m0, m1 = swap(m0, "gy", False), swap(m1, "gy", True)
     a2, f1, u_own, u_yh, sy, q2, m0, m1 = call(
         middle_kernel,
-        [BIG, (27, 64, 128), (4, ROWS, 128), (4, ROWS, 128), ONE, (72, 128), X2, X2],
+        [BIG, BIG, (4, ROWS, 128), (4, ROWS, 128), ONE, (72, 128), X2, X2],
         scratch=[BIG] * 7,
         name="middle",
+        mib=24,
     )(tx, ax, sx, m0, m1)
     m0, m1 = swap(m0, "gx", False), swap(m1, "gx", True)
     a2, m0, m1 = call(span_kernel_2, [BIG, Y2, Y2], name="span2")(a2, m0, m1)
     m0, m1 = swap(m0, "gy", False), swap(m1, "gy", True)
-    adjoint, grad = call(last_kernel, [(27, 4, 8, 256), (4, 8, 256)], scratch=[BIG] * 5, name="last")(
+    adjoint, grad = call(last_kernel, [(27, 4, 8, 256), (4, 8, 256)], scratch=[BIG] * 5 + [(ROWS, 128)], name="last", mib=20)(
         a2, populations, blockage, solid_mask, f1, u_own, u_yh, sx, sy, q2, m0, m1
     )
     return adjoint, grad

time: 79.5 us -> 68.4 us (0.86)
  local copies, waits for them, and re-layouts: 7.58 us -> 0.02 us
  Pallas kernels: 19 us -> 15.3 us
    unnamed x20 -> x8, local copies, waits for them, and re-layouts: 7.58 us -> 0.02 us
    pallas_call x1, Pallas kernels: 2.76 us -> 0.67 us  [body(): call(span_kernel, [BIG, BIG, ONE, Y1, Y1], name='span')(tx, ax, sx, m0, m1)]
    pallas_call x1, Pallas kernels: 1.99 us -> 0.78 us  [body(): call(first_kernel, [BIG, BIG, ONE, X1, X1], name='first')]
where the time goes in v1:
time: 68.4 us; the launch traced here: 67.9 us
  waiting for transfers between devices  33.5 us (49%)
  starting transfers between devices  18.3 us (27%)
  Pallas kernels  15.3 us (22%)
  between operations  0.73 us (1%)
    ppermute x8, waiting for transfers between devices, swap(): return lax.ppermute(x, axis, pairs)  31 us
    ppermute x8, starting transfers between devices, swap(): return lax.ppermute(x, axis, pairs)  16.7 us
    pallas_call x1, Pallas kernels, body(): call(middle_kernel, [BIG, BIG, (4, ROWS, 128), (4, ROWS, 128), ONE, (72,...  5.8 us
    pallas_call x1, Pallas kernels, body(): call(last_kernel, [(27, 4, 8, 256), (4, 8, 256)], scratch=[BIG] * 5 + [(R...  5.27 us
    ppermute x1, waiting for transfers between devices, body(): cut = lax.ppermute(cut, 'gz', [(0, 1), (1, 0)])  2.51 us
    pallas_call x1, Pallas kernels, body(): call(cut_kernel, [(56, 128)], scratch=halves + [pltpu.SemaphoreType.DMA((...  2.23 us
    ppermute x1, starting transfers between devices, body(): cut = lax.ppermute(cut, 'gz', [(0, 1), (1, 0)])  1.65 us
  transfers between devices with their start and end apart: 9, of which 7 were waited for; matrix products, arithmetic and copies ran while one was open for 0% of the time, Pallas kernels for 0%

profile of v1, /device:TPU:0, one launch (start us, length us, event | category | flops | bytes accessed | tf_op | source)
XLA Modules:
  0.0 67.9 jit_solution(10649925759950600348)
XLA Ops:
  0.6 0.0 copy-start.3
  0.6 0.0 copy-start.2
  0.7 0.0 copy-start
  0.7 0.0 copy-start.1
  0.7 2.2 %cut.1 = f32[56,128]{1,0:T(8,128)} custom-call(f32[27,4,8,256]{3,2,1,0:T(8,128)} %pops.3, f32[4,8,256]{2,1,0:T(8,128)} %block.3, s32[4,8,256]{2,1,0:T(8,128)} %mask.3, f32[27,4,8,256]{3,2,1,0:T(8,128)} %cot.1), custom_call_target="tpu_custom_call" | custom-call | tf_op jit(solution)/shard_map/cut/pallas_call | solution.py:558
  2.9 1.7 %collective-permute-start = (f32[56,128]{1,0:T(8,128)}, f32[56,128]{1,0:T(8,128)S(1)}, u32[]{:S(2)}, u32[]{:S(2)}) collective-permute-start(f32[56,128]{1,0:T(8,128)} %cut.1), channel_id=1, source_target_pairs={{0,1},{1,0},{2,3},{3,2},{4,5},{5,4},{6,7},{7,6},{8,9},{9,8},{10,11... | collective-permute-start | bytes 86024 | tf_op jit(solution)/shard_map/ppermute | solution.py:559
  4.6 2.5 %collective-permute-done.cut = f32[56,128]{1,0:T(8,128)S(1)} collective-permute-done((f32[56,128]{1,0:T(8,128)}, f32[56,128]{1,0:T(8,128)S(1)}, u32[]{:S(2)}, u32[]{:S(2)}) %collective-permute-start) | collective-permute-done | bytes 28704 | tf_op jit(solution)/shard_map/ppermute | solution.py:559
  7.1 0.0 copy-done.3
  7.1 0.0 copy-done.2
  7.1 0.0 copy-done
  7.1 0.0 copy-done.1
  7.1 0.8 %first.1 = (f32[27,136,128]{2,1,0:T(8,128)S(1)}, f32[27,136,128]{2,1,0:T(8,128)S(1)}, f32[1,136,128]{2,1,0:T(8,128)S(1)}, f32[608,128]{1,0:T(8,128)S(1)}, f32[608,128]{1,0:T(8,128)S(1)}) custom-call(f32[27,4,8,256]{3,2,1,0:T(8,128)S(1)} %copy-done, f32[4,8,256]{2,1,0:T(8,128)S(1)} %copy-done.2, s32[4,8,256]{2,1,0:T(8,128)S(1)} %copy-done.3, ...), custom_call_target="tpu_custom_call" | custom-call | tf_op jit(solution)/shard_map/first/pallas_call | solution.py:560
  7.9 3.2 %collective-permute-start.1 = (f32[608,128]{1,0:T(8,128)S(1)}, f32[608,128]{1,0:T(8,128)S(1)}, u32[]{:S(2)}, u32[]{:S(2)}) collective-permute-start(f32[608,128]{1,0:T(8,128)S(1)} %get-tuple-element.26), channel_id=1, source_target_pairs={{0,16},{16,0},{32,48},{48,32},{64,80},{80,64},{96,112},{112,96},{1... | collective-permute-start | bytes 933896 | tf_op jit(solution)/shard_map/ppermute | solution.py:544
  11.1 4.0 %collective-permute-start.2 = (f32[608,128]{1,0:T(8,128)S(1)}, f32[608,128]{1,0:T(8,128)S(1)}, u32[]{:S(2)}, u32[]{:S(2)}) collective-permute-start(f32[608,128]{1,0:T(8,128)S(1)} %get-tuple-element.27), channel_id=1, source_target_pairs={{0,112},{16,32},{32,16},{48,64},{64,48},{80,96},{96,80},{112,0},{1... | collective-permute-start | bytes 933896 | tf_op jit(solution)/shard_map/ppermute | solution.py:544
  15.1 4.5 %collective-permute-done.1.got0 = f32[608,128]{1,0:T(8,128)S(1)} collective-permute-done((f32[608,128]{1,0:T(8,128)S(1)}, f32[608,128]{1,0:T(8,128)S(1)}, u32[]{:S(2)}, u32[]{:S(2)}) %collective-permute-start.1) | collective-permute-done | bytes 311328 | tf_op jit(solution)/shard_map/ppermute | solution.py:544
  19.6 8.1 %collective-permute-done.2.got1 = f32[608,128]{1,0:T(8,128)S(1)} collective-permute-done((f32[608,128]{1,0:T(8,128)S(1)}, f32[608,128]{1,0:T(8,128)S(1)}, u32[]{:S(2)}, u32[]{:S(2)}) %collective-permute-start.2) | collective-permute-done | bytes 311328 | tf_op jit(solution)/shard_map/ppermute | solution.py:544
  27.6 0.7 span.1
  28.3 0.1 collective-permute-start.3
  28.4 3.1 %collective-permute-start.4 = (f32[632,128]{1,0:T(8,128)S(1)}, f32[632,128]{1,0:T(8,128)S(1)}, u32[]{:S(2)}, u32[]{:S(2)}) collective-permute-start(f32[632,128]{1,0:T(8,128)S(1)} %get-tuple-element.32), channel_id=1, source_target_pairs={{0,14},{2,4},{4,2},{6,8},{8,6},{10,12},{12,10},{14,0},{1,15},{3,5}... | collective-permute-start | bytes 970760 | tf_op jit(solution)/shard_map/ppermute | solution.py:544
  31.5 0.0 collective-permute-done.3.got0
  31.5 4.7 %collective-permute-done.4.got1 = f32[632,128]{1,0:T(8,128)S(1)} collective-permute-done((f32[632,128]{1,0:T(8,128)S(1)}, f32[632,128]{1,0:T(8,128)S(1)}, u32[]{:S(2)}, u32[]{:S(2)}) %collective-permute-start.4) | collective-permute-done | bytes 323616 | tf_op jit(solution)/shard_map/ppermute | solution.py:544
  36.2 5.8 %middle.1 = (f32[27,136,128]{2,1,0:T(8,128)S(1)}, f32[27,136,128]{2,1,0:T(8,128)S(1)}, f32[4,136,128]{2,1,0:T(8,128)S(1)}, f32[4,136,128]{2,1,0:T(8,128)S(1)}, f...) custom-call(f32[27,136,128]{2,1,0:T(8,128)S(1)} %get-tuple-element.28.tx, ...), custom_call_target="tpu_custom_call" | custom-call | tf_op jit(solution)/shard_map/middle/pallas_call | solution.py:564
  42.0 1.0 %collective-permute-start.5 = (f32[440,128]{1,0:T(8,128)S(1)}, f32[440,128]{1,0:T(8,128)S(1)}, u32[]{:S(2)}, u32[]{:S(2)}) collective-permute-start(f32[440,128]{1,0:T(8,128)S(1)} %get-tuple-element.34), channel_id=1, source_target_pairs={{0,16},{16,0},{32,48},{48,32},{64,80},{80,64},{96,112},{112,96},{1... | collective-permute-start | bytes 675848 | tf_op jit(solution)/shard_map/ppermute | solution.py:544
  43.0 2.5 %collective-permute-start.6 = (f32[440,128]{1,0:T(8,128)S(1)}, f32[440,128]{1,0:T(8,128)S(1)}, u32[]{:S(2)}, u32[]{:S(2)}) collective-permute-start(f32[440,128]{1,0:T(8,128)S(1)} %get-tuple-element.35), channel_id=1, source_target_pairs={{0,112},{16,32},{32,16},{48,64},{64,48},{80,96},{96,80},{112,0},{1... | collective-permute-start | bytes 675848 | tf_op jit(solution)/shard_map/ppermute | solution.py:544
  45.5 6.6 %collective-permute-done.5.got0 = f32[440,128]{1,0:T(8,128)S(1)} collective-permute-done((f32[440,128]{1,0:T(8,128)S(1)}, f32[440,128]{1,0:T(8,128)S(1)}, u32[]{:S(2)}, u32[]{:S(2)}) %collective-permute-start.5) | collective-permute-done | bytes 225312 | tf_op jit(solution)/shard_map/ppermute | solution.py:544
  52.1 3.1 %collective-permute-done.6.got1 = f32[440,128]{1,0:T(8,128)S(1)} collective-permute-done((f32[440,128]{1,0:T(8,128)S(1)}, f32[440,128]{1,0:T(8,128)S(1)}, u32[]{:S(2)}, u32[]{:S(2)}) %collective-permute-start.6) | collective-permute-done | bytes 225312 | tf_op jit(solution)/shard_map/ppermute | solution.py:544
  55.1 0.6 span2.1
  55.7 0.1 collective-permute-start.7
  55.8 2.8 %collective-permute-start.8 = (f32[464,128]{1,0:T(8,128)S(1)}, f32[464,128]{1,0:T(8,128)S(1)}, u32[]{:S(2)}, u32[]{:S(2)}) collective-permute-start(f32[464,128]{1,0:T(8,128)S(1)} %get-tuple-element.43), channel_id=1, source_target_pairs={{0,14},{2,4},{4,2},{6,8},{8,6},{10,12},{12,10},{14,0},{1,15},{3,5}... | collective-permute-start | bytes 712712 | tf_op jit(solution)/shard_map/ppermute | solution.py:544
  58.6 0.0 collective-permute-done.7.got0
  58.6 4.0 %collective-permute-done.8.got1 = f32[464,128]{1,0:T(8,128)S(1)} collective-permute-done((f32[464,128]{1,0:T(8,128)S(1)}, f32[464,128]{1,0:T(8,128)S(1)}, u32[]{:S(2)}, u32[]{:S(2)}) %collective-permute-start.8) | collective-permute-done | bytes 237600 | tf_op jit(solution)/shard_map/ppermute | solution.py:544
  62.6 5.3 %last.1 = (f32[27,4,8,256]{3,2,1,0:T(8,128)}, f32[4,8,256]{2,1,0:T(8,128)}) custom-call(f32[27,136,128]{2,1,0:T(8,128)S(1)} %get-tuple-element.36.a2, f32[27,4,8,256]{3,2,1,0:T(8,128)S(1)} %copy-done, f32[4,8,256]{2,1,0:T(8,128)S(1)} %copy-done.2, s32[4,8,256]{2,1,0:T(8,128)S(1)} %copy-done.3, f32[27,136,128]{2,1,0:T(8,128)S(1)} %get-tuple-element.37.f1, ...), custom_call_target="tpu_custom_call" | custom-call | tf_op jit(solution)/shard_map/last/pallas_call | solution.py:574
Async XLA Ops:
  0.6 6.4 %copy-start.3 = (s32[4,8,256]{2,1,0:T(8,128)S(1)}, s32[4,8,256]{2,1,0:T(8,128)}, u32[]{:S(2)}) copy-start(s32[4,8,256]{2,1,0:T(8,128)} %mask.3) | copy-start | bytes 98308
  0.6 6.4 %copy-start.2 = (f32[4,8,256]{2,1,0:T(8,128)S(1)}, f32[4,8,256]{2,1,0:T(8,128)}, u32[]{:S(2)}) copy-start(f32[4,8,256]{2,1,0:T(8,128)} %block.3) | copy-start | bytes 98308
  0.7 6.4 %copy-start = (f32[27,4,8,256]{3,2,1,0:T(8,128)S(1)}, f32[27,4,8,256]{3,2,1,0:T(8,128)}, u32[]{:S(2)}) copy-start(f32[27,4,8,256]{3,2,1,0:T(8,128)} %pops.3) | copy-start | bytes 2654212
  0.7 6.4 %copy-start.1 = (f32[27,4,8,256]{3,2,1,0:T(8,128)S(1)}, f32[27,4,8,256]{3,2,1,0:T(8,128)}, u32[]{:S(2)}) copy-start(f32[27,4,8,256]{3,2,1,0:T(8,128)} %cot.1) | copy-start | bytes 2654212
  2.9 4.2 %collective-permute-start = (f32[56,128]{1,0:T(8,128)}, f32[56,128]{1,0:T(8,128)S(1)}, u32[]{:S(2)}, u32[]{:S(2)}) collective-permute-start(f32[56,128]{1,0:T(8,128)} %cut.1), channel_id=1, source_target_pairs={{0,1},{1,0},{2,3},{3,2},{4,5},{5,4},{6,7},{7,6},{8,9},{9,8},{10,11... | collective-permute-start | bytes 86024 | tf_op jit(solution)/shard_map/ppermute | solution.py:559
  7.9 11.7 %collective-permute-start.1 = (f32[608,128]{1,0:T(8,128)S(1)}, f32[608,128]{1,0:T(8,128)S(1)}, u32[]{:S(2)}, u32[]{:S(2)}) collective-permute-start(f32[608,128]{1,0:T(8,128)S(1)} %get-tuple-element.26), channel_id=1, source_target_pairs={{0,16},{16,0},{32,48},{48,32},{64,80},{80,64},{96,112},{112,96},{1... | collective-permute-start | bytes 933896 | tf_op jit(solution)/shard_map/ppermute | solution.py:544
  11.1 16.6 %collective-permute-start.2 = (f32[608,128]{1,0:T(8,128)S(1)}, f32[608,128]{1,0:T(8,128)S(1)}, u32[]{:S(2)}, u32[]{:S(2)}) collective-permute-start(f32[608,128]{1,0:T(8,128)S(1)} %get-tuple-element.27), channel_id=1, source_target_pairs={{0,112},{16,32},{32,16},{48,64},{64,48},{80,96},{96,80},{112,0},{1... | collective-permute-start | bytes 933896 | tf_op jit(solution)/shard_map/ppermute | solution.py:544
  28.3 3.2 %collective-permute-start.3 = (f32[632,128]{1,0:T(8,128)S(1)}, f32[632,128]{1,0:T(8,128)S(1)}, u32[]{:S(2)}, u32[]{:S(2)}) collective-permute-start(f32[632,128]{1,0:T(8,128)S(1)} %get-tuple-element.31), channel_id=1, source_target_pairs={{0,2},{2,0},{4,6},{6,4},{8,10},{10,8},{12,14},{14,12},{1,3},{3,1},... | collective-permute-start | bytes 970760 | tf_op jit(solution)/shard_map/ppermute | solution.py:544
  28.4 7.8 %collective-permute-start.4 = (f32[632,128]{1,0:T(8,128)S(1)}, f32[632,128]{1,0:T(8,128)S(1)}, u32[]{:S(2)}, u32[]{:S(2)}) collective-permute-start(f32[632,128]{1,0:T(8,128)S(1)} %get-tuple-element.32), channel_id=1, source_target_pairs={{0,14},{2,4},{4,2},{6,8},{8,6},{10,12},{12,10},{14,0},{1,15},{3,5}... | collective-permute-start | bytes 970760 | tf_op jit(solution)/shard_map/ppermute | solution.py:544
  42.0 10.0 %collective-permute-start.5 = (f32[440,128]{1,0:T(8,128)S(1)}, f32[440,128]{1,0:T(8,128)S(1)}, u32[]{:S(2)}, u32[]{:S(2)}) collective-permute-start(f32[440,128]{1,0:T(8,128)S(1)} %get-tuple-element.34), channel_id=1, source_target_pairs={{0,16},{16,0},{32,48},{48,32},{64,80},{80,64},{96,112},{112,96},{1... | collective-permute-start | bytes 675848 | tf_op jit(solution)/shard_map/ppermute | solution.py:544
  43.0 12.1 %collective-permute-start.6 = (f32[440,128]{1,0:T(8,128)S(1)}, f32[440,128]{1,0:T(8,128)S(1)}, u32[]{:S(2)}, u32[]{:S(2)}) collective-permute-start(f32[440,128]{1,0:T(8,128)S(1)} %get-tuple-element.35), channel_id=1, source_target_pairs={{0,112},{16,32},{32,16},{48,64},{64,48},{80,96},{96,80},{112,0},{1... | collective-permute-start | bytes 675848 | tf_op jit(solution)/shard_map/ppermute | solution.py:544
  55.7 2.9 %collective-permute-start.7 = (f32[464,128]{1,0:T(8,128)S(1)}, f32[464,128]{1,0:T(8,128)S(1)}, u32[]{:S(2)}, u32[]{:S(2)}) collective-permute-start(f32[464,128]{1,0:T(8,128)S(1)} %get-tuple-element.42), channel_id=1, source_target_pairs={{0,2},{2,0},{4,6},{6,4},{8,10},{10,8},{12,14},{14,12},{1,3},{3,1},... | collective-permute-start | bytes 712712 | tf_op jit(solution)/shard_map/ppermute | solution.py:544
  55.8 6.8 %collective-permute-start.8 = (f32[464,128]{1,0:T(8,128)S(1)}, f32[464,128]{1,0:T(8,128)S(1)}, u32[]{:S(2)}, u32[]{:S(2)}) collective-permute-start(f32[464,128]{1,0:T(8,128)S(1)} %get-tuple-element.43), channel_id=1, source_target_pairs={{0,14},{2,4},{4,2},{6,8},{8,6},{10,12},{12,10},{14,0},{1,15},{3,5}... | collective-permute-start | bytes 712712 | tf_op jit(solution)/shard_map/ppermute | solution.py:544

commit v2 on v1

v2 whole, which is shorter than its diff:
```python
import functools
import jax
import jax.numpy as jnp
from jax import lax
from jax.experimental import pallas as pl
from jax.experimental.pallas import tpu as pltpu
from jax.sharding import PartitionSpec as P

DIRS = [(a, b, d) for a in (-1, 0, 1) for b in (-1, 0, 1) for d in (-1, 0, 1)]
WEIGHTS = [(8.0 / 27.0, 2.0 / 27.0, 1.0 / 54.0, 1.0 / 216.0)[abs(a) + abs(b) + abs(d)] for a, b, d in DIRS]
OMEGA = 1.25
NT = 17
ROWS = NT * 8
MINI = pl.ds(128, 8)
F32 = jnp.float32


def tile(n):
    return pl.ds(n * 8, 8) if isinstance(n, int) else pl.ds(pl.multiple_of(n * 8, 8), 8)


def lanes():
    return lax.broadcasted_iota(jnp.int32, (8, 128), 1)


def subs():
    return lax.broadcasted_iota(jnp.int32, (8, 128), 0)


def roll_l(v, k):
    return pltpu.roll(v, k, 1)


def roll_s(v, k):
    return pltpu.roll(v, k, 0)


def mod128(k):
    return lax.rem(k + 256, 128)


def sides(axis):
    parity = lax.rem(lax.axis_index(axis), 2)
    return (1 - 2 * parity, 2 * parity - 1)


def moments(f):
    rho = f[13]
    mom = [None, None, None]
    for i in range(13):
        plus, minus = f[i] + f[26 - i], f[26 - i] - f[i]
        rho = rho + plus
        for k in range(3):
            c = DIRS[26 - i][k]
            if c:
                term = minus if c > 0 else -minus
                mom[k] = term if mom[k] is None else (mom[k] + minus if c > 0 else mom[k] - minus)
    inv = 1.0 / rho
    return rho, [m * inv for m in mom]


def dot_c(vec, comps):
    out = None
    for c, v in zip(vec, comps):
        if c:
            if out is None:
                out = v if c > 0 else -v
            else:
                out = out + v if c > 0 else out - v
    return out


def collide(f, solid, rho, u):
    fluid = 1.0 - solid
    own = (1.0 - OMEGA) * fluid
    base = OMEGA * fluid * rho
    rest = base * (1.0 - 1.5 * (u[0] * u[0] + u[1] * u[1] + u[2] * u[2]))
    out = [None] * 27
    for i in range(13):
        j = 26 - i
        w = WEIGHTS[i]
        cu = dot_c(DIRS[j], u)
        bc = base * cu
        even = w * (rest + 4.5 * (bc * cu))
        odd = (3.0 * w) * bc
        out[j] = own * f[j] + solid * f[i] + (even + odd)
        out[i] = own * f[i] + solid * f[j] + (even - odd)
    out[13] = (own + solid) * f[13] + WEIGHTS[13] * rest
    return out


def pull_back(p, solid, u, f=None, rho=None):
    w0 = WEIGHTS[13] * p[13]
    w1 = [None] * 3
    w2 = {}
    add = lambda x, y: y if x is None else x + y
    by_class = {}
    for i in range(13):
        j = 26 - i
        plus, minus = WEIGHTS[i] * (p[j] + p[i]), WEIGHTS[i] * (p[j] - p[i])
        w0 = w0 + plus
        c = DIRS[j]
        for k in range(3):
            if c[k]:
                w1[k] = add(w1[k], minus if c[k] > 0 else -minus)
            for m in range(k, 3):
                cc = c[k] * c[m]
                if cc:
                    w2[(k, m)] = add(w2.get((k, m)), plus if cc > 0 else -plus)
    at = lambda k, m: w2[(min(k, m), max(k, m))]
    w2u = [at(k, 0) * u[0] + at(k, 1) * u[1] + at(k, 2) * u[2] for k in range(3)]
    uwu = u[0] * w2u[0] + u[1] * w2u[1] + u[2] * w2u[2]
    uu = u[0] * u[0] + u[1] * u[1] + u[2] * u[2]
    fluid = 1.0 - solid
    own = (1.0 - OMEGA) * fluid
    gain = OMEGA * fluid
    g_rho = gain * (w0 * (1.0 + 1.5 * uu) - 4.5 * uwu)
    g_mom = [gain * (3.0 * w1[k] + 9.0 * w2u[k] - 3.0 * (u[k] * w0)) for k in range(3)]
    out = [None] * 27
    for i in range(13):
        j = 26 - i
        odd = dot_c(DIRS[j], g_mom)
        out[j] = own * p[j] + solid * p[i] + (g_rho + odd)
        out[i] = own * p[i] + solid * p[j] + (g_rho - odd)
    out[13] = (own + solid) * p[13] + g_rho
    if f is None:
        return out, None
    blame = OMEGA * (p[13] * f[13])
    for i in range(13):
        j = 26 - i
        blame = blame + (p[i] * (f[j] - (1.0 - OMEGA) * f[i]) + p[j] * (f[i] - (1.0 - OMEGA) * f[j]))
    w1u = w1[0] * u[0] + w1[1] * u[1] + w1[2] * u[2]
    blame = blame - (OMEGA * rho) * (w0 * (1.0 - 1.5 * uu) + 3.0 * w1u + 4.5 * uwu)
    return out, blame


STRIP_ROW = (7, 6, 0, 1)


def sources(bp, ext):
    if bp == 0:
        return [(0, None, 0, None), (2, None, 2, None)] if ext else []
    if bp == 1:
        return [(0, None, None, 0)] + ([(1, None, 0, None), (None, 7, 2, None)] if ext else [])
    return [(2, None, None, 7)] + ([(3, None, 2, None), (None, 0, 0, None)] if ext else [])


def shift_z(t0, t1, dp, ins, lane):
    if dp == 1:
        return jnp.where(lane == 0, ins, roll_l(t0, 1)), roll_l(jnp.where(lane == 127, t0, t1), 1)
    if dp == -1:
        return roll_l(jnp.where(lane == 0, t1, t0), 127), jnp.where(lane == 127, ins, roll_l(t1, 127))
    return t0, t1


def direction(a, b, d):
    return 9 * (a + 1) + 3 * (b + 1) + d + 1


def stream(own, rows, strip_rows, out, out_rows, out_strip_rows, orient, gz, low, high):
    lane, sub = lanes(), subs()
    ext = out_rows is not None

    def body(x, carry):
        for a in (-1, 0, 1):
            for b in (-1, 0, 1):
                xs = x - orient * a
                bp = orient * b
                into = direction(a, b, 0) + orient * (2 * gz - 1)
                ins = roll_l(own[into, MINI, :], 127 - 2 * gz - 4 * xs)
                for d in (-1, 0, 1):
                    i = direction(a, b, d)
                    pair = shift_z(own[i, tile(2 * xs), :], own[i, tile(2 * xs + 1), :], orient * d, ins, lane)
                    for half in (0, 1):
                        v = pair[half]
                        if bp:
                            v = roll_s(v, bp % 8)
                        out[i, tile(2 * x + half), :] = v
        return carry

    lax.fori_loop(low, high, body, 0)

    for a in (-1, 0, 1):
        for b in (-1, 0, 1):
            bp, ap = orient * b, orient * a
            into = direction(a, b, 0) + orient * (2 * gz - 1)
            for k_in, row_in, k_out, row_out in sources(bp, ext):
                if k_in is None:
                    line = own[into, pl.ds(128 + row_in, 1), :]
                else:
                    line = strip_rows[into, pl.ds(STRIP_ROW[k_in], 1), :]
                ins = jnp.sum(jnp.where(lane == 4 * sub + 3 * gz, jnp.broadcast_to(line, (8, 128)), 0.0), axis=1, keepdims=True)
                for d in (-1, 0, 1):
                    i = direction(a, b, d)
                    if k_in is None:
                        t0, t1 = (own[i, pl.ds(8 * half + row_in, 8, stride=16), :] for half in (0, 1))
                    else:
                        t0, t1 = rows[i, k_in, 0:8, :], rows[i, k_in, 8:16, :]
                    pair = shift_z(t0, t1, orient * d, ins, lane)
                    for half in (0, 1):
                        v = pair[half]
                        if ap:
                            v = roll_s(v, ap % 8)
                        if k_out is None:
                            out[i, pl.ds(8 * half + row_out, 8, stride=16), :] = v
                        else:
                            out_rows[i, k_out, 8 * half : 8 * half + 8, :] = v

    wall = lane == 127 * gz
    for a in (-1, 0, 1):
        for b in (-1, 0, 1):
            i = direction(a, b, 0) + orient * (1 - 2 * gz)
            for x in range(low, high):
                here = tile(2 * x + gz)
                out[i, here, :] = jnp.where(wall, own[26 - i, here, :], out[i, here, :])
            if ext:
                for k in (0, 2):
                    here = tile(gz)
                    out_rows[i, k, here, :] = jnp.where(wall, rows[26 - i, k, here, :], out_rows[i, k, here, :])

    slot = lax.rem(lane, 4)
    edge = 1 - gz
    for a in (-1, 0, 1):
        for b in (-1, 0, 1):
            bp, ap = orient * b, orient * a
            outof = direction(a, b, 0) + orient * (1 - 2 * gz)
            need = [k for k, _, _, _ in sources(bp, ext) if k is not None]
            rim = jnp.zeros((8, 128), F32)
            for xe in range(8):
                src = own[outof, tile(2 * xe + edge), :]
                rim = jnp.where(lane == 4 * xe + 3 * gz, roll_l(src, 4 * xe + 1 + 2 * gz), rim)
            rim_rows = jnp.zeros((8, 128), F32)
            for k in need:
                src = pltpu.roll(roll_l(rows[outof, k, tile(edge), :], 1 + 2 * gz), 0, 1, stride=4, stride_axis=0)
                line = jnp.sum(jnp.where(lane == 4 * sub + 3 * gz, src, 0.0), axis=0, keepdims=True)
                rim_rows = jnp.where(sub == STRIP_ROW[k], line, rim_rows)
            for d in (-1, 0, 1):
                i = direction(a, b, d)
                dp = orient * d

                def shifted(v, edge_values):
                    if dp == 1:
                        v = jnp.where(slot == 0, edge_values, roll_l(v, 1))
                    if dp == -1:
                        v = jnp.where(slot == 3, edge_values, roll_l(v, 127))
                    return roll_l(v, (4 * ap) % 128) if ap else v

                vo = shifted(own[i, MINI, :], rim)
                vy = shifted(strip_rows[i], rim_rows) if need else None
                if bp == 0:
                    out[i, MINI, :] = vo
                    if ext:
                        out_strip_rows[i] = vy
                else:
                    last = 7 if bp == 1 else 0
                    out[i, MINI, :] = roll_s(jnp.where(sub == last, vy, vo), bp % 8)
                    if ext:
                        out_strip_rows[i] = roll_s(jnp.where(sub == last, vo, vy), bp % 8)


def entries(e, orient, stride, extra):
    others = [(r // 3, r % 3) for r in range(9)]
    number = lambda across, d: 3 * across + d if stride == 9 else 9 * across + d
    inward, outward = stride * (orient * e + 1), stride * (1 - orient * e)
    out = [(0, inward + number(c, d), 1, None, orient * (c - 1), 0) for c, d in others]
    out += [(0, stride + number(c, d), 1, None, orient * (c - 1), 0) for c, d in others]
    out += [(0, inward + number(c, d), 2, outward + number(c, d) if d != 1 else None, orient * (c - 1), orient * (d - 1)) for c, d in others]
    if extra:
        out += [(1, stride * (1 - e) + number(c, d), 1, None, 1 - c, 0) for c, d in others]
        out += [(2, 0, 1, None, 0, 0)]
    return out


def row_kinds(which, bp):
    if which == 1:
        return {1: (0,), 0: (), -1: (2,)}[bp]
    return {1: (0, 1), 0: (0, 2), -1: (2, 3)}[bp]


def near_plane(e):
    return 2 + 3 * ((e + 1) // 2)


def pack_faces(msg, e, orient, gz, arrays):
    near = near_plane(e)
    walls = {-1: (lanes() == 0) & (gz == 0), 1: (lanes() == 127) & (gz == 1)}
    for n, (which, i, layer, stash, _, dp) in enumerate(entries(e, orient, 9, len(arrays) > 1)):
        ref, plane = arrays[which], near if layer == 1 else near - e
        for half in (0, 1):
            v = ref[i, tile(2 * plane + half), :]
            if stash is not None and half == (dp + 1) // 2:
                v = jnp.where(walls[dp], ref[stash, tile(2 * near + half), :], v)
            msg[(2 * n + half) * 8 : (2 * n + half) * 8 + 8, :] = v


def unpack_faces(msg, s, orient, arrays):
    near = near_plane(s) + s
    for n, (which, i, layer, stash, _, dp) in enumerate(entries(-s, orient, 9, len(arrays) > 1)):
        ref, plane = arrays[which], near if layer == 1 else near + s
        for half in (0, 1):
            v = msg[(2 * n + half) * 8 : (2 * n + half) * 8 + 8, :]
            ref[i, tile(2 * plane + half), :] = v
            if stash is not None and half == (dp + 1) // 2:
                ref[stash, tile(2 * near + half), :] = v


def pack_sides(msg, e, orient, gz, arrays, strips):
    near = 7 * ((e + 1) // 2)
    lane = lax.broadcasted_iota(jnp.int32, (4, 128), 1)
    walls = {-1: (lane == 0) & (gz == 0), 1: (lane == 127) & (gz == 1)}
    items = entries(e, orient, 3, len(arrays) > 1)
    for n, (which, i, layer, stash, _, dp) in enumerate(items):
        ref, row = arrays[which], near if layer == 1 else near - e
        for half in (0, 1):
            v = ref[i, pl.ds(32 + 8 * half + row, 4, stride=16), :]
            if stash is not None and half == (dp + 1) // 2:
                v = jnp.where(walls[dp], ref[stash, pl.ds(32 + 8 * half + near, 4, stride=16), :], v)
            msg[8 * n + 4 * half : 8 * n + 4 * half + 4, :] = v
        msg[8 * len(items) + n : 8 * len(items) + n + 1, :] = strips[which][i, pl.ds(row, 1), :]


def unpack_sides(msg, s, orient, rows, strip_rows):
    k = s + 1
    near = 7 * ((1 - s) // 2)
    items = entries(-s, orient, 3, len(rows) > 1)
    for n, (which, i, layer, _, _, _) in enumerate(items):
        for half in (0, 1):
            rows[which][i, k + layer - 1, 8 * half + 2 : 8 * half + 6, :] = msg[8 * n + 4 * half : 8 * n + 4 * half + 4, :]
        row = near if layer == 1 else near + s
        strip_rows[which][i, pl.ds(row, 1), :] = msg[8 * len(items) + n : 8 * len(items) + n + 1, :]


def edge_rows(e, orient, extra):
    return 2 * sum(len(row_kinds(item[0], item[4])) for item in entries(e, orient, 9, extra))


def pack_edges(msg, e, orient, gz, rows, strips, strip_rows):
    near = near_plane(e)
    lane = lanes()
    lane2 = lax.broadcasted_iota(jnp.int32, (2, 128), 1)
    half2 = lax.broadcasted_iota(jnp.int32, (2, 128), 0)
    walls = {-1: (lane2 == 0) & (half2 == 0) & (gz == 0), 1: (lane2 == 127) & (half2 == 1) & (gz == 1)}
    items = entries(e, orient, 9, len(rows) > 1)
    at = 0
    tiles = (len(items) + 31) // 32
    packed = [[jnp.zeros((8, 128), F32) for _ in range(tiles)] for _ in range(2)]
    for n, (which, i, layer, stash, bp, dp) in enumerate(items):
        plane = near if layer == 1 else near - e
        for k in row_kinds(which, bp):
            v = rows[which][i, k, pl.ds(plane, 2, stride=8), :]
            if stash is not None:
                v = jnp.where(walls[dp], rows[which][stash, k, pl.ds(near, 2, stride=8), :], v)
            msg[at : at + 2, :] = v
            at += 2
        s = 4 * (n % 32)
        for kind, v in enumerate((strips[which][i], strip_rows[which][i])):
            moved = roll_l(v, mod128(s - 4 * plane))
            packed[kind][n // 32] = jnp.where((lane >= s) & (lane < s + 4), moved, packed[kind][n // 32])
    at = -(-at // 8) * 8
    for v in packed[0] + packed[1]:
        msg[at : at + 8, :] = v
        at += 8


def unpack_edges(msg, s, orient, rows, owns, strip_rows):
    near = near_plane(s) + s
    plane_of = lax.div(lanes(), 4)
    items = entries(-s, orient, 9, len(rows) > 1)
    at = 0
    base = -(-edge_rows(1, orient, len(rows) > 1) // 8) * 8
    tiles = (len(items) + 31) // 32
    for n, (which, i, layer, stash, bp, _) in enumerate(items):
        plane = near if layer == 1 else near + s
        for k in row_kinds(which, bp):
            v = msg[at : at + 2, :]
            at += 2
            rows[which][i, k, pl.ds(plane, 2, stride=8), :] = v
            if stash is not None:
                rows[which][stash, k, pl.ds(near, 2, stride=8), :] = v
        for kind in (0, 1):
            r = base + 8 * (tiles * kind + n // 32)
            moved = roll_l(msg[r : r + 8, :], mod128(4 * plane - 4 * (n % 32)))
            if kind:
                strip_rows[which][i] = jnp.where(plane_of == plane, moved, strip_rows[which][i])
            else:
                owns[which][i, MINI, :] = jnp.where(plane_of == plane, moved, owns[which][i, MINI, :])


def reflect_rows(rows, orient):
    for a in range(3):
        for d in (0, 2):
            for k, b in ((0, 1 + orient), (2, 1 - orient)):
                rows[9 * a + 3 * (2 - b) + d, k] = rows[9 * a + 3 * b + d, k + 1]


def solid_of(blockage, mask):
    m = mask.astype(F32)
    return blockage * (1.0 - m) + m


def cut_kernel(pops_hbm, block_hbm, mask_hbm, cot_hbm, msg, pops, block, mask, cot, sems):
    gz = lax.axis_index("gz")
    lane = lanes()
    z = pl.ds(pl.multiple_of(128 * (1 - gz), 128), 128)
    copies = []
    for n, (src, dst) in enumerate(((pops_hbm, pops), (cot_hbm, cot))):
        copies.append(pltpu.make_async_copy(src.at[:, :, :, z], dst, sems.at[n]))
    for n, (src, dst) in enumerate(((block_hbm, block), (mask_hbm, mask))):
        copies.append(pltpu.make_async_copy(src.at[:, :, z], dst, sems.at[n + 2]))
    for copy in copies:
        copy.start()
    for copy in copies:
        copy.wait()
    for n in range(7):
        acc = jnp.zeros((8, 128), F32)
        for j in range(8):
            slot = 8 * n + j
            if slot > 54:
                break
            for x in range(4):
                if slot == 54:
                    edge = solid_of(block[x], mask[x])
                else:
                    ref, i = (pops, slot) if slot < 27 else (cot, slot - 27)
                    edge = ref[i, x]
                at = 16 * j + 4 * x
                moved = roll_l(edge, mod128(at + 4 - 4 * gz))
                acc = jnp.where((lane >= at) & (lane < at + 4), moved, acc)
        msg[8 * n : 8 * n + 8, :] = acc


def first_kernel(pops, block, mask, cot, after, tx, ax, sx, msg0, msg1):
    gz = lax.axis_index("gz")

    def body(x, carry):
        for half in (0, 1):
            z = pl.ds(128 * half, 128)
            here = tile(2 * (x + 2) + half)
            s = solid_of(block[x, :, z], mask[x, :, z])
            sx[0, here, :] = s
            f = [pops[i, x, :, z] for i in range(27)]
            rho, u = moments(f)
            out = collide(f, s, rho, u)
            for i in range(27):
                tx[i, here, :] = out[i]
                ax[i, here, :] = cot[i, x, :, z]
        return carry

    lax.fori_loop(0, 4, body, 0)
    for msg, e in zip((msg0, msg1), sides("gx")):
        pack_faces(msg, e, 1, gz, (tx, ax, sx))


def strip_kernel(cut, tx, ax, sx, tm, am, sm, msg0, msg1):
    gz = lax.axis_index("gz")

    def slot(n):
        return roll_l(cut[8 * (n // 8) : 8 * (n // 8) + 8, :], (8 - 16 * (n % 8)) % 128)

    s = slot(54)
    sm[0] = s
    f = [slot(i) for i in range(27)]
    rho, u = moments(f)
    out = collide(f, s, rho, u)
    for i in range(27):
        tm[i] = out[i]
        am[i] = slot(27 + i)
    for msg, e in zip((msg0, msg1), sides("gy")):
        pack_sides(msg, e, 1, gz, (tx, ax, sx), (tm, am, sm))


def edge_kernel(tm, am, sm, got0, got1, msg0, msg1, tr, ar, sr, tmr, amr, smr):
    gz = lax.axis_index("gz")
    rows, strip_rows = (tr, ar, sr), (tmr, amr, smr)
    for msg, s in zip((got0, got1), sides("gy")):
        unpack_sides(msg, s, 1, rows, strip_rows)
    for msg, e in zip((msg0, msg1), sides("gx")):
        pack_edges(msg, e, 1, gz, rows, (tm, am, sm), strip_rows)


def edge_kernel_2(tm, got0, got1, msg0, msg1, tr, tmr):
    gz = lax.axis_index("gz")
    for msg, s in zip((got0, got1), sides("gy")):
        unpack_sides(msg, s, -1, (tr,), (tmr,))
    for msg, e in zip((msg0, msg1), sides("gx")):
        pack_edges(msg, e, -1, gz, (tr,), (tm,), (tmr,))


def gather_in(pairs, strips):
    def body(n, carry):
        for src, dst in pairs:
            for i in range(src.shape[0]):
                dst[i, tile(n), :] = src[i, tile(n), :]
        return carry

    lax.fori_loop(4, 12, body, 0)
    for (_, dst), strip in zip(pairs, strips):
        for i in range(strip.shape[0]):
            dst[i, MINI, :] = strip[i]


def receive(orient, owns, rows, strip_rows, by_y, faces, edges):
    for msg, s in zip(by_y, sides("gy")):
        unpack_sides(msg, s, orient, rows, strip_rows)
    for face, edge, s in zip(faces, edges, sides("gx")):
        unpack_faces(face, s, orient, owns)
        unpack_edges(edge, s, orient, rows, owns, strip_rows)
    reflect_rows(rows[0], orient)


def middle_kernel(
    tx, ax, sx, tm, am, sm, y0, y1, x0, x1, e0, e1,
    a2, a2m, f1, u_own, u_rows, u_strip, s_own, s_rows, s_strip, q2, ym0, ym1, xm0, xm1,
    t, a, tr, ar, tmr, amr, fr, fmr, c, cr, cmr, f2, p,
):
    gz = lax.axis_index("gz")
    gather_in(((tx, t), (ax, a), (sx, s_own)), (tm, am, sm))
    receive(1, (t, a, s_own), (tr, ar, s_rows), (tmr, amr, s_strip), (y0, y1), (x0, x1), (e0, e1))
    stream(t, tr, tmr, f1, fr, fmr, 1, gz, 1, 7)

    def collide_at(load, solid, store, store_u):
        f = [load(i) for i in range(27)]
        rho, u = moments(f)
        for n, v in enumerate([rho] + u):
            store_u(n, v)
        out = collide(f, solid, rho, u)
        for i in range(27):
            store(i, out[i])

    def again(k, carry):
        here = tile(jnp.where(k == 12, 16, k + 2))

        def put(i, v):
            c[i, here, :] = v

        def put_u(n, v):
            u_own[n, here, :] = v

        collide_at(lambda i: f1[i, here, :], s_own[0, here, :], put, put_u)
        return carry

    lax.fori_loop(0, 13, again, 0)

    def again_rows(k, carry):
        for half in (0, 1):
            here = tile(half)

            def put(i, v):
                cr[i, 2 * k, here, :] = v

            def put_u(n, v):
                u_rows[n, 2 * k, here, :] = v

            collide_at(lambda i: fr[i, 2 * k, here, :], s_rows[0, 2 * k, here, :], put, put_u)
        return carry

    lax.fori_loop(0, 2, again_rows, 0)

    def put_strip(i, v):
        cmr[i] = v

    def put_strip_u(n, v):
        u_strip[n] = v

    collide_at(lambda i: fmr[i], s_strip[0], put_strip, put_strip_u)
    stream(c, cr, cmr, f2, None, None, 1, gz, 2, 6)
    stream(a, ar, amr, p, None, None, -1, gz, 2, 6)

    def back(here):
        f = [f2[i, here, :] for i in range(27)]
        rho, u = moments(f)
        return pull_back([p[i, here, :] for i in range(27)], s_own[0, here, :], u, f, rho)

    def back_own(k, carry):
        here = tile(k + 4)
        out, blame = back(here)
        for i in range(27):
            a2[i, here, :] = out[i]
        q2[tile(k), :] = blame
        return carry

    lax.fori_loop(0, 8, back_own, 0)
    out, _ = back(MINI)
    for i in range(27):
        a2m[i] = out[i]
    for msg, e in zip((ym0, ym1), sides("gy")):
        pack_sides(msg, e, -1, gz, (a2,), (a2m,))
    for msg, e in zip((xm0, xm1), sides("gx")):
        pack_faces(msg, e, -1, gz, (a2,))


def last_kernel(
    a2, a2m, pops, mask, f1, u_own, u_rows, u_strip, s_own, s_rows, s_strip, q2, y0, y1, x0, x1, e0, e1,
    adjoint, grad,
    t, tr, tmr, p, pr, pmr, c, cr, cmr, q1,
):
    gz = lax.axis_index("gz")
    gather_in(((a2, t),), (a2m,))
    receive(-1, (t,), (tr,), (tmr,), (y0, y1), (x0, x1), (e0, e1))
    stream(t, tr, tmr, p, pr, pmr, -1, gz, 1, 7)

    def again(k, carry):
        here = tile(jnp.where(k == 12, 16, k + 2))
        u = [u_own[n, here, :] for n in (1, 2, 3)]
        out, blame = pull_back([p[i, here, :] for i in range(27)], s_own[0, here, :], u, [f1[i, here, :] for i in range(27)], u_own[0, here, :])
        for i in range(27):
            c[i, here, :] = out[i]
        q1[here, :] = blame
        return carry

    lax.fori_loop(0, 13, again, 0)

    def again_rows(k, carry):
        for half in (0, 1):
            here = tile(half)
            u = [u_rows[n, 2 * k, here, :] for n in (1, 2, 3)]
            out, _ = pull_back([pr[i, 2 * k, here, :] for i in range(27)], s_rows[0, 2 * k, here, :], u)
            for i in range(27):
                cr[i, 2 * k, here, :] = out[i]
        return carry

    lax.fori_loop(0, 2, again_rows, 0)
    out, _ = pull_back([pmr[i] for i in range(27)], s_strip[0], [u_strip[n] for n in (1, 2, 3)])
    for i in range(27):
        cmr[i] = out[i]
    stream(c, cr, cmr, p, None, None, -1, gz, 2, 6)

    def back(x, carry):
        for half in (0, 1):
            z = pl.ds(128 * half, 128)
            here = tile(2 * x + 4 + half)
            f = [pops[i, x, :, z] for i in range(27)]
            rho, u = moments(f)
            out, blame = pull_back([p[i, here, :] for i in range(27)], s_own[0, here, :], u, f, rho)
            for i in range(27):
                adjoint[i, x, :, z] = out[i]
            grad[x, :, z] = (1.0 - mask[x, :, z].astype(F32)) * (q1[here, :] + q2[tile(2 * x + half), :] + blame)
        return carry

    lax.fori_loop(0, 4, back, 0)


def call(kernel, outs, scratch=(), name=None, mib=8, in_specs=None):
    return pl.pallas_call(
        kernel,
        out_shape=[jax.ShapeDtypeStruct(s, F32) for s in outs],
        scratch_shapes=[pltpu.VMEM(s, F32) if isinstance(s, tuple) else s for s in scratch],
        **({} if in_specs is None else {"in_specs": in_specs}),
        compiler_params=pltpu.CompilerParams(vmem_limit_bytes=mib * 1024 * 1024),
        name=name,
    )


def swap(x, axis, odd):
    n = lax.axis_size(axis)
    pairs = [(i, (i ^ 1) if not odd else ((i + 1) % n if i % 2 else (i - 1) % n)) for i in range(n)]
    return lax.ppermute(x, axis, pairs)


BIG = (27, ROWS, 128)
ONE = (1, ROWS, 128)
STRIP = (27, 8, 128)
STRIP1 = (1, 8, 128)
HALO = (27, 4, 16, 128)
HALO1 = (1, 4, 16, 128)


def face_shape(n):
    return (16 * n, 128)


def side_shape(n):
    return (8 * n + -(-n // 8) * 8, 128)


def edge_shape(extra):
    n = 37 if extra else 27
    return (-(-edge_rows(1, 1, extra) // 8) * 8 + 16 * (-(-n // 32)), 128)


def swaps(pair, axis):
    return [swap(pair[0], axis, False), swap(pair[1], axis, True)]


def body(populations, blockage, solid_mask, cotangent):
    halves = [pltpu.VMEM((27, 4, 8, 128), F32), pltpu.VMEM((4, 8, 128), F32), pltpu.VMEM((4, 8, 128), jnp.int32), pltpu.VMEM((27, 4, 8, 128), F32)]
    anywhere = [pl.BlockSpec(memory_space=pltpu.HBM)] * 4
    (cut,) = call(cut_kernel, [(56, 128)], scratch=halves + [pltpu.SemaphoreType.DMA((4,))], name="cut", mib=60, in_specs=anywhere)(
        populations, blockage, solid_mask, cotangent
    )
    tx, ax, sx, *faces = call(first_kernel, [BIG, BIG, ONE, face_shape(37), face_shape(37)], name="first")(
        populations, blockage, solid_mask, cotangent, cut
    )
    cut = lax.ppermute(cut, "gz", [(0, 1), (1, 0)])
    tm, am, sm, *by_y = call(strip_kernel, [STRIP, STRIP, STRIP1, side_shape(37), side_shape(37)], name="strip")(cut, tx, ax, sx)
    by_y = swaps(by_y, "gy")
    faces, _ = lax.optimization_barrier((faces, tm))
    faces = swaps(faces, "gx")
    edges = call(
        edge_kernel, [edge_shape(True)] * 2, scratch=[HALO, HALO, HALO1, STRIP, STRIP, STRIP1], name="edge", mib=12
    )(tm, am, sm, *by_y)
    edges = swaps(edges, "gx")
    a2, a2m, f1, u_own, u_rows, u_strip, s_own, s_rows, s_strip, q2, *out = call(
        middle_kernel,
        [BIG, STRIP, BIG, (4, ROWS, 128), (4, 4, 16, 128), (4, 8, 128), ONE, HALO1, STRIP1, (64, 128)]
        + [side_shape(27)] * 2
        + [face_shape(27)] * 2,
        scratch=[BIG, BIG, HALO, HALO, STRIP, STRIP, HALO, STRIP, BIG, HALO, STRIP, BIG, BIG],
        name="middle",
        mib=24,
    )(tx, ax, sx, tm, am, sm, *by_y, *faces, *edges)
    by_y = swaps(out[:2], "gy")
    faces = swaps(out[2:], "gx")
    edges = call(edge_kernel_2, [edge_shape(False)] * 2, scratch=[HALO, STRIP], name="edge2", mib=8)(a2m, *by_y)
    edges = swaps(edges, "gx")
    adjoint, grad = call(
        last_kernel,
        [populations.shape, blockage.shape],
        scratch=[BIG, HALO, STRIP, BIG, HALO, STRIP, BIG, HALO, STRIP, (ROWS, 128)],
        name="last",
        mib=20,
    )(a2, a2m, populations, solid_mask, f1, u_own, u_rows, u_strip, s_own, s_rows, s_strip, q2, *by_y, *faces, *edges)
    return adjoint, grad


def solution(mesh):
    placed = (P(None, "gx", "gy", "gz"), P("gx", "gy", "gz"), P("gx", "gy", "gz"), P(None, "gx", "gy", "gz"))
    return jax.shard_map(
        body, mesh=mesh, in_specs=placed, out_specs=(P(None, "gx", "gy", "gz"), P("gx", "gy", "gz")), check_vma=False
    )
```

time: 68.4 us -> 62.4 us (0.912)
  waiting for transfers between devices: 33.5 us -> 17.5 us
  starting transfers between devices: 18.3 us -> 27.3 us
  local copies, waits for them, and re-layouts: 0.02 us -> 0.78 us
    ppermute x8 -> x12, waiting for transfers between devices: 31 us -> 16.3 us  [swap(): return lax.ppermute(x, axis, pairs)]
    ppermute x8 -> x12, starting transfers between devices: 16.7 us -> 25.6 us  [swap(): return lax.ppermute(x, axis, pairs)]
    ppermute x1, waiting for transfers between devices: 2.51 us -> 1.19 us  [body(): cut = lax.ppermute(cut, 'gz', [(0, 1), (1, 0)])]
    unnamed x8 -> x10, local copies, waits for them, and re-layouts: 0.02 us -> 0.78 us
    pallas_call x5 -> x6, Pallas kernels: 13.1 us -> 13.7 us  [the longest x1 6.26 us: body(): call(middle_kernel, [BIG, STRIP, BIG, (4, ROWS, 128), (4, 4, 16, 128), (4...]
  transfers between devices with their start and end apart: 9 -> 13, of which waited for: 7 -> 7; matrix products, arithmetic and copies ran while one was open for 0% -> 0% of each run, Pallas kernels for 0% -> 2%
where the time goes in v2:
time: 62.4 us; the launch traced here: 62.2 us
  starting transfers between devices  27.3 us (44%)
  waiting for transfers between devices  17.5 us (28%)
  Pallas kernels  15.9 us (25%)
  local copies, waits for them, and re-layouts  0.78 us (1%)
  between operations  0.72 us (1%)
    ppermute x12, starting transfers between devices, swap(): return lax.ppermute(x, axis, pairs)  25.6 us
    ppermute x12, waiting for transfers between devices, swap(): return lax.ppermute(x, axis, pairs)  16.3 us
    pallas_call x1, Pallas kernels, body(): call(middle_kernel, [BIG, STRIP, BIG, (4, ROWS, 128), (4, 4, 16, 128), (4...  6.26 us
    pallas_call x1, Pallas kernels, body(): call(last_kernel, [populations.shape, blockage.shape], scratch=[BIG, HALO...  5.97 us
    pallas_call x1, Pallas kernels, body(): call(cut_kernel, [(56, 128)], scratch=halves + [pltpu.SemaphoreType.DMA((...  2.23 us
    ppermute x1, starting transfers between devices, body(): cut = lax.ppermute(cut, 'gz', [(0, 1), (1, 0)])  1.65 us
  transfers between devices with their start and end apart: 13, of which 7 were waited for; matrix products, arithmetic and copies ran while one was open for 0% of the time, Pallas kernels for 2%

profile of v2, /device:TPU:0, one launch (start us, length us, event | category | flops | bytes accessed | tf_op | source)
XLA Modules:
  0.0 62.2 jit_solution(17427535097425358688)
XLA Ops:
  0.6 0.0 copy-start.2
  0.6 0.0 copy-start
  0.7 0.0 copy-start.1
  0.7 0.0 copy-start.3
  0.7 2.2 %cut.1.after = f32[56,128]{1,0:T(8,128)} custom-call(f32[27,4,8,256]{3,2,1,0:T(8,128)} %pops.3, f32[4,8,256]{2,1,0:T(8,128)} %block.1, s32[4,8,256]{2,1,0:T(8,128)} %mask.3, f32[27,4,8,256]{3,2,1,0:T(8,128)} %cot.1), custom_call_target="tpu_custom_call" | custom-call | tf_op jit(solution)/shard_map/cut/pallas_call | solution.py:688
  2.9 1.7 %collective-permute-start = (f32[56,128]{1,0:T(8,128)}, f32[56,128]{1,0:T(8,128)S(1)}, u32[]{:S(2)}, u32[]{:S(2)}) collective-permute-start(f32[56,128]{1,0:T(8,128)} %cut.1.after), channel_id=1, source_target_pairs={{0,1},{1,0},{2,3},{3,2},{4,5},{5,4},{6,7},{7,6},{8,9},{9,8},{10,11... | collective-permute-start | bytes 86024 | tf_op jit(solution)/shard_map/ppermute | solution.py:694
  4.6 0.0 copy-done.2
  4.6 0.0 copy-done
  4.6 0.0 copy-done.1
  4.6 0.0 copy-done.3
  4.6 0.0 copy-start.4
  4.6 0.8 %copy-done.4 = f32[56,128]{1,0:T(8,128)S(1)} copy-done((f32[56,128]{1,0:T(8,128)S(1)}, f32[56,128]{1,0:T(8,128)}, u32[]{:S(2)}) %copy-start.4) | copy-done | bytes 28696
  5.3 0.5 first.1
  5.9 1.2 %collective-permute-done.cut = f32[56,128]{1,0:T(8,128)S(1)} collective-permute-done((f32[56,128]{1,0:T(8,128)}, f32[56,128]{1,0:T(8,128)S(1)}, u32[]{:S(2)}, u32[]{:S(2)}) %collective-permute-start) | collective-permute-done | bytes 28704 | tf_op jit(solution)/shard_map/ppermute | solution.py:694
  7.1 0.2 strip.1
  7.3 3.2 %collective-permute-start.3 = (f32[592,128]{1,0:T(8,128)S(1)}, f32[592,128]{1,0:T(8,128)S(1)}, u32[]{:S(2)}, u32[]{:S(2)}) collective-permute-start(f32[592,128]{1,0:T(8,128)S(1)} %get-tuple-element.42), channel_id=1, source_target_pairs={{0,16},{16,0},{32,48},{48,32},{64,80},{80,64},{96,112},{112,96},{1... | collective-permute-start | bytes 909320 | tf_op jit(solution)/shard_map/ppermute | solution.py:657
  10.5 4.0 %collective-permute-start.4 = (f32[592,128]{1,0:T(8,128)S(1)}, f32[592,128]{1,0:T(8,128)S(1)}, u32[]{:S(2)}, u32[]{:S(2)}) collective-permute-start(f32[592,128]{1,0:T(8,128)S(1)} %get-tuple-element.43), channel_id=1, source_target_pairs={{0,112},{16,32},{32,16},{48,64},{64,48},{80,96},{96,80},{112,0},{1... | collective-permute-start | bytes 909320 | tf_op jit(solution)/shard_map/ppermute | solution.py:657
  14.5 0.0 collective-permute-start.1
  14.5 3.1 %collective-permute-start.2 = (f32[336,128]{1,0:T(8,128)S(1)}, f32[336,128]{1,0:T(8,128)S(1)}, u32[]{:S(2)}, u32[]{:S(2)}) collective-permute-start(f32[336,128]{1,0:T(8,128)S(1)} %get-tuple-element.39), channel_id=1, source_target_pairs={{0,14},{2,4},{4,2},{6,8},{8,6},{10,12},{12,10},{14,0},{1,15},{3,5}... | collective-permute-start | bytes 516104 | tf_op jit(solution)/shard_map/ppermute | solution.py:657
  17.6 0.0 collective-permute-done.1.got0.y0
  17.6 3.1 %collective-permute-done.2.got1.y1 = f32[336,128]{1,0:T(8,128)S(1)} collective-permute-done((f32[336,128]{1,0:T(8,128)S(1)}, f32[336,128]{1,0:T(8,128)S(1)}, u32[]{:S(2)}, u32[]{:S(2)}) %collective-permute-start.2) | collective-permute-done | bytes 172064 | tf_op jit(solution)/shard_map/ppermute | solution.py:657
  20.7 0.4 edge.1
  21.1 1.0 %collective-permute-start.5 = (f32[160,128]{1,0:T(8,128)S(1)}, f32[160,128]{1,0:T(8,128)S(1)}, u32[]{:S(2)}, u32[]{:S(2)}) collective-permute-start(f32[160,128]{1,0:T(8,128)S(1)} %get-tuple-element.44), channel_id=1, source_target_pairs={{0,16},{16,0},{32,48},{48,32},{64,80},{80,64},{96,112},{112,96},{1... | collective-permute-start | bytes 245768 | tf_op jit(solution)/shard_map/ppermute | solution.py:657
  22.1 2.5 %collective-permute-start.6 = (f32[160,128]{1,0:T(8,128)S(1)}, f32[160,128]{1,0:T(8,128)S(1)}, u32[]{:S(2)}, u32[]{:S(2)}) collective-permute-start(f32[160,128]{1,0:T(8,128)S(1)} %get-tuple-element.45), channel_id=1, source_target_pairs={{0,112},{16,32},{32,16},{48,64},{64,48},{80,96},{96,80},{112,0},{1... | collective-permute-start | bytes 245768 | tf_op jit(solution)/shard_map/ppermute | solution.py:657
  24.5 3.1 %collective-permute-done.5.e0 = f32[160,128]{1,0:T(8,128)S(1)} collective-permute-done((f32[160,128]{1,0:T(8,128)S(1)}, f32[160,128]{1,0:T(8,128)S(1)}, u32[]{:S(2)}, u32[]{:S(2)}) %collective-permute-start.5) | collective-permute-done | bytes 81952 | tf_op jit(solution)/shard_map/ppermute | solution.py:657
  27.6 2.6 %collective-permute-done.6.e1 = f32[160,128]{1,0:T(8,128)S(1)} collective-permute-done((f32[160,128]{1,0:T(8,128)S(1)}, f32[160,128]{1,0:T(8,128)S(1)}, u32[]{:S(2)}, u32[]{:S(2)}) %collective-permute-start.6) | collective-permute-done | bytes 81952 | tf_op jit(solution)/shard_map/ppermute | solution.py:657
  30.2 0.0 collective-permute-done.3.x0
  30.2 0.0 collective-permute-done.4.x1
  30.2 6.3 %middle.1 = (f32[27,136,128]{2,1,0:T(8,128)S(1)}, f32[27,8,128]{2,1,0:T(8,128)S(1)}, f32[27,136,128]{2,1,0:T(8,128)S(1)}, f32[4,136,128]{2,1,0:T(8,128)S(1)}, f3...) custom-call(f32[27,136,128]{2,1,0:T(8,128)S(1)} %get-tuple-element.3, ...), custom_call_target="tpu_custom_call" | custom-call | tf_op jit(solution)/shard_map/middle/pallas_call | solution.py:703
  36.5 1.4 %collective-permute-start.9 = (f32[432,128]{1,0:T(8,128)S(1)}, f32[432,128]{1,0:T(8,128)S(1)}, u32[]{:S(2)}, u32[]{:S(2)}) collective-permute-start(f32[432,128]{1,0:T(8,128)S(1)} %get-tuple-element.58), channel_id=1, source_target_pairs={{0,16},{16,0},{32,48},{48,32},{64,80},{80,64},{96,112},{112,96},{1... | collective-permute-start | bytes 663560 | tf_op jit(solution)/shard_map/ppermute | solution.py:657
  37.9 2.1 %collective-permute-start.10 = (f32[432,128]{1,0:T(8,128)S(1)}, f32[432,128]{1,0:T(8,128)S(1)}, u32[]{:S(2)}, u32[]{:S(2)}) collective-permute-start(f32[432,128]{1,0:T(8,128)S(1)} %get-tuple-element.59), channel_id=1, source_target_pairs={{0,112},{16,32},{32,16},{48,64},{64,48},{80,96},{96,80},{112,0},{1... | collective-permute-start | bytes 663560 | tf_op jit(solution)/shard_map/ppermute | solution.py:657
  40.0 0.0 collective-permute-start.7
  40.0 3.1 %collective-permute-start.8 = (f32[248,128]{1,0:T(8,128)S(1)}, f32[248,128]{1,0:T(8,128)S(1)}, u32[]{:S(2)}, u32[]{:S(2)}) collective-permute-start(f32[248,128]{1,0:T(8,128)S(1)} %get-tuple-element.57), channel_id=1, source_target_pairs={{0,14},{2,4},{4,2},{6,8},{8,6},{10,12},{12,10},{14,0},{1,15},{3,5}... | collective-permute-start | bytes 380936 | tf_op jit(solution)/shard_map/ppermute | solution.py:657
  43.1 0.0 collective-permute-done.7.got0.y0
  43.1 2.6 %collective-permute-done.8.got1.y1 = f32[248,128]{1,0:T(8,128)S(1)} collective-permute-done((f32[248,128]{1,0:T(8,128)S(1)}, f32[248,128]{1,0:T(8,128)S(1)}, u32[]{:S(2)}, u32[]{:S(2)}) %collective-permute-start.8) | collective-permute-done | bytes 127008 | tf_op jit(solution)/shard_map/ppermute | solution.py:657
  45.7 0.3 edge2.1
  46.0 2.4 %collective-permute-start.11 = (f32[128,128]{1,0:T(8,128)S(1)}, f32[128,128]{1,0:T(8,128)S(1)}, u32[]{:S(2)}, u32[]{:S(2)}) collective-permute-start(f32[128,128]{1,0:T(8,128)S(1)} %get-tuple-element.60), channel_id=1, source_target_pairs={{0,16},{16,0},{32,48},{48,32},{64,80},{80,64},{96,112},{112,96},{1... | collective-permute-start | bytes 196616 | tf_op jit(solution)/shard_map/ppermute | solution.py:657
  48.3 2.9 %collective-permute-start.12 = (f32[128,128]{1,0:T(8,128)S(1)}, f32[128,128]{1,0:T(8,128)S(1)}, u32[]{:S(2)}, u32[]{:S(2)}) collective-permute-start(f32[128,128]{1,0:T(8,128)S(1)} %get-tuple-element.61), channel_id=1, source_target_pairs={{0,112},{16,32},{32,16},{48,64},{64,48},{80,96},{96,80},{112,0},{1... | collective-permute-start | bytes 196616 | tf_op jit(solution)/shard_map/ppermute | solution.py:657
  51.3 0.6 collective-permute-done.11.e0
  51.8 4.4 %collective-permute-done.12.e1 = f32[128,128]{1,0:T(8,128)S(1)} collective-permute-done((f32[128,128]{1,0:T(8,128)S(1)}, f32[128,128]{1,0:T(8,128)S(1)}, u32[]{:S(2)}, u32[]{:S(2)}) %collective-permute-start.12) | collective-permute-done | bytes 65568 | tf_op jit(solution)/shard_map/ppermute | solution.py:657
  56.2 0.0 collective-permute-done.9.x0
  56.2 0.0 collective-permute-done.10.x1
  56.2 6.0 %last.1 = (f32[27,4,8,256]{3,2,1,0:T(8,128)}, f32[4,8,256]{2,1,0:T(8,128)}) custom-call(f32[27,136,128]{2,1,0:T(8,128)S(1)} %get-tuple-element.46.a2, f32[27,8,128]{2,1,0:T(8,128)S(1)} %get-tuple-element.47.tm.a2m, f32[27,4,8,256]{3,2,1,0:T(8,128)S(1)} %copy-done, s32[4,8,256]{2,1,0:T(8,128)S(1)} %copy-done.2, f32[27,136,128]{2,1,0:T(8,128)S(1)} %get-tuple-element.48.f1, ...), custom_call_target="tpu_custom_call" | custom-call | tf_op jit(solution)/shard_map/last/pallas_call | solution.py:716
Async XLA Ops:
  0.6 3.9 %copy-start.2 = (s32[4,8,256]{2,1,0:T(8,128)S(1)}, s32[4,8,256]{2,1,0:T(8,128)}, u32[]{:S(2)}) copy-start(s32[4,8,256]{2,1,0:T(8,128)} %mask.3) | copy-start | bytes 98308
  0.6 3.9 %copy-start = (f32[27,4,8,256]{3,2,1,0:T(8,128)S(1)}, f32[27,4,8,256]{3,2,1,0:T(8,128)}, u32[]{:S(2)}) copy-start(f32[27,4,8,256]{3,2,1,0:T(8,128)} %pops.3) | copy-start | bytes 2654212
  0.7 3.9 %copy-start.1 = (f32[27,4,8,256]{3,2,1,0:T(8,128)S(1)}, f32[27,4,8,256]{3,2,1,0:T(8,128)}, u32[]{:S(2)}) copy-start(f32[27,4,8,256]{3,2,1,0:T(8,128)} %cot.1) | copy-start | bytes 2654212
  0.7 3.9 %copy-start.3 = (f32[4,8,256]{2,1,0:T(8,128)S(1)}, f32[4,8,256]{2,1,0:T(8,128)}, u32[]{:S(2)}) copy-start(f32[4,8,256]{2,1,0:T(8,128)} %block.1) | copy-start | bytes 98308
  2.9 4.2 %collective-permute-start = (f32[56,128]{1,0:T(8,128)}, f32[56,128]{1,0:T(8,128)S(1)}, u32[]{:S(2)}, u32[]{:S(2)}) collective-permute-start(f32[56,128]{1,0:T(8,128)} %cut.1.after), channel_id=1, source_target_pairs={{0,1},{1,0},{2,3},{3,2},{4,5},{5,4},{6,7},{7,6},{8,9},{9,8},{10,11... | collective-permute-start | bytes 86024 | tf_op jit(solution)/shard_map/ppermute | solution.py:694
  4.6 0.8 %copy-start.4 = (f32[56,128]{1,0:T(8,128)S(1)}, f32[56,128]{1,0:T(8,128)}, u32[]{:S(2)}) copy-start(f32[56,128]{1,0:T(8,128)} %cut.1.after) | copy-start | bytes 86020
  7.3 22.9 %collective-permute-start.3 = (f32[592,128]{1,0:T(8,128)S(1)}, f32[592,128]{1,0:T(8,128)S(1)}, u32[]{:S(2)}, u32[]{:S(2)}) collective-permute-start(f32[592,128]{1,0:T(8,128)S(1)} %get-tuple-element.42), channel_id=1, source_target_pairs={{0,16},{16,0},{32,48},{48,32},{64,80},{80,64},{96,112},{112,96},{1... | collective-permute-start | bytes 909320 | tf_op jit(solution)/shard_map/ppermute | solution.py:657
  10.5 19.7 %collective-permute-start.4 = (f32[592,128]{1,0:T(8,128)S(1)}, f32[592,128]{1,0:T(8,128)S(1)}, u32[]{:S(2)}, u32[]{:S(2)}) collective-permute-start(f32[592,128]{1,0:T(8,128)S(1)} %get-tuple-element.43), channel_id=1, source_target_pairs={{0,112},{16,32},{32,16},{48,64},{64,48},{80,96},{96,80},{112,0},{1... | collective-permute-start | bytes 909320 | tf_op jit(solution)/shard_map/ppermute | solution.py:657
  14.5 3.1 %collective-permute-start.1 = (f32[336,128]{1,0:T(8,128)S(1)}, f32[336,128]{1,0:T(8,128)S(1)}, u32[]{:S(2)}, u32[]{:S(2)}) collective-permute-start(f32[336,128]{1,0:T(8,128)S(1)} %get-tuple-element.38), channel_id=1, source_target_pairs={{0,2},{2,0},{4,6},{6,4},{8,10},{10,8},{12,14},{14,12},{1,3},{3,1},... | collective-permute-start | bytes 516104 | tf_op jit(solution)/shard_map/ppermute | solution.py:657
  14.5 6.2 %collective-permute-start.2 = (f32[336,128]{1,0:T(8,128)S(1)}, f32[336,128]{1,0:T(8,128)S(1)}, u32[]{:S(2)}, u32[]{:S(2)}) collective-permute-start(f32[336,128]{1,0:T(8,128)S(1)} %get-tuple-element.39), channel_id=1, source_target_pairs={{0,14},{2,4},{4,2},{6,8},{8,6},{10,12},{12,10},{14,0},{1,15},{3,5}... | collective-permute-start | bytes 516104 | tf_op jit(solution)/shard_map/ppermute | solution.py:657
  21.1 6.6 %collective-permute-start.5 = (f32[160,128]{1,0:T(8,128)S(1)}, f32[160,128]{1,0:T(8,128)S(1)}, u32[]{:S(2)}, u32[]{:S(2)}) collective-permute-start(f32[160,128]{1,0:T(8,128)S(1)} %get-tuple-element.44), channel_id=1, source_target_pairs={{0,16},{16,0},{32,48},{48,32},{64,80},{80,64},{96,112},{112,96},{1... | collective-permute-start | bytes 245768 | tf_op jit(solution)/shard_map/ppermute | solution.py:657
  22.1 8.2 %collective-permute-start.6 = (f32[160,128]{1,0:T(8,128)S(1)}, f32[160,128]{1,0:T(8,128)S(1)}, u32[]{:S(2)}, u32[]{:S(2)}) collective-permute-start(f32[160,128]{1,0:T(8,128)S(1)} %get-tuple-element.45), channel_id=1, source_target_pairs={{0,112},{16,32},{32,16},{48,64},{64,48},{80,96},{96,80},{112,0},{1... | collective-permute-start | bytes 245768 | tf_op jit(solution)/shard_map/ppermute | solution.py:657
  36.5 19.7 %collective-permute-start.9 = (f32[432,128]{1,0:T(8,128)S(1)}, f32[432,128]{1,0:T(8,128)S(1)}, u32[]{:S(2)}, u32[]{:S(2)}) collective-permute-start(f32[432,128]{1,0:T(8,128)S(1)} %get-tuple-element.58), channel_id=1, source_target_pairs={{0,16},{16,0},{32,48},{48,32},{64,80},{80,64},{96,112},{112,96},{1... | collective-permute-start | bytes 663560 | tf_op jit(solution)/shard_map/ppermute | solution.py:657
  37.9 18.3 %collective-permute-start.10 = (f32[432,128]{1,0:T(8,128)S(1)}, f32[432,128]{1,0:T(8,128)S(1)}, u32[]{:S(2)}, u32[]{:S(2)}) collective-permute-start(f32[432,128]{1,0:T(8,128)S(1)} %get-tuple-element.59), channel_id=1, source_target_pairs={{0,112},{16,32},{32,16},{48,64},{64,48},{80,96},{96,80},{112,0},{1... | collective-permute-start | bytes 663560 | tf_op jit(solution)/shard_map/ppermute | solution.py:657
  40.0 3.1 %collective-permute-start.7 = (f32[248,128]{1,0:T(8,128)S(1)}, f32[248,128]{1,0:T(8,128)S(1)}, u32[]{:S(2)}, u32[]{:S(2)}) collective-permute-start(f32[248,128]{1,0:T(8,128)S(1)} %get-tuple-element.56), channel_id=1, source_target_pairs={{0,2},{2,0},{4,6},{6,4},{8,10},{10,8},{12,14},{14,12},{1,3},{3,1},... | collective-permute-start | bytes 380936 | tf_op jit(solution)/shard_map/ppermute | solution.py:657
  40.0 5.7 %collective-permute-start.8 = (f32[248,128]{1,0:T(8,128)S(1)}, f32[248,128]{1,0:T(8,128)S(1)}, u32[]{:S(2)}, u32[]{:S(2)}) collective-permute-start(f32[248,128]{1,0:T(8,128)S(1)} %get-tuple-element.57), channel_id=1, source_target_pairs={{0,14},{2,4},{4,2},{6,8},{8,6},{10,12},{12,10},{14,0},{1,15},{3,5}... | collective-permute-start | bytes 380936 | tf_op jit(solution)/shard_map/ppermute | solution.py:657
  46.0 5.8 %collective-permute-start.11 = (f32[128,128]{1,0:T(8,128)S(1)}, f32[128,128]{1,0:T(8,128)S(1)}, u32[]{:S(2)}, u32[]{:S(2)}) collective-permute-start(f32[128,128]{1,0:T(8,128)S(1)} %get-tuple-element.60), channel_id=1, source_target_pairs={{0,16},{16,0},{32,48},{48,32},{64,80},{80,64},{96,112},{112,96},{1... | collective-permute-start | bytes 196616 | tf_op jit(solution)/shard_map/ppermute | solution.py:657
  48.3 7.9 %collective-permute-start.12 = (f32[128,128]{1,0:T(8,128)S(1)}, f32[128,128]{1,0:T(8,128)S(1)}, u32[]{:S(2)}, u32[]{:S(2)}) collective-permute-start(f32[128,128]{1,0:T(8,128)S(1)} %get-tuple-element.61), channel_id=1, source_target_pairs={{0,112},{16,32},{32,16},{48,64},{64,48},{80,96},{96,80},{112,0},{1... | collective-permute-start | bytes 196616 | tf_op jit(solution)/shard_map/ppermute | solution.py:657

commit v3 on v2

--- a/solution.py
+++ b/solution.py
@@ -9,14 +9,17 @@
 DIRS = [(a, b, d) for a in (-1, 0, 1) for b in (-1, 0, 1) for d in (-1, 0, 1)]
 WEIGHTS = [(8.0 / 27.0, 2.0 / 27.0, 1.0 / 54.0, 1.0 / 216.0)[abs(a) + abs(b) + abs(d)] for a, b, d in DIRS]
 OMEGA = 1.25
-NT = 17
-ROWS = NT * 8
-MINI = pl.ds(128, 8)
+ROWS = 144
+MINI = pl.ds(0, 8)
 F32 = jnp.float32
 
 
+def octet(n):
+    return pl.ds(n * 8, 8) if isinstance(n, int) else pl.ds(pl.multiple_of(n * 8, 8), 8)
+
+
 def tile(n):
-    return pl.ds(n * 8, 8) if isinstance(n, int) else pl.ds(pl.multiple_of(n * 8, 8), 8)
+    return octet(n + 1)
 
 
 def lanes():
@@ -42,6 +45,25 @@
 def sides(axis):
     parity = lax.rem(lax.axis_index(axis), 2)
     return (1 - 2 * parity, 2 * parity - 1)
+
+
+class Later:
+    def __init__(self, group):
+        self.group, self.held = group, []
+
+    def put(self, ref, at, value):
+        self.held.append((ref, at, value))
+        if len(self.held) >= self.group:
+            self.flush()
+
+    def flush(self):
+        for ref, at, value in self.held:
+            ref[at] = value
+        self.held = []
+
+
+ALL = slice(None)
+OWN_GROUP, ROW_GROUP, STRIP_GROUP, PACK_GROUP = 18, 12, 12, 16
 
 
 def moments(f):
@@ -153,6 +175,13 @@
     return t0, t1
 
 
+def fan_out(line, sub, gz):
+    v = roll_l(jnp.broadcast_to(line, (8, 128)), 127 - 2 * gz)
+    for bit in (1, 2, 4):
+        v = jnp.where((sub & bit) != 0, roll_l(v, 128 - 4 * bit), v)
+    return v
+
+
 def direction(a, b, d):
     return 9 * (a + 1) + 3 * (b + 1) + d + 1
 
@@ -162,100 +191,113 @@
     ext = out_rows is not None
 
     def body(x, carry):
+        later = Later(OWN_GROUP)
         for a in (-1, 0, 1):
             for b in (-1, 0, 1):
                 xs = x - orient * a
                 bp = orient * b
                 into = direction(a, b, 0) + orient * (2 * gz - 1)
                 ins = roll_l(own[into, MINI, :], 127 - 2 * gz - 4 * xs)
+                if bp:
+                    ins = roll_s(ins, bp % 8)
                 for d in (-1, 0, 1):
                     i = direction(a, b, d)
-                    pair = shift_z(own[i, tile(2 * xs), :], own[i, tile(2 * xs + 1), :], orient * d, ins, lane)
+                    t0, t1 = (own[i, pl.ds(16 * xs + 8 * half + 8 - bp, 8), :] for half in (0, 1))
+                    pair = shift_z(t0, t1, orient * d, ins, lane)
                     for half in (0, 1):
-                        v = pair[half]
-                        if bp:
-                            v = roll_s(v, bp % 8)
-                        out[i, tile(2 * x + half), :] = v
+                        later.put(out, (i, tile(2 * x + half), ALL), pair[half])
+        later.flush()
         return carry
 
     lax.fori_loop(low, high, body, 0)
 
+    jobs = []
     for a in (-1, 0, 1):
         for b in (-1, 0, 1):
             bp, ap = orient * b, orient * a
             into = direction(a, b, 0) + orient * (2 * gz - 1)
             for k_in, row_in, k_out, row_out in sources(bp, ext):
                 if k_in is None:
-                    line = own[into, pl.ds(128 + row_in, 1), :]
+                    line = own[into, pl.ds(row_in, 1), :]
                 else:
                     line = strip_rows[into, pl.ds(STRIP_ROW[k_in], 1), :]
-                ins = jnp.sum(jnp.where(lane == 4 * sub + 3 * gz, jnp.broadcast_to(line, (8, 128)), 0.0), axis=1, keepdims=True)
-                for d in (-1, 0, 1):
-                    i = direction(a, b, d)
-                    if k_in is None:
-                        t0, t1 = (own[i, pl.ds(8 * half + row_in, 8, stride=16), :] for half in (0, 1))
-                    else:
-                        t0, t1 = rows[i, k_in, 0:8, :], rows[i, k_in, 8:16, :]
-                    pair = shift_z(t0, t1, orient * d, ins, lane)
-                    for half in (0, 1):
-                        v = pair[half]
-                        if ap:
-                            v = roll_s(v, ap % 8)
-                        if k_out is None:
-                            out[i, pl.ds(8 * half + row_out, 8, stride=16), :] = v
-                        else:
-                            out_rows[i, k_out, 8 * half : 8 * half + 8, :] = v
+                jobs.append((a, b, ap, k_in, row_in, k_out, row_out, jnp.sum(jnp.where(lane == 4 * sub + 3 * gz, jnp.broadcast_to(line, (8, 128)), 0.0), axis=1, keepdims=True)))
+    later = Later(ROW_GROUP)
+    for a, b, ap, k_in, row_in, k_out, row_out, ins in jobs:
+        for d in (-1, 0, 1):
+            i = direction(a, b, d)
+            if k_in is None:
+                t0, t1 = (own[i, pl.ds(8 + 8 * half + row_in, 8, stride=16), :] for half in (0, 1))
+            else:
+                t0, t1 = rows[i, k_in, 0:8, :], rows[i, k_in, 8:16, :]
+            pair = shift_z(t0, t1, orient * d, ins, lane)
+            for half in (0, 1):
+                v = pair[half]
+                if ap:
+                    v = roll_s(v, ap % 8)
+                if k_out is None:
+                    later.put(out, (i, pl.ds(8 + 8 * half + row_out, 8, stride=16), ALL), v)
+                else:
+                    later.put(out_rows, (i, k_out, octet(half), ALL), v)
+    later.flush()
 
     wall = lane == 127 * gz
+    later = Later(ROW_GROUP)
     for a in (-1, 0, 1):
         for b in (-1, 0, 1):
             i = direction(a, b, 0) + orient * (1 - 2 * gz)
             for x in range(low, high):
                 here = tile(2 * x + gz)
-                out[i, here, :] = jnp.where(wall, own[26 - i, here, :], out[i, here, :])
+                later.put(out, (i, here, ALL), jnp.where(wall, own[26 - i, here, :], out[i, here, :]))
             if ext:
                 for k in (0, 2):
-                    here = tile(gz)
-                    out_rows[i, k, here, :] = jnp.where(wall, rows[26 - i, k, here, :], out_rows[i, k, here, :])
+                    here = octet(gz)
+                    later.put(out_rows, (i, k, here, ALL), jnp.where(wall, rows[26 - i, k, here, :], out_rows[i, k, here, :]))
+    later.flush()
 
     slot = lax.rem(lane, 4)
     edge = 1 - gz
+    later = Later(STRIP_GROUP)
+    rims = []
     for a in (-1, 0, 1):
         for b in (-1, 0, 1):
             bp, ap = orient * b, orient * a
             outof = direction(a, b, 0) + orient * (1 - 2 * gz)
             need = [k for k, _, _, _ in sources(bp, ext) if k is not None]
             rim = jnp.zeros((8, 128), F32)
-            for xe in range(8):
+            for xe in range(low - ap, high - ap):
                 src = own[outof, tile(2 * xe + edge), :]
                 rim = jnp.where(lane == 4 * xe + 3 * gz, roll_l(src, 4 * xe + 1 + 2 * gz), rim)
             rim_rows = jnp.zeros((8, 128), F32)
             for k in need:
-                src = pltpu.roll(roll_l(rows[outof, k, tile(edge), :], 1 + 2 * gz), 0, 1, stride=4, stride_axis=0)
+                src = pltpu.roll(roll_l(rows[outof, k, octet(edge), :], 1 + 2 * gz), 0, 1, stride=4, stride_axis=0)
                 line = jnp.sum(jnp.where(lane == 4 * sub + 3 * gz, src, 0.0), axis=0, keepdims=True)
                 rim_rows = jnp.where(sub == STRIP_ROW[k], line, rim_rows)
-            for d in (-1, 0, 1):
-                i = direction(a, b, d)
-                dp = orient * d
-
-                def shifted(v, edge_values):
-                    if dp == 1:
-                        v = jnp.where(slot == 0, edge_values, roll_l(v, 1))
-                    if dp == -1:
-                        v = jnp.where(slot == 3, edge_values, roll_l(v, 127))
-                    return roll_l(v, (4 * ap) % 128) if ap else v
-
-                vo = shifted(own[i, MINI, :], rim)
-                vy = shifted(strip_rows[i], rim_rows) if need else None
-                if bp == 0:
-                    out[i, MINI, :] = vo
-                    if ext:
-                        out_strip_rows[i] = vy
-                else:
-                    last = 7 if bp == 1 else 0
-                    out[i, MINI, :] = roll_s(jnp.where(sub == last, vy, vo), bp % 8)
-                    if ext:
-                        out_strip_rows[i] = roll_s(jnp.where(sub == last, vo, vy), bp % 8)
+            rims.append((a, b, bp, ap, need, rim, rim_rows))
+    for a, b, bp, ap, need, rim, rim_rows in rims:
+        for d in (-1, 0, 1):
+            i = direction(a, b, d)
+            dp = orient * d
+
+            def shifted(v, edge_values):
+                if dp == 1:
+                    v = jnp.where(slot == 0, edge_values, roll_l(v, 1))
+                if dp == -1:
+                    v = jnp.where(slot == 3, edge_values, roll_l(v, 127))
+                return roll_l(v, (4 * ap) % 128) if ap else v
+
+            vo = shifted(own[i, MINI, :], rim)
+            vy = shifted(strip_rows[i], rim_rows) if need else None
+            if bp == 0:
+                later.put(out, (i, MINI, ALL), vo)
+                if ext:
+                    later.put(out_strip_rows, i, vy)
+            else:
+                last = 7 if bp == 1 else 0
+                later.put(out, (i, MINI, ALL), roll_s(jnp.where(sub == last, vy, vo), bp % 8))
+                if ext:
+                    later.put(out_strip_rows, i, roll_s(jnp.where(sub == last, vo, vy), bp % 8))
+    later.flush()
 
 
 def entries(e, orient, stride, extra):
@@ -282,6 +324,7 @@
 
 
 def pack_faces(msg, e, orient, gz, arrays):
+    later = Later(PACK_GROUP)
     near = near_plane(e)
     walls = {-1: (lanes() == 0) & (gz == 0), 1: (lanes() == 127) & (gz == 1)}
     for n, (which, i, layer, stash, _, dp) in enumerate(entries(e, orient, 9, len(arrays) > 1)):
@@ -290,21 +333,25 @@
             v = ref[i, tile(2 * plane + half), :]
             if stash is not None and half == (dp + 1) // 2:
                 v = jnp.where(walls[dp], ref[stash, tile(2 * near + half), :], v)
-            msg[(2 * n + half) * 8 : (2 * n + half) * 8 + 8, :] = v
+            later.put(msg, (slice((2 * n + half) * 8, (2 * n + half) * 8 + 8), ALL), v)
+    later.flush()
 
 
 def unpack_faces(msg, s, orient, arrays):
+    later = Later(PACK_GROUP)
     near = near_plane(s) + s
     for n, (which, i, layer, stash, _, dp) in enumerate(entries(-s, orient, 9, len(arrays) > 1)):
         ref, plane = arrays[which], near if layer == 1 else near + s
         for half in (0, 1):
             v = msg[(2 * n + half) * 8 : (2 * n + half) * 8 + 8, :]
-            ref[i, tile(2 * plane + half), :] = v
+            later.put(ref, (i, tile(2 * plane + half), ALL), v)
             if stash is not None and half == (dp + 1) // 2:
-                ref[stash, tile(2 * near + half), :] = v
+                later.put(ref, (stash, tile(2 * near + half), ALL), v)
+    later.flush()
 
 
 def pack_sides(msg, e, orient, gz, arrays, strips):
+    later = Later(PACK_GROUP)
     near = 7 * ((e + 1) // 2)
     lane = lax.broadcasted_iota(jnp.int32, (4, 128), 1)
     walls = {-1: (lane == 0) & (gz == 0), 1: (lane == 127) & (gz == 1)}
@@ -312,22 +359,25 @@
     for n, (which, i, layer, stash, _, dp) in enumerate(items):
         ref, row = arrays[which], near if layer == 1 else near - e
         for half in (0, 1):
-            v = ref[i, pl.ds(32 + 8 * half + row, 4, stride=16), :]
+            v = ref[i, pl.ds(40 + 8 * half + row, 4, stride=16), :]
             if stash is not None and half == (dp + 1) // 2:
-                v = jnp.where(walls[dp], ref[stash, pl.ds(32 + 8 * half + near, 4, stride=16), :], v)
-            msg[8 * n + 4 * half : 8 * n + 4 * half + 4, :] = v
-        msg[8 * len(items) + n : 8 * len(items) + n + 1, :] = strips[which][i, pl.ds(row, 1), :]
+                v = jnp.where(walls[dp], ref[stash, pl.ds(40 + 8 * half + near, 4, stride=16), :], v)
+            later.put(msg, (slice(8 * n + 4 * half, 8 * n + 4 * half + 4), ALL), v)
+        later.put(msg, (slice(8 * len(items) + n, 8 * len(items) + n + 1), ALL), strips[which][i, pl.ds(row, 1), :])
+    later.flush()
 
 
 def unpack_sides(msg, s, orient, rows, strip_rows):
     k = s + 1
+    later = Later(PACK_GROUP)
     near = 7 * ((1 - s) // 2)
     items = entries(-s, orient, 3, len(rows) > 1)
     for n, (which, i, layer, _, _, _) in enumerate(items):
         for half in (0, 1):
-            rows[which][i, k + layer - 1, 8 * half + 2 : 8 * half + 6, :] = msg[8 * n + 4 * half : 8 * n + 4 * half + 4, :]
+            later.put(rows[which], (i, k + layer - 1, slice(8 * half + 2, 8 * half + 6), ALL), msg[8 * n + 4 * half : 8 * n + 4 * half + 4, :])
         row = near if layer == 1 else near + s
-        strip_rows[which][i, pl.ds(row, 1), :] = msg[8 * len(items) + n : 8 * len(items) + n + 1, :]
+        later.put(strip_rows[which], (i, pl.ds(row, 1), ALL), msg[8 * len(items) + n : 8 * len(items) + n + 1, :])
+    later.flush()
 
 
 def edge_rows(e, orient, extra):
@@ -335,6 +385,7 @@
 
 
 def pack_edges(msg, e, orient, gz, rows, strips, strip_rows):
+    later = Later(PACK_GROUP)
     near = near_plane(e)
     lane = lanes()
     lane2 = lax.broadcasted_iota(jnp.int32, (2, 128), 1)
@@ -350,7 +401,7 @@
             v = rows[which][i, k, pl.ds(plane, 2, stride=8), :]
             if stash is not None:
                 v = jnp.where(walls[dp], rows[which][stash, k, pl.ds(near, 2, stride=8), :], v)
-            msg[at : at + 2, :] = v
+            later.put(msg, (slice(at, at + 2), ALL), v)
             at += 2
         s = 4 * (n % 32)
         for kind, v in enumerate((strips[which][i], strip_rows[which][i])):
@@ -358,8 +409,9 @@
             packed[kind][n // 32] = jnp.where((lane >= s) & (lane < s + 4), moved, packed[kind][n // 32])
     at = -(-at // 8) * 8
     for v in packed[0] + packed[1]:
-        msg[at : at + 8, :] = v
+        later.put(msg, (slice(at, at + 8), ALL), v)
         at += 8
+    later.flush()
 
 
 def unpack_edges(msg, s, orient, rows, owns, strip_rows):
@@ -488,9 +540,11 @@
 
 def gather_in(pairs, strips):
     def body(n, carry):
+        later = Later(PACK_GROUP)
         for src, dst in pairs:
             for i in range(src.shape[0]):
-                dst[i, tile(n), :] = src[i, tile(n), :]
+                later.put(dst, (i, tile(n), ALL), src[i, tile(n), :])
+        later.flush()
         return carry
 
     lax.fori_loop(4, 12, body, 0)
@@ -528,7 +582,7 @@
             store(i, out[i])
 
     def again(k, carry):
-        here = tile(jnp.where(k == 12, 16, k + 2))
+        here = tile(jnp.where(k == 12, -1, k + 2))
 
         def put(i, v):
             c[i, here, :] = v
@@ -543,7 +597,7 @@
 
     def again_rows(k, carry):
         for half in (0, 1):
-            here = tile(half)
+            here = octet(half)
 
             def put(i, v):
                 cr[i, 2 * k, here, :] = v
@@ -576,7 +630,7 @@
         out, blame = back(here)
         for i in range(27):
             a2[i, here, :] = out[i]
-        q2[tile(k), :] = blame
+        q2[octet(k), :] = blame
         return carry
 
     lax.fori_loop(0, 8, back_own, 0)
@@ -600,7 +654,7 @@
     stream(t, tr, tmr, p, pr, pmr, -1, gz, 1, 7)
 
     def again(k, carry):
-        here = tile(jnp.where(k == 12, 16, k + 2))
+        here = tile(jnp.where(k == 12, -1, k + 2))
         u = [u_own[n, here, :] for n in (1, 2, 3)]
         out, blame = pull_back([p[i, here, :] for i in range(27)], s_own[0, here, :], u, [f1[i, here, :] for i in range(27)], u_own[0, here, :])
         for i in range(27):
@@ -612,7 +666,7 @@
 
     def again_rows(k, carry):
         for half in (0, 1):
-            here = tile(half)
+            here = octet(half)
             u = [u_rows[n, 2 * k, here, :] for n in (1, 2, 3)]
             out, _ = pull_back([pr[i, 2 * k, here, :] for i in range(27)], s_rows[0, 2 * k, here, :], u)
             for i in range(27):
@@ -634,7 +688,7 @@
             out, blame = pull_back([p[i, here, :] for i in range(27)], s_own[0, here, :], u, f, rho)
             for i in range(27):
                 adjoint[i, x, :, z] = out[i]
-            grad[x, :, z] = (1.0 - mask[x, :, z].astype(F32)) * (q1[here, :] + q2[tile(2 * x + half), :] + blame)
+            grad[x, :, z] = (1.0 - mask[x, :, z].astype(F32)) * (q1[here, :] + q2[octet(2 * x + half), :] + blame)
         return carry
 
     lax.fori_loop(0, 4, back, 0)
@@ -703,7 +757,7 @@
     a2, a2m, f1, u_own, u_rows, u_strip, s_own, s_rows, s_strip, q2, *out = call(
         middle_kernel,
         [BIG, STRIP, BIG, (4, ROWS, 128), (4, 4, 16, 128), (4, 8, 128), ONE, HALO1, STRIP1, (64, 128)]
-        + [side_shape(27)] * 2
+        + [(440, 128)] * 2
         + [face_shape(27)] * 2,
         scratch=[BIG, BIG, HALO, HALO, STRIP, STRIP, HALO, STRIP, BIG, HALO, STRIP, BIG, BIG],
         name="middle",

time: 62.4 us -> 60.5 us (0.970)
  starting transfers between devices: 27.3 us -> 25.5 us
  Pallas kernels: 15.9 us -> 14.4 us
  local copies, waits for them, and re-layouts: 0.78 us -> 2.28 us
    ppermute x12, starting transfers between devices: 25.6 us -> 23.8 us  [swap(): return lax.ppermute(x, axis, pairs)]
    unnamed x10 -> x12, local copies, waits for them, and re-layouts: 0.78 us -> 2.28 us
    ppermute x1, waiting for transfers between devices: 1.19 us -> 0.01 us  [body(): cut = lax.ppermute(cut, 'gz', [(0, 1), (1, 0)])]
    ppermute x12, waiting for transfers between devices: 16.3 us -> 17.3 us  [swap(): return lax.ppermute(x, axis, pairs)]
    pallas_call x1, Pallas kernels: 6.26 us -> 5.33 us  [body(): call(middle_kernel, [BIG, STRIP, BIG, (4, ROWS, 128), (4, 4, 16, 128), (4...]
  transfers between devices with their start and end apart: 13 -> 13, of which waited for: 7 -> 8; matrix products, arithmetic and copies ran while one was open for 0% -> 0% of each run, Pallas kernels for 2% -> 2%
where the time goes in v3:
time: 60.5 us; the launch traced here: 60.1 us
  starting transfers between devices  25.5 us (42%)
  waiting for transfers between devices  17.3 us (29%)
  Pallas kernels  14.4 us (24%)
  local copies, waits for them, and re-layouts  2.28 us (4%)
  between operations  0.71 us (1%)
    ppermute x12, starting transfers between devices, swap(): return lax.ppermute(x, axis, pairs)  23.8 us
    ppermute x12, waiting for transfers between devices, swap(): return lax.ppermute(x, axis, pairs)  17.3 us
    pallas_call x1, Pallas kernels, body(): call(last_kernel, [populations.shape, blockage.shape], scratch=[BIG, HALO...  5.38 us
    pallas_call x1, Pallas kernels, body(): call(middle_kernel, [BIG, STRIP, BIG, (4, ROWS, 128), (4, 4, 16, 128), (4...  5.33 us
    unnamed x12, local copies, waits for them, and re-layouts  2.28 us
    pallas_call x1, Pallas kernels, body(): call(cut_kernel, [(56, 128)], scratch=halves + [pltpu.SemaphoreType.DMA((...  2.23 us
    ppermute x1, starting transfers between devices, body(): cut = lax.ppermute(cut, 'gz', [(0, 1), (1, 0)])  1.65 us
  transfers between devices with their start and end apart: 13, of which 8 were waited for; matrix products, arithmetic and copies ran while one was open for 0% of the time, Pallas kernels for 2%

profile of v3, /device:TPU:0, one launch (start us, length us, event | category | flops | bytes accessed | tf_op | source)
XLA Modules:
  0.0 60.1 jit_solution(694814595669120913)
XLA Ops:
  0.6 0.0 copy-start
  0.6 0.0 copy-start.1
  0.6 2.2 %cut.1.after = f32[56,128]{1,0:T(8,128)} custom-call(f32[27,4,8,256]{3,2,1,0:T(8,128)} %pops.3, f32[4,8,256]{2,1,0:T(8,128)} %block.1, s32[4,8,256]{2,1,0:T(8,128)} %mask.3, f32[27,4,8,256]{3,2,1,0:T(8,128)} %cot.1), custom_call_target="tpu_custom_call" | custom-call | tf_op jit(solution)/shard_map/cut/pallas_call | solution.py:742
  2.9 1.7 %collective-permute-start = (f32[56,128]{1,0:T(8,128)}, f32[56,128]{1,0:T(8,128)S(1)}, u32[]{:S(2)}, u32[]{:S(2)}) collective-permute-start(f32[56,128]{1,0:T(8,128)} %cut.1.after), channel_id=1, source_target_pairs={{0,1},{1,0},{2,3},{3,2},{4,5},{5,4},{6,7},{7,6},{8,9},{9,8},{10,11... | collective-permute-start | bytes 86024 | tf_op jit(solution)/shard_map/ppermute | solution.py:748
  4.5 0.0 copy-done
  4.5 0.0 copy-done.1
  4.5 0.0 copy-start.2
  4.6 0.8 %copy-done.2 = s32[4,8,256]{2,1,0:T(8,128)S(1)} copy-done((s32[4,8,256]{2,1,0:T(8,128)S(1)}, s32[4,8,256]{2,1,0:T(8,128)}, u32[]{:S(2)}) %copy-start.2) | copy-done | bytes 32792
  5.3 0.0 copy-start.4
  5.3 0.8 %copy-done.4 = f32[4,8,256]{2,1,0:T(8,128)S(1)} copy-done((f32[4,8,256]{2,1,0:T(8,128)S(1)}, f32[4,8,256]{2,1,0:T(8,128)}, u32[]{:S(2)}) %copy-start.4) | copy-done | bytes 32792
  6.1 0.0 copy-start.5
  6.1 0.7 %copy-done.5 = f32[56,128]{1,0:T(8,128)S(1)} copy-done((f32[56,128]{1,0:T(8,128)S(1)}, f32[56,128]{1,0:T(8,128)}, u32[]{:S(2)}) %copy-start.5) | copy-done | bytes 28696
  6.8 0.5 first.1
  7.4 0.0 collective-permute-done.cut
  7.4 0.2 strip.1
  7.6 2.9 %collective-permute-start.3 = (f32[592,128]{1,0:T(8,128)S(1)}, f32[592,128]{1,0:T(8,128)S(1)}, u32[]{:S(2)}, u32[]{:S(2)}) collective-permute-start(f32[592,128]{1,0:T(8,128)S(1)} %get-tuple-element.42), channel_id=1, source_target_pairs={{0,16},{16,0},{32,48},{48,32},{64,80},{80,64},{96,112},{112,96},{1... | collective-permute-start | bytes 909320 | tf_op jit(solution)/shard_map/ppermute | solution.py:711
  10.5 4.2 %collective-permute-start.4 = (f32[592,128]{1,0:T(8,128)S(1)}, f32[592,128]{1,0:T(8,128)S(1)}, u32[]{:S(2)}, u32[]{:S(2)}) collective-permute-start(f32[592,128]{1,0:T(8,128)S(1)} %get-tuple-element.43), channel_id=1, source_target_pairs={{0,112},{16,32},{32,16},{48,64},{64,48},{80,96},{96,80},{112,0},{1... | collective-permute-start | bytes 909320 | tf_op jit(solution)/shard_map/ppermute | solution.py:711
  14.7 0.0 collective-permute-start.1
  14.7 3.1 %collective-permute-start.2 = (f32[336,128]{1,0:T(8,128)S(1)}, f32[336,128]{1,0:T(8,128)S(1)}, u32[]{:S(2)}, u32[]{:S(2)}) collective-permute-start(f32[336,128]{1,0:T(8,128)S(1)} %get-tuple-element.39), channel_id=1, source_target_pairs={{0,14},{2,4},{4,2},{6,8},{8,6},{10,12},{12,10},{14,0},{1,15},{3,5}... | collective-permute-start | bytes 516104 | tf_op jit(solution)/shard_map/ppermute | solution.py:711
  17.8 0.0 collective-permute-done.1.got0.y0
  17.8 3.1 %collective-permute-done.2.got1.y1 = f32[336,128]{1,0:T(8,128)S(1)} collective-permute-done((f32[336,128]{1,0:T(8,128)S(1)}, f32[336,128]{1,0:T(8,128)S(1)}, u32[]{:S(2)}, u32[]{:S(2)}) %collective-permute-start.2) | collective-permute-done | bytes 172064 | tf_op jit(solution)/shard_map/ppermute | solution.py:711
  20.9 0.4 edge.1
  21.3 0.7 %collective-permute-start.5 = (f32[160,128]{1,0:T(8,128)S(1)}, f32[160,128]{1,0:T(8,128)S(1)}, u32[]{:S(2)}, u32[]{:S(2)}) collective-permute-start(f32[160,128]{1,0:T(8,128)S(1)} %get-tuple-element.44), channel_id=1, source_target_pairs={{0,16},{16,0},{32,48},{48,32},{64,80},{80,64},{96,112},{112,96},{1... | collective-permute-start | bytes 245768 | tf_op jit(solution)/shard_map/ppermute | solution.py:711
  22.0 0.0 copy-start.3
  22.0 2.7 %collective-permute-start.6 = (f32[160,128]{1,0:T(8,128)S(1)}, f32[160,128]{1,0:T(8,128)S(1)}, u32[]{:S(2)}, u32[]{:S(2)}) collective-permute-start(f32[160,128]{1,0:T(8,128)S(1)} %get-tuple-element.45), channel_id=1, source_target_pairs={{0,112},{16,32},{32,16},{48,64},{64,48},{80,96},{96,80},{112,0},{1... | collective-permute-start | bytes 245768 | tf_op jit(solution)/shard_map/ppermute | solution.py:711
  24.8 3.3 %collective-permute-done.5.e0 = f32[160,128]{1,0:T(8,128)S(1)} collective-permute-done((f32[160,128]{1,0:T(8,128)S(1)}, f32[160,128]{1,0:T(8,128)S(1)}, u32[]{:S(2)}, u32[]{:S(2)}) %collective-permute-start.5) | collective-permute-done | bytes 81952 | tf_op jit(solution)/shard_map/ppermute | solution.py:711
  28.0 3.3 %collective-permute-done.6.e1 = f32[160,128]{1,0:T(8,128)S(1)} collective-permute-done((f32[160,128]{1,0:T(8,128)S(1)}, f32[160,128]{1,0:T(8,128)S(1)}, u32[]{:S(2)}, u32[]{:S(2)}) %collective-permute-start.6) | collective-permute-done | bytes 81952 | tf_op jit(solution)/shard_map/ppermute | solution.py:711
  31.3 0.0 collective-permute-done.3.x0
  31.3 0.0 collective-permute-done.4.x1
  31.3 5.3 %middle.1 = (f32[27,144,128]{2,1,0:T(8,128)S(1)}, f32[27,8,128]{2,1,0:T(8,128)S(1)}, f32[27,144,128]{2,1,0:T(8,128)S(1)}, f32[4,144,128]{2,1,0:T(8,128)S(1)}, f3...) custom-call(f32[27,144,128]{2,1,0:T(8,128)S(1)} %get-tuple-element.3, ...), custom_call_target="tpu_custom_call" | custom-call | tf_op jit(solution)/shard_map/middle/pallas_call | solution.py:757
  36.7 0.1 collective-permute-start.7
  36.8 3.1 %collective-permute-start.8 = (f32[440,128]{1,0:T(8,128)S(1)}, f32[440,128]{1,0:T(8,128)S(1)}, u32[]{:S(2)}, u32[]{:S(2)}) collective-permute-start(f32[440,128]{1,0:T(8,128)S(1)} %get-tuple-element.57), channel_id=1, source_target_pairs={{0,14},{2,4},{4,2},{6,8},{8,6},{10,12},{12,10},{14,0},{1,15},{3,5}... | collective-permute-start | bytes 675848 | tf_op jit(solution)/shard_map/ppermute | solution.py:711
  39.9 0.6 %collective-permute-start.9 = (f32[432,128]{1,0:T(8,128)S(1)}, f32[432,128]{1,0:T(8,128)S(1)}, u32[]{:S(2)}, u32[]{:S(2)}) collective-permute-start(f32[432,128]{1,0:T(8,128)S(1)} %get-tuple-element.58), channel_id=1, source_target_pairs={{0,16},{16,0},{32,48},{48,32},{64,80},{80,64},{96,112},{112,96},{1... | collective-permute-start | bytes 663560 | tf_op jit(solution)/shard_map/ppermute | solution.py:711
  40.5 2.8 %collective-permute-start.10 = (f32[432,128]{1,0:T(8,128)S(1)}, f32[432,128]{1,0:T(8,128)S(1)}, u32[]{:S(2)}, u32[]{:S(2)}) collective-permute-start(f32[432,128]{1,0:T(8,128)S(1)} %get-tuple-element.59), channel_id=1, source_target_pairs={{0,112},{16,32},{32,16},{48,64},{64,48},{80,96},{96,80},{112,0},{1... | collective-permute-start | bytes 663560 | tf_op jit(solution)/shard_map/ppermute | solution.py:711
  43.2 0.0 collective-permute-done.7.got0.y0
  43.2 0.3 collective-permute-done.8.got1.y1
  43.5 0.3 edge2.1
  43.8 1.9 %collective-permute-start.11 = (f32[128,128]{1,0:T(8,128)S(1)}, f32[128,128]{1,0:T(8,128)S(1)}, u32[]{:S(2)}, u32[]{:S(2)}) collective-permute-start(f32[128,128]{1,0:T(8,128)S(1)} %get-tuple-element.60), channel_id=1, source_target_pairs={{0,16},{16,0},{32,48},{48,32},{64,80},{80,64},{96,112},{112,96},{1... | collective-permute-start | bytes 196616 | tf_op jit(solution)/shard_map/ppermute | solution.py:711
  45.7 1.7 %collective-permute-start.12 = (f32[128,128]{1,0:T(8,128)S(1)}, f32[128,128]{1,0:T(8,128)S(1)}, u32[]{:S(2)}, u32[]{:S(2)}) collective-permute-start(f32[128,128]{1,0:T(8,128)S(1)} %get-tuple-element.61), channel_id=1, source_target_pairs={{0,112},{16,32},{32,16},{48,64},{64,48},{80,96},{96,80},{112,0},{1... | collective-permute-start | bytes 196616 | tf_op jit(solution)/shard_map/ppermute | solution.py:711
  47.4 2.3 %collective-permute-done.9.x0 = f32[432,128]{1,0:T(8,128)S(1)} collective-permute-done((f32[432,128]{1,0:T(8,128)S(1)}, f32[432,128]{1,0:T(8,128)S(1)}, u32[]{:S(2)}, u32[]{:S(2)}) %collective-permute-start.9) | collective-permute-done | bytes 221216 | tf_op jit(solution)/shard_map/ppermute | solution.py:711
  49.7 3.6 %collective-permute-done.10.x1 = f32[432,128]{1,0:T(8,128)S(1)} collective-permute-done((f32[432,128]{1,0:T(8,128)S(1)}, f32[432,128]{1,0:T(8,128)S(1)}, u32[]{:S(2)}, u32[]{:S(2)}) %collective-permute-start.10) | collective-permute-done | bytes 221216 | tf_op jit(solution)/shard_map/ppermute | solution.py:711
  53.4 0.9 %collective-permute-done.11.e0 = f32[128,128]{1,0:T(8,128)S(1)} collective-permute-done((f32[128,128]{1,0:T(8,128)S(1)}, f32[128,128]{1,0:T(8,128)S(1)}, u32[]{:S(2)}, u32[]{:S(2)}) %collective-permute-start.11) | collective-permute-done | bytes 65568 | tf_op jit(solution)/shard_map/ppermute | solution.py:711
  54.2 0.5 collective-permute-done.12.e1
  54.8 0.0 copy-done.3
  54.8 5.4 %last.1 = (f32[27,4,8,256]{3,2,1,0:T(8,128)}, f32[4,8,256]{2,1,0:T(8,128)}) custom-call(f32[27,144,128]{2,1,0:T(8,128)S(1)} %get-tuple-element.46.a2, f32[27,8,128]{2,1,0:T(8,128)S(1)} %get-tuple-element.47.tm.a2m, f32[27,4,8,256]{3,2,1,0:T(8,128)S(1)} %copy-done, s32[4,8,256]{2,1,0:T(8,128)S(1)} %copy-done.3, f32[27,144,128]{2,1,0:T(8,128)S(1)} %get-tuple-element.48.f1, ...), custom_call_target="tpu_custom_call" | custom-call | tf_op jit(solution)/shard_map/last/pallas_call | solution.py:770
Async XLA Ops:
  0.6 3.9 %copy-start = (f32[27,4,8,256]{3,2,1,0:T(8,128)S(1)}, f32[27,4,8,256]{3,2,1,0:T(8,128)}, u32[]{:S(2)}) copy-start(f32[27,4,8,256]{3,2,1,0:T(8,128)} %pops.3) | copy-start | bytes 2654212
  0.6 3.9 %copy-start.1 = (f32[27,4,8,256]{3,2,1,0:T(8,128)S(1)}, f32[27,4,8,256]{3,2,1,0:T(8,128)}, u32[]{:S(2)}) copy-start(f32[27,4,8,256]{3,2,1,0:T(8,128)} %cot.1) | copy-start | bytes 2654212
  2.9 4.5 %collective-permute-start = (f32[56,128]{1,0:T(8,128)}, f32[56,128]{1,0:T(8,128)S(1)}, u32[]{:S(2)}, u32[]{:S(2)}) collective-permute-start(f32[56,128]{1,0:T(8,128)} %cut.1.after), channel_id=1, source_target_pairs={{0,1},{1,0},{2,3},{3,2},{4,5},{5,4},{6,7},{7,6},{8,9},{9,8},{10,11... | collective-permute-start | bytes 86024 | tf_op jit(solution)/shard_map/ppermute | solution.py:748
  4.5 0.8 %copy-start.2 = (s32[4,8,256]{2,1,0:T(8,128)S(1)}, s32[4,8,256]{2,1,0:T(8,128)}, u32[]{:S(2)}) copy-start(s32[4,8,256]{2,1,0:T(8,128)} %mask.3) | copy-start | bytes 98308
  5.3 0.8 %copy-start.4 = (f32[4,8,256]{2,1,0:T(8,128)S(1)}, f32[4,8,256]{2,1,0:T(8,128)}, u32[]{:S(2)}) copy-start(f32[4,8,256]{2,1,0:T(8,128)} %block.1) | copy-start | bytes 98308
  6.1 0.7 %copy-start.5 = (f32[56,128]{1,0:T(8,128)S(1)}, f32[56,128]{1,0:T(8,128)}, u32[]{:S(2)}) copy-start(f32[56,128]{1,0:T(8,128)} %cut.1.after) | copy-start | bytes 86020
  7.6 23.7 %collective-permute-start.3 = (f32[592,128]{1,0:T(8,128)S(1)}, f32[592,128]{1,0:T(8,128)S(1)}, u32[]{:S(2)}, u32[]{:S(2)}) collective-permute-start(f32[592,128]{1,0:T(8,128)S(1)} %get-tuple-element.42), channel_id=1, source_target_pairs={{0,16},{16,0},{32,48},{48,32},{64,80},{80,64},{96,112},{112,96},{1... | collective-permute-start | bytes 909320 | tf_op jit(solution)/shard_map/ppermute | solution.py:711
  10.5 20.8 %collective-permute-start.4 = (f32[592,128]{1,0:T(8,128)S(1)}, f32[592,128]{1,0:T(8,128)S(1)}, u32[]{:S(2)}, u32[]{:S(2)}) collective-permute-start(f32[592,128]{1,0:T(8,128)S(1)} %get-tuple-element.43), channel_id=1, source_target_pairs={{0,112},{16,32},{32,16},{48,64},{64,48},{80,96},{96,80},{112,0},{1... | collective-permute-start | bytes 909320 | tf_op jit(solution)/shard_map/ppermute | solution.py:711
  14.7 3.1 %collective-permute-start.1 = (f32[336,128]{1,0:T(8,128)S(1)}, f32[336,128]{1,0:T(8,128)S(1)}, u32[]{:S(2)}, u32[]{:S(2)}) collective-permute-start(f32[336,128]{1,0:T(8,128)S(1)} %get-tuple-element.38), channel_id=1, source_target_pairs={{0,2},{2,0},{4,6},{6,4},{8,10},{10,8},{12,14},{14,12},{1,3},{3,1},... | collective-permute-start | bytes 516104 | tf_op jit(solution)/shard_map/ppermute | solution.py:711
  14.7 6.2 %collective-permute-start.2 = (f32[336,128]{1,0:T(8,128)S(1)}, f32[336,128]{1,0:T(8,128)S(1)}, u32[]{:S(2)}, u32[]{:S(2)}) collective-permute-start(f32[336,128]{1,0:T(8,128)S(1)} %get-tuple-element.39), channel_id=1, source_target_pairs={{0,14},{2,4},{4,2},{6,8},{8,6},{10,12},{12,10},{14,0},{1,15},{3,5}... | collective-permute-start | bytes 516104 | tf_op jit(solution)/shard_map/ppermute | solution.py:711
  21.3 6.7 %collective-permute-start.5 = (f32[160,128]{1,0:T(8,128)S(1)}, f32[160,128]{1,0:T(8,128)S(1)}, u32[]{:S(2)}, u32[]{:S(2)}) collective-permute-start(f32[160,128]{1,0:T(8,128)S(1)} %get-tuple-element.44), channel_id=1, source_target_pairs={{0,16},{16,0},{32,48},{48,32},{64,80},{80,64},{96,112},{112,96},{1... | collective-permute-start | bytes 245768 | tf_op jit(solution)/shard_map/ppermute | solution.py:711
  22.0 32.7 %copy-start.3 = (s32[4,8,256]{2,1,0:T(8,128)S(1)}, s32[4,8,256]{2,1,0:T(8,128)}, u32[]{:S(2)}) copy-start(s32[4,8,256]{2,1,0:T(8,128)} %mask.3) | copy-start | bytes 98308
  22.0 9.3 %collective-permute-start.6 = (f32[160,128]{1,0:T(8,128)S(1)}, f32[160,128]{1,0:T(8,128)S(1)}, u32[]{:S(2)}, u32[]{:S(2)}) collective-permute-start(f32[160,128]{1,0:T(8,128)S(1)} %get-tuple-element.45), channel_id=1, source_target_pairs={{0,112},{16,32},{32,16},{48,64},{64,48},{80,96},{96,80},{112,0},{1... | collective-permute-start | bytes 245768 | tf_op jit(solution)/shard_map/ppermute | solution.py:711
  36.7 6.6 %collective-permute-start.7 = (f32[440,128]{1,0:T(8,128)S(1)}, f32[440,128]{1,0:T(8,128)S(1)}, u32[]{:S(2)}, u32[]{:S(2)}) collective-permute-start(f32[440,128]{1,0:T(8,128)S(1)} %get-tuple-element.56), channel_id=1, source_target_pairs={{0,2},{2,0},{4,6},{6,4},{8,10},{10,8},{12,14},{14,12},{1,3},{3,1},... | collective-permute-start | bytes 675848 | tf_op jit(solution)/shard_map/ppermute | solution.py:711
  36.8 6.8 %collective-permute-start.8 = (f32[440,128]{1,0:T(8,128)S(1)}, f32[440,128]{1,0:T(8,128)S(1)}, u32[]{:S(2)}, u32[]{:S(2)}) collective-permute-start(f32[440,128]{1,0:T(8,128)S(1)} %get-tuple-element.57), channel_id=1, source_target_pairs={{0,14},{2,4},{4,2},{6,8},{8,6},{10,12},{12,10},{14,0},{1,15},{3,5}... | collective-permute-start | bytes 675848 | tf_op jit(solution)/shard_map/ppermute | solution.py:711
  39.9 9.9 %collective-permute-start.9 = (f32[432,128]{1,0:T(8,128)S(1)}, f32[432,128]{1,0:T(8,128)S(1)}, u32[]{:S(2)}, u32[]{:S(2)}) collective-permute-start(f32[432,128]{1,0:T(8,128)S(1)} %get-tuple-element.58), channel_id=1, source_target_pairs={{0,16},{16,0},{32,48},{48,32},{64,80},{80,64},{96,112},{112,96},{1... | collective-permute-start | bytes 663560 | tf_op jit(solution)/shard_map/ppermute | solution.py:711
  40.5 12.9 %collective-permute-start.10 = (f32[432,128]{1,0:T(8,128)S(1)}, f32[432,128]{1,0:T(8,128)S(1)}, u32[]{:S(2)}, u32[]{:S(2)}) collective-permute-start(f32[432,128]{1,0:T(8,128)S(1)} %get-tuple-element.59), channel_id=1, source_target_pairs={{0,112},{16,32},{32,16},{48,64},{64,48},{80,96},{96,80},{112,0},{1... | collective-permute-start | bytes 663560 | tf_op jit(solution)/shard_map/ppermute | solution.py:711
  43.8 10.4 %collective-permute-start.11 = (f32[128,128]{1,0:T(8,128)S(1)}, f32[128,128]{1,0:T(8,128)S(1)}, u32[]{:S(2)}, u32[]{:S(2)}) collective-permute-start(f32[128,128]{1,0:T(8,128)S(1)} %get-tuple-element.60), channel_id=1, source_target_pairs={{0,16},{16,0},{32,48},{48,32},{64,80},{80,64},{96,112},{112,96},{1... | collective-permute-start | bytes 196616 | tf_op jit(solution)/shard_map/ppermute | solution.py:711
  45.7 9.0 %collective-permute-start.12 = (f32[128,128]{1,0:T(8,128)S(1)}, f32[128,128]{1,0:T(8,128)S(1)}, u32[]{:S(2)}, u32[]{:S(2)}) collective-permute-start(f32[128,128]{1,0:T(8,128)S(1)} %get-tuple-element.61), channel_id=1, source_target_pairs={{0,112},{16,32},{32,16},{48,64},{64,48},{80,96},{96,80},{112,0},{1... | collective-permute-start | bytes 196616 | tf_op jit(solution)/shard_map/ppermute | solution.py:711

commit v4 on v3

--- a/solution.py
+++ b/solution.py
@@ -186,11 +186,12 @@
     return 9 * (a + 1) + 3 * (b + 1) + d + 1
 
 
-def stream(own, rows, strip_rows, out, out_rows, out_strip_rows, orient, gz, low, high):
+def stream(own, rows, strip_rows, out, out_rows, out_strip_rows, orient, gz, low, high, inner=True, strip=True):
     lane, sub = lanes(), subs()
     ext = out_rows is not None
 
-    def body(x, carry):
+    def body(n, carry):
+        x = n if inner else jnp.where(n < 3, n, n + 2)
         later = Later(OWN_GROUP)
         for a in (-1, 0, 1):
             for b in (-1, 0, 1):
@@ -209,7 +210,7 @@
         later.flush()
         return carry
 
-    lax.fori_loop(low, high, body, 0)
+    lax.fori_loop(low, high if inner else high - 2, body, 0)
 
     jobs = []
     for a in (-1, 0, 1):
@@ -247,6 +248,8 @@
         for b in (-1, 0, 1):
             i = direction(a, b, 0) + orient * (1 - 2 * gz)
             for x in range(low, high):
+                if not inner and x in (3, 4):
+                    continue
                 here = tile(2 * x + gz)
                 later.put(out, (i, here, ALL), jnp.where(wall, own[26 - i, here, :], out[i, here, :]))
             if ext:
@@ -255,6 +258,8 @@
                     later.put(out_rows, (i, k, here, ALL), jnp.where(wall, rows[26 - i, k, here, :], out_rows[i, k, here, :]))
     later.flush()
 
+    if not strip:
+        return
     slot = lax.rem(lane, 4)
     edge = 1 - gz
     later = Later(STRIP_GROUP)
@@ -562,15 +567,75 @@
     reflect_rows(rows[0], orient)
 
 
+def insert(pairs):
+    def body(k, carry):
+        later = Later(PACK_GROUP)
+        for src, dst in pairs:
+            for i in range(src.shape[0]):
+                later.put(dst, (i, tile(k + 6), ALL), src[i, octet(k), :])
+        later.flush()
+        return carry
+
+    lax.fori_loop(0, 4, body, 0)
+
+
+def inner_kernel(tx, ax, sx, tm, am, sm, y0, y1, f_in, c_in, u_in, p_in, t, a, tr, ar, sr, tmr, amr, smr, f, p):
+    gz = lax.axis_index("gz")
+    gather_in(((tx, t), (ax, a)), (tm, am))
+    for msg, s in zip((y0, y1), sides("gy")):
+        unpack_sides(msg, s, 1, (tr, ar, sr), (tmr, amr, smr))
+    stream(t, tr, tmr, f, None, None, 1, gz, 3, 5, strip=False)
+    stream(a, ar, amr, p, None, None, -1, gz, 3, 5, strip=False)
+
+    def body(k, carry):
+        here, there = tile(k + 6), octet(k)
+        pops = [f[i, here, :] for i in range(27)]
+        rho, u = moments(pops)
+        for n, v in enumerate([rho] + u):
+            u_in[n, there, :] = v
+        out = collide(pops, sx[0, here, :], rho, u)
+        for i in range(27):
+            f_in[i, there, :] = pops[i]
+            c_in[i, there, :] = out[i]
+            p_in[i, there, :] = p[i, here, :]
+        return carry
+
+    lax.fori_loop(0, 4, body, 0)
+
+
+def inner_kernel_2(a2, a2m, f1, u_own, s_own, y0, y1, c_in, q_in, t, tr, tmr, p):
+    gz = lax.axis_index("gz")
+    gather_in(((a2, t),), (a2m,))
+    for msg, s in zip((y0, y1), sides("gy")):
+        unpack_sides(msg, s, -1, (tr,), (tmr,))
+    stream(t, tr, tmr, p, None, None, -1, gz, 3, 5, strip=False)
+
+    def body(k, carry):
+        here, there = tile(k + 6), octet(k)
+        u = [u_own[n, here, :] for n in (1, 2, 3)]
+        out, blame = pull_back([p[i, here, :] for i in range(27)], s_own[0, here, :], u, [f1[i, here, :] for i in range(27)], u_own[0, here, :])
+        for i in range(27):
+            c_in[i, there, :] = out[i]
+        q_in[0, there, :] = blame
+        return carry
+
+    lax.fori_loop(0, 4, body, 0)
+
+
+def outer_tile(k):
+    return tile(jnp.where(k == 8, -1, jnp.where(k < 4, k + 2, k + 6)))
+
+
 def middle_kernel(
-    tx, ax, sx, tm, am, sm, y0, y1, x0, x1, e0, e1,
+    tx, ax, sx, tm, am, sm, y0, y1, x0, x1, e0, e1, f_in, c_in, u_in, p_in,
     a2, a2m, f1, u_own, u_rows, u_strip, s_own, s_rows, s_strip, q2, ym0, ym1, xm0, xm1,
     t, a, tr, ar, tmr, amr, fr, fmr, c, cr, cmr, f2, p,
 ):
     gz = lax.axis_index("gz")
     gather_in(((tx, t), (ax, a), (sx, s_own)), (tm, am, sm))
     receive(1, (t, a, s_own), (tr, ar, s_rows), (tmr, amr, s_strip), (y0, y1), (x0, x1), (e0, e1))
-    stream(t, tr, tmr, f1, fr, fmr, 1, gz, 1, 7)
+    stream(t, tr, tmr, f1, fr, fmr, 1, gz, 1, 7, inner=False)
+    insert(((f_in, f1), (c_in, c), (u_in, u_own)))
 
     def collide_at(load, solid, store, store_u):
         f = [load(i) for i in range(27)]
@@ -582,7 +647,7 @@
             store(i, out[i])
 
     def again(k, carry):
-        here = tile(jnp.where(k == 12, -1, k + 2))
+        here = outer_tile(k)
 
         def put(i, v):
             c[i, here, :] = v
@@ -593,7 +658,7 @@
         collide_at(lambda i: f1[i, here, :], s_own[0, here, :], put, put_u)
         return carry
 
-    lax.fori_loop(0, 13, again, 0)
+    lax.fori_loop(0, 9, again, 0)
 
     def again_rows(k, carry):
         for half in (0, 1):
@@ -618,7 +683,8 @@
 
     collide_at(lambda i: fmr[i], s_strip[0], put_strip, put_strip_u)
     stream(c, cr, cmr, f2, None, None, 1, gz, 2, 6)
-    stream(a, ar, amr, p, None, None, -1, gz, 2, 6)
+    stream(a, ar, amr, p, None, None, -1, gz, 2, 6, inner=False)
+    insert(((p_in, p),))
 
     def back(here):
         f = [f2[i, here, :] for i in range(27)]
@@ -644,25 +710,26 @@
 
 
 def last_kernel(
-    a2, a2m, pops, mask, f1, u_own, u_rows, u_strip, s_own, s_rows, s_strip, q2, y0, y1, x0, x1, e0, e1,
+    a2, a2m, pops, mask, f1, u_own, u_rows, u_strip, s_own, s_rows, s_strip, q2, y0, y1, x0, x1, e0, e1, c_in, q_in,
     adjoint, grad,
     t, tr, tmr, p, pr, pmr, c, cr, cmr, q1,
 ):
     gz = lax.axis_index("gz")
     gather_in(((a2, t),), (a2m,))
     receive(-1, (t,), (tr,), (tmr,), (y0, y1), (x0, x1), (e0, e1))
-    stream(t, tr, tmr, p, pr, pmr, -1, gz, 1, 7)
+    stream(t, tr, tmr, p, pr, pmr, -1, gz, 1, 7, inner=False)
+    insert(((c_in, c), (q_in, q1)))
 
     def again(k, carry):
-        here = tile(jnp.where(k == 12, -1, k + 2))
+        here = outer_tile(k)
         u = [u_own[n, here, :] for n in (1, 2, 3)]
         out, blame = pull_back([p[i, here, :] for i in range(27)], s_own[0, here, :], u, [f1[i, here, :] for i in range(27)], u_own[0, here, :])
         for i in range(27):
             c[i, here, :] = out[i]
-        q1[here, :] = blame
-        return carry
-
-    lax.fori_loop(0, 13, again, 0)
+        q1[0, here, :] = blame
+        return carry
+
+    lax.fori_loop(0, 9, again, 0)
 
     def again_rows(k, carry):
         for half in (0, 1):
@@ -688,13 +755,13 @@
             out, blame = pull_back([p[i, here, :] for i in range(27)], s_own[0, here, :], u, f, rho)
             for i in range(27):
                 adjoint[i, x, :, z] = out[i]
-            grad[x, :, z] = (1.0 - mask[x, :, z].astype(F32)) * (q1[here, :] + q2[octet(2 * x + half), :] + blame)
+            grad[x, :, z] = (1.0 - mask[x, :, z].astype(F32)) * (q1[0, here, :] + q2[octet(2 * x + half), :] + blame)
         return carry
 
     lax.fori_loop(0, 4, back, 0)
 
 
-def call(kernel, outs, scratch=(), name=None, mib=8, in_specs=None):
+def call(kernel, outs, scratch=(), name=None, mib=8, in_specs=None, cost=None):
     return pl.pallas_call(
         kernel,
         out_shape=[jax.ShapeDtypeStruct(s, F32) for s in outs],
@@ -702,6 +769,7 @@
         **({} if in_specs is None else {"in_specs": in_specs}),
         compiler_params=pltpu.CompilerParams(vmem_limit_bytes=mib * 1024 * 1024),
         name=name,
+        cost_estimate=None if cost is None else pl.CostEstimate(flops=0, bytes_accessed=cost, transcendentals=0),
     )
 
 
@@ -713,6 +781,7 @@
 
 BIG = (27, ROWS, 128)
 ONE = (1, ROWS, 128)
+QUAD = (27, 32, 128)
 STRIP = (27, 8, 128)
 STRIP1 = (1, 8, 128)
 HALO = (27, 4, 16, 128)
@@ -754,6 +823,14 @@
         edge_kernel, [edge_shape(True)] * 2, scratch=[HALO, HALO, HALO1, STRIP, STRIP, STRIP1], name="edge", mib=12
     )(tm, am, sm, *by_y)
     edges = swaps(edges, "gx")
+    inner = call(
+        inner_kernel,
+        [QUAD, QUAD, (4, 32, 128), QUAD],
+        scratch=[BIG, BIG, HALO, HALO, HALO1, STRIP, STRIP, STRIP1, BIG, BIG],
+        name="inner",
+        mib=20,
+        cost=6_000_000,
+    )(tx, ax, sx, tm, am, sm, *by_y)
     a2, a2m, f1, u_own, u_rows, u_strip, s_own, s_rows, s_strip, q2, *out = call(
         middle_kernel,
         [BIG, STRIP, BIG, (4, ROWS, 128), (4, 4, 16, 128), (4, 8, 128), ONE, HALO1, STRIP1, (64, 128)]
@@ -762,18 +839,21 @@
         scratch=[BIG, BIG, HALO, HALO, STRIP, STRIP, HALO, STRIP, BIG, HALO, STRIP, BIG, BIG],
         name="middle",
         mib=24,
-    )(tx, ax, sx, tm, am, sm, *by_y, *faces, *edges)
+    )(tx, ax, sx, tm, am, sm, *by_y, *faces, *edges, *inner)
     by_y = swaps(out[:2], "gy")
     faces = swaps(out[2:], "gx")
     edges = call(edge_kernel_2, [edge_shape(False)] * 2, scratch=[HALO, STRIP], name="edge2", mib=8)(a2m, *by_y)
     edges = swaps(edges, "gx")
+    inner = call(
+        inner_kernel_2, [QUAD, (1, 32, 128)], scratch=[BIG, HALO, STRIP, BIG], name="inner2", mib=14, cost=6_000_000
+    )(a2, a2m, f1, u_own, s_own, *by_y)
     adjoint, grad = call(
         last_kernel,
         [populations.shape, blockage.shape],
-        scratch=[BIG, HALO, STRIP, BIG, HALO, STRIP, BIG, HALO, STRIP, (ROWS, 128)],
+        scratch=[BIG, HALO, STRIP, BIG, HALO, STRIP, BIG, HALO, STRIP, ONE],
         name="last",
         mib=20,
-    )(a2, a2m, populations, solid_mask, f1, u_own, u_rows, u_strip, s_own, s_rows, s_strip, q2, *by_y, *faces, *edges)
+    )(a2, a2m, populations, solid_mask, f1, u_own, u_rows, u_strip, s_own, s_rows, s_strip, q2, *by_y, *faces, *edges, *inner)
     return adjoint, grad
 
 

time: 60.5 us -> 59.5 us (0.983)
  waiting for transfers between devices: 17.3 us -> 15.3 us
  Pallas kernels: 14.4 us -> 15.4 us
    ppermute x12, waiting for transfers between devices: 17.3 us -> 15.3 us  [swap(): return lax.ppermute(x, axis, pairs)]
    pallas_call x0 -> x2, Pallas kernels: none -> 1.99 us  [the longest x1 1.21 us: body(): call(inner_kernel, [QUAD, QUAD, (4, 32, 128), QUAD], scratch=[BIG, BIG, H...]
  transfers between devices with their start and end apart: 13 -> 13, of which waited for: 8 -> 8; matrix products, arithmetic and copies ran while one was open for 0% -> 0% of each run, Pallas kernels for 2% -> 5%
where the time goes in v4:
time: 59.5 us; the launch traced here: 59.1 us
  starting transfers between devices  25.5 us (43%)
  Pallas kernels  15.4 us (26%)
  waiting for transfers between devices  15.3 us (26%)
  local copies, waits for them, and re-layouts  2.28 us (4%)
  between operations  0.72 us (1%)
    ppermute x12, starting transfers between devices, swap(): return lax.ppermute(x, axis, pairs)  23.8 us
    ppermute x12, waiting for transfers between devices, swap(): return lax.ppermute(x, axis, pairs)  15.3 us
    pallas_call x1, Pallas kernels, body(): call(last_kernel, [populations.shape, blockage.shape], scratch=[BIG, HALO...  4.91 us
    pallas_call x1, Pallas kernels, body(): call(middle_kernel, [BIG, STRIP, BIG, (4, ROWS, 128), (4, 4, 16, 128), (4...  4.79 us
    unnamed x12, local copies, waits for them, and re-layouts  2.28 us
    pallas_call x1, Pallas kernels, body(): call(cut_kernel, [(56, 128)], scratch=halves + [pltpu.SemaphoreType.DMA((...  2.23 us
    ppermute x1, starting transfers between devices, body(): cut = lax.ppermute(cut, 'gz', [(0, 1), (1, 0)])  1.65 us
    pallas_call x1, Pallas kernels, body(): call(inner_kernel, [QUAD, QUAD, (4, 32, 128), QUAD], scratch=[BIG, BIG, H...  1.21 us
  transfers between devices with their start and end apart: 13, of which 8 were waited for; matrix products, arithmetic and copies ran while one was open for 0% of the time, Pallas kernels for 5%

profile of v4, /device:TPU:0, one launch (start us, length us, event | category | flops | bytes accessed | tf_op | source)
XLA Modules:
  0.0 59.1 jit_solution(17449567905237838029)
XLA Ops:
  0.6 0.0 copy-start
  0.6 0.0 copy-start.1
  0.6 2.2 %cut.1.after = f32[56,128]{1,0:T(8,128)} custom-call(f32[27,4,8,256]{3,2,1,0:T(8,128)} %pops.3, f32[4,8,256]{2,1,0:T(8,128)} %block.1, s32[4,8,256]{2,1,0:T(8,128)} %mask.3, f32[27,4,8,256]{3,2,1,0:T(8,128)} %cot.1), custom_call_target="tpu_custom_call" | custom-call | tf_op jit(solution)/shard_map/cut/pallas_call | solution.py:811
  2.9 1.7 %collective-permute-start = (f32[56,128]{1,0:T(8,128)}, f32[56,128]{1,0:T(8,128)S(1)}, u32[]{:S(2)}, u32[]{:S(2)}) collective-permute-start(f32[56,128]{1,0:T(8,128)} %cut.1.after), channel_id=1, source_target_pairs={{0,1},{1,0},{2,3},{3,2},{4,5},{5,4},{6,7},{7,6},{8,9},{9,8},{10,11... | collective-permute-start | bytes 86024 | tf_op jit(solution)/shard_map/ppermute | solution.py:817
  4.5 0.0 copy-done
  4.5 0.0 copy-done.1
  4.5 0.0 copy-start.2
  4.6 0.8 %copy-done.2 = s32[4,8,256]{2,1,0:T(8,128)S(1)} copy-done((s32[4,8,256]{2,1,0:T(8,128)S(1)}, s32[4,8,256]{2,1,0:T(8,128)}, u32[]{:S(2)}) %copy-start.2) | copy-done | bytes 32792
  5.3 0.0 copy-start.4
  5.3 0.8 %copy-done.4 = f32[4,8,256]{2,1,0:T(8,128)S(1)} copy-done((f32[4,8,256]{2,1,0:T(8,128)S(1)}, f32[4,8,256]{2,1,0:T(8,128)}, u32[]{:S(2)}) %copy-start.4) | copy-done | bytes 32792
  6.1 0.0 copy-start.5
  6.1 0.7 %copy-done.5 = f32[56,128]{1,0:T(8,128)S(1)} copy-done((f32[56,128]{1,0:T(8,128)S(1)}, f32[56,128]{1,0:T(8,128)}, u32[]{:S(2)}) %copy-start.5) | copy-done | bytes 28696
  6.8 0.5 first.1
  7.3 0.0 collective-permute-done.cut
  7.4 0.2 strip.1
  7.6 2.9 %collective-permute-start.3 = (f32[592,128]{1,0:T(8,128)S(1)}, f32[592,128]{1,0:T(8,128)S(1)}, u32[]{:S(2)}, u32[]{:S(2)}) collective-permute-start(f32[592,128]{1,0:T(8,128)S(1)} %get-tuple-element.48), channel_id=1, source_target_pairs={{0,16},{16,0},{32,48},{48,32},{64,80},{80,64},{96,112},{112,96},{1... | collective-permute-start | bytes 909320 | tf_op jit(solution)/shard_map/ppermute | solution.py:779
  10.5 4.2 %collective-permute-start.4 = (f32[592,128]{1,0:T(8,128)S(1)}, f32[592,128]{1,0:T(8,128)S(1)}, u32[]{:S(2)}, u32[]{:S(2)}) collective-permute-start(f32[592,128]{1,0:T(8,128)S(1)} %get-tuple-element.49), channel_id=1, source_target_pairs={{0,112},{16,32},{32,16},{48,64},{64,48},{80,96},{96,80},{112,0},{1... | collective-permute-start | bytes 909320 | tf_op jit(solution)/shard_map/ppermute | solution.py:779
  14.7 0.0 collective-permute-start.1
  14.7 3.1 %collective-permute-start.2 = (f32[336,128]{1,0:T(8,128)S(1)}, f32[336,128]{1,0:T(8,128)S(1)}, u32[]{:S(2)}, u32[]{:S(2)}) collective-permute-start(f32[336,128]{1,0:T(8,128)S(1)} %get-tuple-element.45), channel_id=1, source_target_pairs={{0,14},{2,4},{4,2},{6,8},{8,6},{10,12},{12,10},{14,0},{1,15},{3,5}... | collective-permute-start | bytes 516104 | tf_op jit(solution)/shard_map/ppermute | solution.py:779
  17.8 0.0 collective-permute-done.1.got0.y0
  17.8 3.1 %collective-permute-done.2.got1.y1 = f32[336,128]{1,0:T(8,128)S(1)} collective-permute-done((f32[336,128]{1,0:T(8,128)S(1)}, f32[336,128]{1,0:T(8,128)S(1)}, u32[]{:S(2)}, u32[]{:S(2)}) %collective-permute-start.2) | collective-permute-done | bytes 172064 | tf_op jit(solution)/shard_map/ppermute | solution.py:779
  20.9 0.4 edge.1
  21.3 0.8 %collective-permute-start.5 = (f32[160,128]{1,0:T(8,128)S(1)}, f32[160,128]{1,0:T(8,128)S(1)}, u32[]{:S(2)}, u32[]{:S(2)}) collective-permute-start(f32[160,128]{1,0:T(8,128)S(1)} %get-tuple-element.50), channel_id=1, source_target_pairs={{0,16},{16,0},{32,48},{48,32},{64,80},{80,64},{96,112},{112,96},{1... | collective-permute-start | bytes 245768 | tf_op jit(solution)/shard_map/ppermute | solution.py:779
  22.0 2.7 %collective-permute-start.6 = (f32[160,128]{1,0:T(8,128)S(1)}, f32[160,128]{1,0:T(8,128)S(1)}, u32[]{:S(2)}, u32[]{:S(2)}) collective-permute-start(f32[160,128]{1,0:T(8,128)S(1)} %get-tuple-element.51), channel_id=1, source_target_pairs={{0,112},{16,32},{32,16},{48,64},{64,48},{80,96},{96,80},{112,0},{1... | collective-permute-start | bytes 245768 | tf_op jit(solution)/shard_map/ppermute | solution.py:779
  24.7 1.2 %inner.1 = (f32[27,32,128]{2,1,0:T(8,128)S(1)}, f32[27,32,128]{2,1,0:T(8,128)S(1)}, f32[4,32,128]{2,1,0:T(8,128)S(1)}, f32[27,32,128]{2,1,0:T(8,128)S(1)}) custom-call(f32[27,144,128]{2,1,0:T(8,128)S(1)} %get-tuple-element.38.tx, f32[27,144,128]{2,1,0:T(8,128)S(1)} %get-tuple-element.39.ax, f32[1,144,128]{2,1,0:T(8,128)S(1)} %get-tuple-element.40.sx, ...), custom_call_target="tpu_custom_call" | custom-call | bytes 6000000 | tf_op jit(solution)/shard_map/inner/pallas_call | solution.py:826
  26.0 2.0 %collective-permute-done.5.e0 = f32[160,128]{1,0:T(8,128)S(1)} collective-permute-done((f32[160,128]{1,0:T(8,128)S(1)}, f32[160,128]{1,0:T(8,128)S(1)}, u32[]{:S(2)}, u32[]{:S(2)}) %collective-permute-start.5) | collective-permute-done | bytes 81952 | tf_op jit(solution)/shard_map/ppermute | solution.py:779
  28.0 3.3 %collective-permute-done.6.e1 = f32[160,128]{1,0:T(8,128)S(1)} collective-permute-done((f32[160,128]{1,0:T(8,128)S(1)}, f32[160,128]{1,0:T(8,128)S(1)}, u32[]{:S(2)}, u32[]{:S(2)}) %collective-permute-start.6) | collective-permute-done | bytes 81952 | tf_op jit(solution)/shard_map/ppermute | solution.py:779
  31.3 0.0 collective-permute-done.3.x0
  31.3 0.0 collective-permute-done.4.x1
  31.3 4.8 %middle.1 = (f32[27,144,128]{2,1,0:T(8,128)S(1)}, f32[27,8,128]{2,1,0:T(8,128)S(1)}, f32[27,144,128]{2,1,0:T(8,128)S(1)}, f32[4,144,128]{2,1,0:T(8,128)S(1)}, f3...) custom-call(f32[27,144,128]{2,1,0:T(8,128)S(1)} %get-tuple-element.3, ...), custom_call_target="tpu_custom_call" | custom-call | tf_op jit(solution)/shard_map/middle/pallas_call | solution.py:834
  36.1 0.1 collective-permute-start.7
  36.2 3.1 %collective-permute-start.8 = (f32[440,128]{1,0:T(8,128)S(1)}, f32[440,128]{1,0:T(8,128)S(1)}, u32[]{:S(2)}, u32[]{:S(2)}) collective-permute-start(f32[440,128]{1,0:T(8,128)S(1)} %get-tuple-element.67), channel_id=1, source_target_pairs={{0,14},{2,4},{4,2},{6,8},{8,6},{10,12},{12,10},{14,0},{1,15},{3,5}... | collective-permute-start | bytes 675848 | tf_op jit(solution)/shard_map/ppermute | solution.py:779
  39.3 0.6 %collective-permute-start.9 = (f32[432,128]{1,0:T(8,128)S(1)}, f32[432,128]{1,0:T(8,128)S(1)}, u32[]{:S(2)}, u32[]{:S(2)}) collective-permute-start(f32[432,128]{1,0:T(8,128)S(1)} %get-tuple-element.68), channel_id=1, source_target_pairs={{0,16},{16,0},{32,48},{48,32},{64,80},{80,64},{96,112},{112,96},{1... | collective-permute-start | bytes 663560 | tf_op jit(solution)/shard_map/ppermute | solution.py:779
  39.9 2.8 %collective-permute-start.10 = (f32[432,128]{1,0:T(8,128)S(1)}, f32[432,128]{1,0:T(8,128)S(1)}, u32[]{:S(2)}, u32[]{:S(2)}) collective-permute-start(f32[432,128]{1,0:T(8,128)S(1)} %get-tuple-element.69), channel_id=1, source_target_pairs={{0,112},{16,32},{32,16},{48,64},{64,48},{80,96},{96,80},{112,0},{1... | collective-permute-start | bytes 663560 | tf_op jit(solution)/shard_map/ppermute | solution.py:779
  42.7 0.0 collective-permute-done.7.got0.y0
  42.7 0.3 collective-permute-done.8.got1.y1
  43.0 0.3 edge2.1
  43.3 1.9 %collective-permute-start.11 = (f32[128,128]{1,0:T(8,128)S(1)}, f32[128,128]{1,0:T(8,128)S(1)}, u32[]{:S(2)}, u32[]{:S(2)}) collective-permute-start(f32[128,128]{1,0:T(8,128)S(1)} %get-tuple-element.70), channel_id=1, source_target_pairs={{0,16},{16,0},{32,48},{48,32},{64,80},{80,64},{96,112},{112,96},{1... | collective-permute-start | bytes 196616 | tf_op jit(solution)/shard_map/ppermute | solution.py:779
  45.2 1.7 %collective-permute-start.12 = (f32[128,128]{1,0:T(8,128)S(1)}, f32[128,128]{1,0:T(8,128)S(1)}, u32[]{:S(2)}, u32[]{:S(2)}) collective-permute-start(f32[128,128]{1,0:T(8,128)S(1)} %get-tuple-element.71), channel_id=1, source_target_pairs={{0,112},{16,32},{32,16},{48,64},{64,48},{80,96},{96,80},{112,0},{1... | collective-permute-start | bytes 196616 | tf_op jit(solution)/shard_map/ppermute | solution.py:779
  46.8 0.0 copy-start.3
  46.9 0.8 %inner2.1 = (f32[27,32,128]{2,1,0:T(8,128)S(1)}, f32[1,32,128]{2,1,0:T(8,128)S(1)}) custom-call(f32[27,144,128]{2,1,0:T(8,128)S(1)} %get-tuple-element.56.a2, f32[27,8,128]{2,1,0:T(8,128)S(1)} %get-tuple-element.57.tm.a2m, f32[27,144,128]{2,1,0:T(8,128)S(1)} %get-tuple-element.58.f1, f32[4,144,128]{2,1,0:T(8,128)S(1)} %get-tuple-element.59.u_own, ...), custom_call_target="tpu_custom_call" | custom-call | bytes 6000000 | tf_op jit(solution)/shard_map/inner2/pallas_call | solution.py:847
  47.6 1.6 %collective-permute-done.9.x0 = f32[432,128]{1,0:T(8,128)S(1)} collective-permute-done((f32[432,128]{1,0:T(8,128)S(1)}, f32[432,128]{1,0:T(8,128)S(1)}, u32[]{:S(2)}, u32[]{:S(2)}) %collective-permute-start.9) | collective-permute-done | bytes 221216 | tf_op jit(solution)/shard_map/ppermute | solution.py:779
  49.2 3.6 %collective-permute-done.10.x1 = f32[432,128]{1,0:T(8,128)S(1)} collective-permute-done((f32[432,128]{1,0:T(8,128)S(1)}, f32[432,128]{1,0:T(8,128)S(1)}, u32[]{:S(2)}, u32[]{:S(2)}) %collective-permute-start.10) | collective-permute-done | bytes 221216 | tf_op jit(solution)/shard_map/ppermute | solution.py:779
  52.8 0.9 %collective-permute-done.11.e0 = f32[128,128]{1,0:T(8,128)S(1)} collective-permute-done((f32[128,128]{1,0:T(8,128)S(1)}, f32[128,128]{1,0:T(8,128)S(1)}, u32[]{:S(2)}, u32[]{:S(2)}) %collective-permute-start.11) | collective-permute-done | bytes 65568 | tf_op jit(solution)/shard_map/ppermute | solution.py:779
  53.7 0.5 collective-permute-done.12.e1
  54.2 0.0 copy-done.3
  54.2 4.9 %last.1 = (f32[27,4,8,256]{3,2,1,0:T(8,128)}, f32[4,8,256]{2,1,0:T(8,128)}) custom-call(f32[27,144,128]{2,1,0:T(8,128)S(1)} %get-tuple-element.56.a2, f32[27,8,128]{2,1,0:T(8,128)S(1)} %get-tuple-element.57.tm.a2m, f32[27,4,8,256]{3,2,1,0:T(8,128)S(1)} %copy-done, s32[4,8,256]{2,1,0:T(8,128)S(1)} %copy-done.3, f32[27,144,128]{2,1,0:T(8,128)S(1)} %get-tuple-element.58.f1, ...), custom_call_target="tpu_custom_call" | custom-call | tf_op jit(solution)/shard_map/last/pallas_call | solution.py:850
Async XLA Ops:
  0.6 3.9 %copy-start = (f32[27,4,8,256]{3,2,1,0:T(8,128)S(1)}, f32[27,4,8,256]{3,2,1,0:T(8,128)}, u32[]{:S(2)}) copy-start(f32[27,4,8,256]{3,2,1,0:T(8,128)} %pops.3) | copy-start | bytes 2654212
  0.6 3.9 %copy-start.1 = (f32[27,4,8,256]{3,2,1,0:T(8,128)S(1)}, f32[27,4,8,256]{3,2,1,0:T(8,128)}, u32[]{:S(2)}) copy-start(f32[27,4,8,256]{3,2,1,0:T(8,128)} %cot.1) | copy-start | bytes 2654212
  2.9 4.5 %collective-permute-start = (f32[56,128]{1,0:T(8,128)}, f32[56,128]{1,0:T(8,128)S(1)}, u32[]{:S(2)}, u32[]{:S(2)}) collective-permute-start(f32[56,128]{1,0:T(8,128)} %cut.1.after), channel_id=1, source_target_pairs={{0,1},{1,0},{2,3},{3,2},{4,5},{5,4},{6,7},{7,6},{8,9},{9,8},{10,11... | collective-permute-start | bytes 86024 | tf_op jit(solution)/shard_map/ppermute | solution.py:817
  4.5 0.8 %copy-start.2 = (s32[4,8,256]{2,1,0:T(8,128)S(1)}, s32[4,8,256]{2,1,0:T(8,128)}, u32[]{:S(2)}) copy-start(s32[4,8,256]{2,1,0:T(8,128)} %mask.3) | copy-start | bytes 98308
  5.3 0.8 %copy-start.4 = (f32[4,8,256]{2,1,0:T(8,128)S(1)}, f32[4,8,256]{2,1,0:T(8,128)}, u32[]{:S(2)}) copy-start(f32[4,8,256]{2,1,0:T(8,128)} %block.1) | copy-start | bytes 98308
  6.1 0.7 %copy-start.5 = (f32[56,128]{1,0:T(8,128)S(1)}, f32[56,128]{1,0:T(8,128)}, u32[]{:S(2)}) copy-start(f32[56,128]{1,0:T(8,128)} %cut.1.after) | copy-start | bytes 86020
  7.6 23.7 %collective-permute-start.3 = (f32[592,128]{1,0:T(8,128)S(1)}, f32[592,128]{1,0:T(8,128)S(1)}, u32[]{:S(2)}, u32[]{:S(2)}) collective-permute-start(f32[592,128]{1,0:T(8,128)S(1)} %get-tuple-element.48), channel_id=1, source_target_pairs={{0,16},{16,0},{32,48},{48,32},{64,80},{80,64},{96,112},{112,96},{1... | collective-permute-start | bytes 909320 | tf_op jit(solution)/shard_map/ppermute | solution.py:779
  10.5 20.8 %collective-permute-start.4 = (f32[592,128]{1,0:T(8,128)S(1)}, f32[592,128]{1,0:T(8,128)S(1)}, u32[]{:S(2)}, u32[]{:S(2)}) collective-permute-start(f32[592,128]{1,0:T(8,128)S(1)} %get-tuple-element.49), channel_id=1, source_target_pairs={{0,112},{16,32},{32,16},{48,64},{64,48},{80,96},{96,80},{112,0},{1... | collective-permute-start | bytes 909320 | tf_op jit(solution)/shard_map/ppermute | solution.py:779
  14.7 3.1 %collective-permute-start.1 = (f32[336,128]{1,0:T(8,128)S(1)}, f32[336,128]{1,0:T(8,128)S(1)}, u32[]{:S(2)}, u32[]{:S(2)}) collective-permute-start(f32[336,128]{1,0:T(8,128)S(1)} %get-tuple-element.44), channel_id=1, source_target_pairs={{0,2},{2,0},{4,6},{6,4},{8,10},{10,8},{12,14},{14,12},{1,3},{3,1},... | collective-permute-start | bytes 516104 | tf_op jit(solution)/shard_map/ppermute | solution.py:779
  14.7 6.2 %collective-permute-start.2 = (f32[336,128]{1,0:T(8,128)S(1)}, f32[336,128]{1,0:T(8,128)S(1)}, u32[]{:S(2)}, u32[]{:S(2)}) collective-permute-start(f32[336,128]{1,0:T(8,128)S(1)} %get-tuple-element.45), channel_id=1, source_target_pairs={{0,14},{2,4},{4,2},{6,8},{8,6},{10,12},{12,10},{14,0},{1,15},{3,5}... | collective-permute-start | bytes 516104 | tf_op jit(solution)/shard_map/ppermute | solution.py:779
  21.3 6.7 %collective-permute-start.5 = (f32[160,128]{1,0:T(8,128)S(1)}, f32[160,128]{1,0:T(8,128)S(1)}, u32[]{:S(2)}, u32[]{:S(2)}) collective-permute-start(f32[160,128]{1,0:T(8,128)S(1)} %get-tuple-element.50), channel_id=1, source_target_pairs={{0,16},{16,0},{32,48},{48,32},{64,80},{80,64},{96,112},{112,96},{1... | collective-permute-start | bytes 245768 | tf_op jit(solution)/shard_map/ppermute | solution.py:779
  22.0 9.3 %collective-permute-start.6 = (f32[160,128]{1,0:T(8,128)S(1)}, f32[160,128]{1,0:T(8,128)S(1)}, u32[]{:S(2)}, u32[]{:S(2)}) collective-permute-start(f32[160,128]{1,0:T(8,128)S(1)} %get-tuple-element.51), channel_id=1, source_target_pairs={{0,112},{16,32},{32,16},{48,64},{64,48},{80,96},{96,80},{112,0},{1... | collective-permute-start | bytes 245768 | tf_op jit(solution)/shard_map/ppermute | solution.py:779
  36.1 6.6 %collective-permute-start.7 = (f32[440,128]{1,0:T(8,128)S(1)}, f32[440,128]{1,0:T(8,128)S(1)}, u32[]{:S(2)}, u32[]{:S(2)}) collective-permute-start(f32[440,128]{1,0:T(8,128)S(1)} %get-tuple-element.66), channel_id=1, source_target_pairs={{0,2},{2,0},{4,6},{6,4},{8,10},{10,8},{12,14},{14,12},{1,3},{3,1},... | collective-permute-start | bytes 675848 | tf_op jit(solution)/shard_map/ppermute | solution.py:779
  36.2 6.8 %collective-permute-start.8 = (f32[440,128]{1,0:T(8,128)S(1)}, f32[440,128]{1,0:T(8,128)S(1)}, u32[]{:S(2)}, u32[]{:S(2)}) collective-permute-start(f32[440,128]{1,0:T(8,128)S(1)} %get-tuple-element.67), channel_id=1, source_target_pairs={{0,14},{2,4},{4,2},{6,8},{8,6},{10,12},{12,10},{14,0},{1,15},{3,5}... | collective-permute-start | bytes 675848 | tf_op jit(solution)/shard_map/ppermute | solution.py:779
  39.3 9.9 %collective-permute-start.9 = (f32[432,128]{1,0:T(8,128)S(1)}, f32[432,128]{1,0:T(8,128)S(1)}, u32[]{:S(2)}, u32[]{:S(2)}) collective-permute-start(f32[432,128]{1,0:T(8,128)S(1)} %get-tuple-element.68), channel_id=1, source_target_pairs={{0,16},{16,0},{32,48},{48,32},{64,80},{80,64},{96,112},{112,96},{1... | collective-permute-start | bytes 663560 | tf_op jit(solution)/shard_map/ppermute | solution.py:779
  39.9 12.9 %collective-permute-start.10 = (f32[432,128]{1,0:T(8,128)S(1)}, f32[432,128]{1,0:T(8,128)S(1)}, u32[]{:S(2)}, u32[]{:S(2)}) collective-permute-start(f32[432,128]{1,0:T(8,128)S(1)} %get-tuple-element.69), channel_id=1, source_target_pairs={{0,112},{16,32},{32,16},{48,64},{64,48},{80,96},{96,80},{112,0},{1... | collective-permute-start | bytes 663560 | tf_op jit(solution)/shard_map/ppermute | solution.py:779
  43.3 10.4 %collective-permute-start.11 = (f32[128,128]{1,0:T(8,128)S(1)}, f32[128,128]{1,0:T(8,128)S(1)}, u32[]{:S(2)}, u32[]{:S(2)}) collective-permute-start(f32[128,128]{1,0:T(8,128)S(1)} %get-tuple-element.70), channel_id=1, source_target_pairs={{0,16},{16,0},{32,48},{48,32},{64,80},{80,64},{96,112},{112,96},{1... | collective-permute-start | bytes 196616 | tf_op jit(solution)/shard_map/ppermute | solution.py:779
  45.2 9.0 %collective-permute-start.12 = (f32[128,128]{1,0:T(8,128)S(1)}, f32[128,128]{1,0:T(8,128)S(1)}, u32[]{:S(2)}, u32[]{:S(2)}) collective-permute-start(f32[128,128]{1,0:T(8,128)S(1)} %get-tuple-element.71), channel_id=1, source_target_pairs={{0,112},{16,32},{32,16},{48,64},{64,48},{80,96},{96,80},{112,0},{1... | collective-permute-start | bytes 196616 | tf_op jit(solution)/shard_map/ppermute | solution.py:779
  46.8 7.4 %copy-start.3 = (s32[4,8,256]{2,1,0:T(8,128)S(1)}, s32[4,8,256]{2,1,0:T(8,128)}, u32[]{:S(2)}) copy-start(s32[4,8,256]{2,1,0:T(8,128)} %mask.3) | copy-start | bytes 98308

commit v5 on v4

--- a/solution.py
+++ b/solution.py
@@ -455,19 +455,14 @@
     return blockage * (1.0 - m) + m
 
 
-def cut_kernel(pops_hbm, block_hbm, mask_hbm, cot_hbm, msg, pops, block, mask, cot, sems):
+def lead_kernel(out):
+    out[...] = jnp.zeros((8, 128), F32)
+
+
+def cut_kernel(pops, block, mask, cot, after, msg):
     gz = lax.axis_index("gz")
     lane = lanes()
-    z = pl.ds(pl.multiple_of(128 * (1 - gz), 128), 128)
-    copies = []
-    for n, (src, dst) in enumerate(((pops_hbm, pops), (cot_hbm, cot))):
-        copies.append(pltpu.make_async_copy(src.at[:, :, :, z], dst, sems.at[n]))
-    for n, (src, dst) in enumerate(((block_hbm, block), (mask_hbm, mask))):
-        copies.append(pltpu.make_async_copy(src.at[:, :, z], dst, sems.at[n + 2]))
-    for copy in copies:
-        copy.start()
-    for copy in copies:
-        copy.wait()
+    top = gz == 0
     for n in range(7):
         acc = jnp.zeros((8, 128), F32)
         for j in range(8):
@@ -476,12 +471,13 @@
                 break
             for x in range(4):
                 if slot == 54:
-                    edge = solid_of(block[x], mask[x])
+                    hi = solid_of(block[x, :, 128:256], mask[x, :, 128:256])
+                    lo = solid_of(block[x, :, 0:128], mask[x, :, 0:128])
                 else:
                     ref, i = (pops, slot) if slot < 27 else (cot, slot - 27)
-                    edge = ref[i, x]
+                    hi, lo = ref[i, x, :, 128:256], ref[i, x, :, 0:128]
                 at = 16 * j + 4 * x
-                moved = roll_l(edge, mod128(at + 4 - 4 * gz))
+                moved = roll_l(jnp.where(top, hi, lo), mod128(at + 4 - 4 * gz))
                 acc = jnp.where((lane >= at) & (lane < at + 4), moved, acc)
         msg[8 * n : 8 * n + 8, :] = acc
 
@@ -769,7 +765,7 @@
         **({} if in_specs is None else {"in_specs": in_specs}),
         compiler_params=pltpu.CompilerParams(vmem_limit_bytes=mib * 1024 * 1024),
         name=name,
-        cost_estimate=None if cost is None else pl.CostEstimate(flops=0, bytes_accessed=cost, transcendentals=0),
+        cost_estimate=None if cost is None else pl.CostEstimate(flops=2000 * cost if name == "lead" else 0, bytes_accessed=cost, transcendentals=0),
     )
 
 
@@ -806,11 +802,8 @@
 
 
 def body(populations, blockage, solid_mask, cotangent):
-    halves = [pltpu.VMEM((27, 4, 8, 128), F32), pltpu.VMEM((4, 8, 128), F32), pltpu.VMEM((4, 8, 128), jnp.int32), pltpu.VMEM((27, 4, 8, 128), F32)]
-    anywhere = [pl.BlockSpec(memory_space=pltpu.HBM)] * 4
-    (cut,) = call(cut_kernel, [(56, 128)], scratch=halves + [pltpu.SemaphoreType.DMA((4,))], name="cut", mib=60, in_specs=anywhere)(
-        populations, blockage, solid_mask, cotangent
-    )
+    (lead,) = call(lead_kernel, [(8, 128)], name="lead", cost=12_000_000)()
+    (cut,) = call(cut_kernel, [(56, 128)], name="cut")(populations, blockage, solid_mask, cotangent, lead)
     tx, ax, sx, *faces = call(first_kernel, [BIG, BIG, ONE, face_shape(37), face_shape(37)], name="first")(
         populations, blockage, solid_mask, cotangent, cut
     )

time: 59.5 us -> 57.5 us (0.966)
  Pallas kernels: 15.4 us -> 13.4 us
  local copies, waits for them, and re-layouts: 2.28 us -> 1.41 us
  starting transfers between devices: 25.5 us -> 26.2 us
    pallas_call x1 -> x2, Pallas kernels: 2.23 us -> 0.31 us  [the longest x1 0.31 us: body(): call(cut_kernel, [(56, 128)], name='cut')]
    ppermute x1, waiting for transfers between devices: 0.01 us -> 1.75 us  [body(): cut = lax.ppermute(cut, 'gz', [(0, 1), (1, 0)])]
    ppermute x12, waiting for transfers between devices: 15.3 us -> 13.9 us  [swap(): return lax.ppermute(x, axis, pairs)]
    unnamed x12 -> x8, local copies, waits for them, and re-layouts: 2.28 us -> 1.41 us
    ppermute x12, starting transfers between devices: 23.8 us -> 24.5 us  [swap(): return lax.ppermute(x, axis, pairs)]
  transfers between devices with their start and end apart: 13 -> 13, of which waited for: 8 -> 9; matrix products, arithmetic and copies ran while one was open for 0% -> 0% of each run, Pallas kernels for 5% -> 6%
where the time goes in v5:
time: 57.5 us; the launch traced here: 57.3 us
  starting transfers between devices  26.2 us (46%)
  waiting for transfers between devices  15.6 us (27%)
  Pallas kernels  13.4 us (23%)
  local copies, waits for them, and re-layouts  1.41 us (2%)
  between operations  0.74 us (1%)
    ppermute x12, starting transfers between devices, swap(): return lax.ppermute(x, axis, pairs)  24.5 us
    ppermute x12, waiting for transfers between devices, swap(): return lax.ppermute(x, axis, pairs)  13.9 us
    pallas_call x1, Pallas kernels, body(): call(last_kernel, [populations.shape, blockage.shape], scratch=[BIG, HALO...  4.92 us
    pallas_call x1, Pallas kernels, body(): call(middle_kernel, [BIG, STRIP, BIG, (4, ROWS, 128), (4, 4, 16, 128), (4...  4.79 us
    ppermute x1, waiting for transfers between devices, body(): cut = lax.ppermute(cut, 'gz', [(0, 1), (1, 0)])  1.75 us
    ppermute x1, starting transfers between devices, body(): cut = lax.ppermute(cut, 'gz', [(0, 1), (1, 0)])  1.65 us
    unnamed x8, local copies, waits for them, and re-layouts  1.41 us
    pallas_call x1, Pallas kernels, body(): call(inner_kernel, [QUAD, QUAD, (4, 32, 128), QUAD], scratch=[BIG, BIG, H...  1.18 us
  transfers between devices with their start and end apart: 13, of which 9 were waited for; matrix products, arithmetic and copies ran while one was open for 0% of the time, Pallas kernels for 6%

profile of v5, /device:TPU:0, one launch (start us, length us, event | category | flops | bytes accessed | tf_op | source)
XLA Modules:
  0.0 57.3 jit_solution(4936932295249282798)
XLA Ops:
  0.6 0.0 copy-start.2
  0.6 0.0 copy-start
  0.7 0.0 copy-start.1
  0.7 0.0 copy-start.3
  0.7 0.7 %copy-done.2 = s32[4,8,256]{2,1,0:T(8,128)S(1)} copy-done((s32[4,8,256]{2,1,0:T(8,128)S(1)}, s32[4,8,256]{2,1,0:T(8,128)}, u32[]{:S(2)}) %copy-start.2) | copy-done | bytes 32792
  1.4 0.4 copy-done
  1.8 0.3 copy-done.1
  2.1 0.0 copy-done.3
  2.1 0.3 cut.1.after
  2.4 1.7 %collective-permute-start = (f32[56,128]{1,0:T(8,128)S(1)}, f32[56,128]{1,0:T(8,128)S(1)}, u32[]{:S(2)}, u32[]{:S(2)}) collective-permute-start(f32[56,128]{1,0:T(8,128)S(1)} %cut.1.after), channel_id=1, source_target_pairs={{0,1},{1,0},{2,3},{3,2},{4,5},{5,4},{6,7},{7,6},{8,9},{9,8},{10,11... | collective-permute-start | bytes 86024 | tf_op jit(solution)/shard_map/ppermute | solution.py:810
  4.1 0.5 first.1
  4.6 1.8 %collective-permute-done.cut = f32[56,128]{1,0:T(8,128)S(1)} collective-permute-done((f32[56,128]{1,0:T(8,128)S(1)}, f32[56,128]{1,0:T(8,128)S(1)}, u32[]{:S(2)}, u32[]{:S(2)}) %collective-permute-start) | collective-permute-done | bytes 28704 | tf_op jit(solution)/shard_map/ppermute | solution.py:810
  6.4 0.2 strip.1
  6.6 3.2 %collective-permute-start.3 = (f32[592,128]{1,0:T(8,128)S(1)}, f32[592,128]{1,0:T(8,128)S(1)}, u32[]{:S(2)}, u32[]{:S(2)}) collective-permute-start(f32[592,128]{1,0:T(8,128)S(1)} %get-tuple-element.48), channel_id=1, source_target_pairs={{0,16},{16,0},{32,48},{48,32},{64,80},{80,64},{96,112},{112,96},{1... | collective-permute-start | bytes 909320 | tf_op jit(solution)/shard_map/ppermute | solution.py:775
  9.8 4.0 %collective-permute-start.4 = (f32[592,128]{1,0:T(8,128)S(1)}, f32[592,128]{1,0:T(8,128)S(1)}, u32[]{:S(2)}, u32[]{:S(2)}) collective-permute-start(f32[592,128]{1,0:T(8,128)S(1)} %get-tuple-element.49), channel_id=1, source_target_pairs={{0,112},{16,32},{32,16},{48,64},{64,48},{80,96},{96,80},{112,0},{1... | collective-permute-start | bytes 909320 | tf_op jit(solution)/shard_map/ppermute | solution.py:775
  13.8 0.0 collective-permute-start.1
  13.8 3.1 %collective-permute-start.2 = (f32[336,128]{1,0:T(8,128)S(1)}, f32[336,128]{1,0:T(8,128)S(1)}, u32[]{:S(2)}, u32[]{:S(2)}) collective-permute-start(f32[336,128]{1,0:T(8,128)S(1)} %get-tuple-element.45), channel_id=1, source_target_pairs={{0,14},{2,4},{4,2},{6,8},{8,6},{10,12},{12,10},{14,0},{1,15},{3,5}... | collective-permute-start | bytes 516104 | tf_op jit(solution)/shard_map/ppermute | solution.py:775
  16.9 0.0 collective-permute-done.1.got0.y0
  16.9 3.1 %collective-permute-done.2.got1.y1 = f32[336,128]{1,0:T(8,128)S(1)} collective-permute-done((f32[336,128]{1,0:T(8,128)S(1)}, f32[336,128]{1,0:T(8,128)S(1)}, u32[]{:S(2)}, u32[]{:S(2)}) %collective-permute-start.2) | collective-permute-done | bytes 172064 | tf_op jit(solution)/shard_map/ppermute | solution.py:775
  20.0 0.4 edge.1
  20.4 1.0 %collective-permute-start.5 = (f32[160,128]{1,0:T(8,128)S(1)}, f32[160,128]{1,0:T(8,128)S(1)}, u32[]{:S(2)}, u32[]{:S(2)}) collective-permute-start(f32[160,128]{1,0:T(8,128)S(1)} %get-tuple-element.50), channel_id=1, source_target_pairs={{0,16},{16,0},{32,48},{48,32},{64,80},{80,64},{96,112},{112,96},{1... | collective-permute-start | bytes 245768 | tf_op jit(solution)/shard_map/ppermute | solution.py:775
  21.4 2.5 %collective-permute-start.6 = (f32[160,128]{1,0:T(8,128)S(1)}, f32[160,128]{1,0:T(8,128)S(1)}, u32[]{:S(2)}, u32[]{:S(2)}) collective-permute-start(f32[160,128]{1,0:T(8,128)S(1)} %get-tuple-element.51), channel_id=1, source_target_pairs={{0,112},{16,32},{32,16},{48,64},{64,48},{80,96},{96,80},{112,0},{1... | collective-permute-start | bytes 245768 | tf_op jit(solution)/shard_map/ppermute | solution.py:775
  23.8 1.2 %inner.1 = (f32[27,32,128]{2,1,0:T(8,128)S(1)}, f32[27,32,128]{2,1,0:T(8,128)S(1)}, f32[4,32,128]{2,1,0:T(8,128)S(1)}, f32[27,32,128]{2,1,0:T(8,128)S(1)}) custom-call(f32[27,144,128]{2,1,0:T(8,128)S(1)} %get-tuple-element.38.tx, f32[27,144,128]{2,1,0:T(8,128)S(1)} %get-tuple-element.39.ax, f32[1,144,128]{2,1,0:T(8,128)S(1)} %get-tuple-element.40.sx, ...), custom_call_target="tpu_custom_call" | custom-call | bytes 6000000 | tf_op jit(solution)/shard_map/inner/pallas_call | solution.py:819
  25.0 1.9 %collective-permute-done.5.e0 = f32[160,128]{1,0:T(8,128)S(1)} collective-permute-done((f32[160,128]{1,0:T(8,128)S(1)}, f32[160,128]{1,0:T(8,128)S(1)}, u32[]{:S(2)}, u32[]{:S(2)}) %collective-permute-start.5) | collective-permute-done | bytes 81952 | tf_op jit(solution)/shard_map/ppermute | solution.py:775
  26.9 2.6 %collective-permute-done.6.e1 = f32[160,128]{1,0:T(8,128)S(1)} collective-permute-done((f32[160,128]{1,0:T(8,128)S(1)}, f32[160,128]{1,0:T(8,128)S(1)}, u32[]{:S(2)}, u32[]{:S(2)}) %collective-permute-start.6) | collective-permute-done | bytes 81952 | tf_op jit(solution)/shard_map/ppermute | solution.py:775
  29.5 0.0 collective-permute-done.3.x0
  29.5 0.0 collective-permute-done.4.x1
  29.5 4.8 %middle.1 = (f32[27,144,128]{2,1,0:T(8,128)S(1)}, f32[27,8,128]{2,1,0:T(8,128)S(1)}, f32[27,144,128]{2,1,0:T(8,128)S(1)}, f32[4,144,128]{2,1,0:T(8,128)S(1)}, f3...) custom-call(f32[27,144,128]{2,1,0:T(8,128)S(1)} %get-tuple-element.3, ...), custom_call_target="tpu_custom_call" | custom-call | tf_op jit(solution)/shard_map/middle/pallas_call | solution.py:827
  34.3 0.1 collective-permute-start.7
  34.4 3.1 %collective-permute-start.8 = (f32[440,128]{1,0:T(8,128)S(1)}, f32[440,128]{1,0:T(8,128)S(1)}, u32[]{:S(2)}, u32[]{:S(2)}) collective-permute-start(f32[440,128]{1,0:T(8,128)S(1)} %get-tuple-element.67), channel_id=1, source_target_pairs={{0,14},{2,4},{4,2},{6,8},{8,6},{10,12},{12,10},{14,0},{1,15},{3,5}... | collective-permute-start | bytes 675848 | tf_op jit(solution)/shard_map/ppermute | solution.py:775
  37.5 0.7 %collective-permute-start.9 = (f32[432,128]{1,0:T(8,128)S(1)}, f32[432,128]{1,0:T(8,128)S(1)}, u32[]{:S(2)}, u32[]{:S(2)}) collective-permute-start(f32[432,128]{1,0:T(8,128)S(1)} %get-tuple-element.68), channel_id=1, source_target_pairs={{0,16},{16,0},{32,48},{48,32},{64,80},{80,64},{96,112},{112,96},{1... | collective-permute-start | bytes 663560 | tf_op jit(solution)/shard_map/ppermute | solution.py:775
  38.1 2.8 %collective-permute-start.10 = (f32[432,128]{1,0:T(8,128)S(1)}, f32[432,128]{1,0:T(8,128)S(1)}, u32[]{:S(2)}, u32[]{:S(2)}) collective-permute-start(f32[432,128]{1,0:T(8,128)S(1)} %get-tuple-element.69), channel_id=1, source_target_pairs={{0,112},{16,32},{32,16},{48,64},{64,48},{80,96},{96,80},{112,0},{1... | collective-permute-start | bytes 663560 | tf_op jit(solution)/shard_map/ppermute | solution.py:775
  40.9 0.0 collective-permute-done.7.got0.y0
  40.9 0.2 collective-permute-done.8.got1.y1
  41.1 0.3 edge2.1
  41.4 2.1 %collective-permute-start.11 = (f32[128,128]{1,0:T(8,128)S(1)}, f32[128,128]{1,0:T(8,128)S(1)}, u32[]{:S(2)}, u32[]{:S(2)}) collective-permute-start(f32[128,128]{1,0:T(8,128)S(1)} %get-tuple-element.70), channel_id=1, source_target_pairs={{0,16},{16,0},{32,48},{48,32},{64,80},{80,64},{96,112},{112,96},{1... | collective-permute-start | bytes 196616 | tf_op jit(solution)/shard_map/ppermute | solution.py:775
  43.5 2.0 %collective-permute-start.12 = (f32[128,128]{1,0:T(8,128)S(1)}, f32[128,128]{1,0:T(8,128)S(1)}, u32[]{:S(2)}, u32[]{:S(2)}) collective-permute-start(f32[128,128]{1,0:T(8,128)S(1)} %get-tuple-element.71), channel_id=1, source_target_pairs={{0,112},{16,32},{32,16},{48,64},{64,48},{80,96},{96,80},{112,0},{1... | collective-permute-start | bytes 196616 | tf_op jit(solution)/shard_map/ppermute | solution.py:775
  45.6 0.8 %inner2.1 = (f32[27,32,128]{2,1,0:T(8,128)S(1)}, f32[1,32,128]{2,1,0:T(8,128)S(1)}) custom-call(f32[27,144,128]{2,1,0:T(8,128)S(1)} %get-tuple-element.56.a2, f32[27,8,128]{2,1,0:T(8,128)S(1)} %get-tuple-element.57.tm.a2m, f32[27,144,128]{2,1,0:T(8,128)S(1)} %get-tuple-element.58.f1, f32[4,144,128]{2,1,0:T(8,128)S(1)} %get-tuple-element.59.u_own, ...), custom_call_target="tpu_custom_call" | custom-call | bytes 6000000 | tf_op jit(solution)/shard_map/inner2/pallas_call | solution.py:840
  46.4 1.0 %collective-permute-done.9.x0 = f32[432,128]{1,0:T(8,128)S(1)} collective-permute-done((f32[432,128]{1,0:T(8,128)S(1)}, f32[432,128]{1,0:T(8,128)S(1)}, u32[]{:S(2)}, u32[]{:S(2)}) %collective-permute-start.9) | collective-permute-done | bytes 221216 | tf_op jit(solution)/shard_map/ppermute | solution.py:775
  47.3 3.7 %collective-permute-done.10.x1 = f32[432,128]{1,0:T(8,128)S(1)} collective-permute-done((f32[432,128]{1,0:T(8,128)S(1)}, f32[432,128]{1,0:T(8,128)S(1)}, u32[]{:S(2)}, u32[]{:S(2)}) %collective-permute-start.10) | collective-permute-done | bytes 221216 | tf_op jit(solution)/shard_map/ppermute | solution.py:775
  51.0 0.9 %collective-permute-done.11.e0 = f32[128,128]{1,0:T(8,128)S(1)} collective-permute-done((f32[128,128]{1,0:T(8,128)S(1)}, f32[128,128]{1,0:T(8,128)S(1)}, u32[]{:S(2)}, u32[]{:S(2)}) %collective-permute-start.11) | collective-permute-done | bytes 65568 | tf_op jit(solution)/shard_map/ppermute | solution.py:775
  51.9 0.5 collective-permute-done.12.e1
  52.4 4.9 %last.1 = (f32[27,4,8,256]{3,2,1,0:T(8,128)}, f32[4,8,256]{2,1,0:T(8,128)}) custom-call(f32[27,144,128]{2,1,0:T(8,128)S(1)} %get-tuple-element.56.a2, f32[27,8,128]{2,1,0:T(8,128)S(1)} %get-tuple-element.57.tm.a2m, f32[27,4,8,256]{3,2,1,0:T(8,128)S(1)} %copy-done, s32[4,8,256]{2,1,0:T(8,128)S(1)} %copy-done.2, f32[27,144,128]{2,1,0:T(8,128)S(1)} %get-tuple-element.58.f1, ...), custom_call_target="tpu_custom_call" | custom-call | tf_op jit(solution)/shard_map/last/pallas_call | solution.py:843
  (1 shorter events, 0.0 us)
Async XLA Ops:
  0.6 0.8 %copy-start.2 = (s32[4,8,256]{2,1,0:T(8,128)S(1)}, s32[4,8,256]{2,1,0:T(8,128)}, u32[]{:S(2)}) copy-start(s32[4,8,256]{2,1,0:T(8,128)} %mask.5) | copy-start | bytes 98308
  0.6 1.2 %copy-start = (f32[27,4,8,256]{3,2,1,0:T(8,128)S(1)}, f32[27,4,8,256]{3,2,1,0:T(8,128)}, u32[]{:S(2)}) copy-start(f32[27,4,8,256]{3,2,1,0:T(8,128)} %pops.5) | copy-start | bytes 2654212
  0.7 1.4 %copy-start.1 = (f32[27,4,8,256]{3,2,1,0:T(8,128)S(1)}, f32[27,4,8,256]{3,2,1,0:T(8,128)}, u32[]{:S(2)}) copy-start(f32[27,4,8,256]{3,2,1,0:T(8,128)} %cot.3) | copy-start | bytes 2654212
  0.7 1.4 %copy-start.3 = (f32[4,8,256]{2,1,0:T(8,128)S(1)}, f32[4,8,256]{2,1,0:T(8,128)}, u32[]{:S(2)}) copy-start(f32[4,8,256]{2,1,0:T(8,128)} %block.3) | copy-start | bytes 98308
  2.4 4.0 %collective-permute-start = (f32[56,128]{1,0:T(8,128)S(1)}, f32[56,128]{1,0:T(8,128)S(1)}, u32[]{:S(2)}, u32[]{:S(2)}) collective-permute-start(f32[56,128]{1,0:T(8,128)S(1)} %cut.1.after), channel_id=1, source_target_pairs={{0,1},{1,0},{2,3},{3,2},{4,5},{5,4},{6,7},{7,6},{8,9},{9,8},{10,11... | collective-permute-start | bytes 86024 | tf_op jit(solution)/shard_map/ppermute | solution.py:810
  6.6 22.9 %collective-permute-start.3 = (f32[592,128]{1,0:T(8,128)S(1)}, f32[592,128]{1,0:T(8,128)S(1)}, u32[]{:S(2)}, u32[]{:S(2)}) collective-permute-start(f32[592,128]{1,0:T(8,128)S(1)} %get-tuple-element.48), channel_id=1, source_target_pairs={{0,16},{16,0},{32,48},{48,32},{64,80},{80,64},{96,112},{112,96},{1... | collective-permute-start | bytes 909320 | tf_op jit(solution)/shard_map/ppermute | solution.py:775
  9.8 19.7 %collective-permute-start.4 = (f32[592,128]{1,0:T(8,128)S(1)}, f32[592,128]{1,0:T(8,128)S(1)}, u32[]{:S(2)}, u32[]{:S(2)}) collective-permute-start(f32[592,128]{1,0:T(8,128)S(1)} %get-tuple-element.49), channel_id=1, source_target_pairs={{0,112},{16,32},{32,16},{48,64},{64,48},{80,96},{96,80},{112,0},{1... | collective-permute-start | bytes 909320 | tf_op jit(solution)/shard_map/ppermute | solution.py:775
  13.8 3.1 %collective-permute-start.1 = (f32[336,128]{1,0:T(8,128)S(1)}, f32[336,128]{1,0:T(8,128)S(1)}, u32[]{:S(2)}, u32[]{:S(2)}) collective-permute-start(f32[336,128]{1,0:T(8,128)S(1)} %get-tuple-element.44), channel_id=1, source_target_pairs={{0,2},{2,0},{4,6},{6,4},{8,10},{10,8},{12,14},{14,12},{1,3},{3,1},... | collective-permute-start | bytes 516104 | tf_op jit(solution)/shard_map/ppermute | solution.py:775
  13.8 6.2 %collective-permute-start.2 = (f32[336,128]{1,0:T(8,128)S(1)}, f32[336,128]{1,0:T(8,128)S(1)}, u32[]{:S(2)}, u32[]{:S(2)}) collective-permute-start(f32[336,128]{1,0:T(8,128)S(1)} %get-tuple-element.45), channel_id=1, source_target_pairs={{0,14},{2,4},{4,2},{6,8},{8,6},{10,12},{12,10},{14,0},{1,15},{3,5}... | collective-permute-start | bytes 516104 | tf_op jit(solution)/shard_map/ppermute | solution.py:775
  20.4 6.6 %collective-permute-start.5 = (f32[160,128]{1,0:T(8,128)S(1)}, f32[160,128]{1,0:T(8,128)S(1)}, u32[]{:S(2)}, u32[]{:S(2)}) collective-permute-start(f32[160,128]{1,0:T(8,128)S(1)} %get-tuple-element.50), channel_id=1, source_target_pairs={{0,16},{16,0},{32,48},{48,32},{64,80},{80,64},{96,112},{112,96},{1... | collective-permute-start | bytes 245768 | tf_op jit(solution)/shard_map/ppermute | solution.py:775
  21.4 8.2 %collective-permute-start.6 = (f32[160,128]{1,0:T(8,128)S(1)}, f32[160,128]{1,0:T(8,128)S(1)}, u32[]{:S(2)}, u32[]{:S(2)}) collective-permute-start(f32[160,128]{1,0:T(8,128)S(1)} %get-tuple-element.51), channel_id=1, source_target_pairs={{0,112},{16,32},{32,16},{48,64},{64,48},{80,96},{96,80},{112,0},{1... | collective-permute-start | bytes 245768 | tf_op jit(solution)/shard_map/ppermute | solution.py:775
  34.3 6.6 %collective-permute-start.7 = (f32[440,128]{1,0:T(8,128)S(1)}, f32[440,128]{1,0:T(8,128)S(1)}, u32[]{:S(2)}, u32[]{:S(2)}) collective-permute-start(f32[440,128]{1,0:T(8,128)S(1)} %get-tuple-element.66), channel_id=1, source_target_pairs={{0,2},{2,0},{4,6},{6,4},{8,10},{10,8},{12,14},{14,12},{1,3},{3,1},... | collective-permute-start | bytes 675848 | tf_op jit(solution)/shard_map/ppermute | solution.py:775
  34.4 6.7 %collective-permute-start.8 = (f32[440,128]{1,0:T(8,128)S(1)}, f32[440,128]{1,0:T(8,128)S(1)}, u32[]{:S(2)}, u32[]{:S(2)}) collective-permute-start(f32[440,128]{1,0:T(8,128)S(1)} %get-tuple-element.67), channel_id=1, source_target_pairs={{0,14},{2,4},{4,2},{6,8},{8,6},{10,12},{12,10},{14,0},{1,15},{3,5}... | collective-permute-start | bytes 675848 | tf_op jit(solution)/shard_map/ppermute | solution.py:775
  37.5 9.9 %collective-permute-start.9 = (f32[432,128]{1,0:T(8,128)S(1)}, f32[432,128]{1,0:T(8,128)S(1)}, u32[]{:S(2)}, u32[]{:S(2)}) collective-permute-start(f32[432,128]{1,0:T(8,128)S(1)} %get-tuple-element.68), channel_id=1, source_target_pairs={{0,16},{16,0},{32,48},{48,32},{64,80},{80,64},{96,112},{112,96},{1... | collective-permute-start | bytes 663560 | tf_op jit(solution)/shard_map/ppermute | solution.py:775
  38.1 12.9 %collective-permute-start.10 = (f32[432,128]{1,0:T(8,128)S(1)}, f32[432,128]{1,0:T(8,128)S(1)}, u32[]{:S(2)}, u32[]{:S(2)}) collective-permute-start(f32[432,128]{1,0:T(8,128)S(1)} %get-tuple-element.69), channel_id=1, source_target_pairs={{0,112},{16,32},{32,16},{48,64},{64,48},{80,96},{96,80},{112,0},{1... | collective-permute-start | bytes 663560 | tf_op jit(solution)/shard_map/ppermute | solution.py:775
  41.4 10.5 %collective-permute-start.11 = (f32[128,128]{1,0:T(8,128)S(1)}, f32[128,128]{1,0:T(8,128)S(1)}, u32[]{:S(2)}, u32[]{:S(2)}) collective-permute-start(f32[128,128]{1,0:T(8,128)S(1)} %get-tuple-element.70), channel_id=1, source_target_pairs={{0,16},{16,0},{32,48},{48,32},{64,80},{80,64},{96,112},{112,96},{1... | collective-permute-start | bytes 196616 | tf_op jit(solution)/shard_map/ppermute | solution.py:775
  43.5 8.9 %collective-permute-start.12 = (f32[128,128]{1,0:T(8,128)S(1)}, f32[128,128]{1,0:T(8,128)S(1)}, u32[]{:S(2)}, u32[]{:S(2)}) collective-permute-start(f32[128,128]{1,0:T(8,128)S(1)} %get-tuple-element.71), channel_id=1, source_target_pairs={{0,112},{16,32},{32,16},{48,64},{64,48},{80,96},{96,80},{112,0},{1... | collective-permute-start | bytes 196616 | tf_op jit(solution)/shard_map/ppermute | solution.py:775

commit v6 on v5

--- a/solution.py
+++ b/solution.py
@@ -725,7 +725,15 @@
         q1[0, here, :] = blame
         return carry
 
-    lax.fori_loop(0, 9, again, 0)
+    def again_outside(k, carry):
+        here = outer_tile(jnp.where(k < 2, k, k + 4))
+        out, _ = pull_back([p[i, here, :] for i in range(27)], s_own[0, here, :], [u_own[n, here, :] for n in (1, 2, 3)])
+        for i in range(27):
+            c[i, here, :] = out[i]
+        return carry
+
+    lax.fori_loop(2, 6, again, 0)
+    lax.fori_loop(0, 5, again_outside, 0)
 
     def again_rows(k, carry):
         for half in (0, 1):

time: 57.5 us -> 57.4 us (level)
  no operation moved by 1% of the time
where the time goes in v6:
time: 57.4 us; the launch traced here: 57.2 us
  starting transfers between devices  26.2 us (46%)
  waiting for transfers between devices  15.6 us (27%)
  Pallas kernels  13.3 us (23%)
  local copies, waits for them, and re-layouts  1.41 us (2%)
  between operations  0.74 us (1%)
    ppermute x12, starting transfers between devices, swap(): return lax.ppermute(x, axis, pairs)  24.5 us
    ppermute x12, waiting for transfers between devices, swap(): return lax.ppermute(x, axis, pairs)  13.9 us
    pallas_call x1, Pallas kernels, body(): call(last_kernel, [populations.shape, blockage.shape], scratch=[BIG, HALO...  4.83 us
    pallas_call x1, Pallas kernels, body(): call(middle_kernel, [BIG, STRIP, BIG, (4, ROWS, 128), (4, 4, 16, 128), (4...  4.79 us
    ppermute x1, waiting for transfers between devices, body(): cut = lax.ppermute(cut, 'gz', [(0, 1), (1, 0)])  1.75 us
    ppermute x1, starting transfers between devices, body(): cut = lax.ppermute(cut, 'gz', [(0, 1), (1, 0)])  1.65 us
    unnamed x8, local copies, waits for them, and re-layouts  1.41 us
    pallas_call x1, Pallas kernels, body(): call(inner_kernel, [QUAD, QUAD, (4, 32, 128), QUAD], scratch=[BIG, BIG, H...  1.18 us
  transfers between devices with their start and end apart: 13, of which 9 were waited for; matrix products, arithmetic and copies ran while one was open for 0% of the time, Pallas kernels for 6%

profile of v6, /device:TPU:0, one launch (start us, length us, event | category | flops | bytes accessed | tf_op | source)
XLA Modules:
  0.0 57.2 jit_solution(10016955219300059788)
XLA Ops:
  0.6 0.0 copy-start.2
  0.6 0.0 copy-start
  0.7 0.0 copy-start.1
  0.7 0.0 copy-start.3
  0.7 0.7 %copy-done.2 = s32[4,8,256]{2,1,0:T(8,128)S(1)} copy-done((s32[4,8,256]{2,1,0:T(8,128)S(1)}, s32[4,8,256]{2,1,0:T(8,128)}, u32[]{:S(2)}) %copy-start.2) | copy-done | bytes 32792
  1.4 0.4 copy-done
  1.8 0.3 copy-done.1
  2.1 0.0 copy-done.3
  2.1 0.3 cut.1.after
  2.4 1.7 %collective-permute-start = (f32[56,128]{1,0:T(8,128)S(1)}, f32[56,128]{1,0:T(8,128)S(1)}, u32[]{:S(2)}, u32[]{:S(2)}) collective-permute-start(f32[56,128]{1,0:T(8,128)S(1)} %cut.1.after), channel_id=1, source_target_pairs={{0,1},{1,0},{2,3},{3,2},{4,5},{5,4},{6,7},{7,6},{8,9},{9,8},{10,11... | collective-permute-start | bytes 86024 | tf_op jit(solution)/shard_map/ppermute | solution.py:818
  4.1 0.5 first.1
  4.6 1.8 %collective-permute-done.cut = f32[56,128]{1,0:T(8,128)S(1)} collective-permute-done((f32[56,128]{1,0:T(8,128)S(1)}, f32[56,128]{1,0:T(8,128)S(1)}, u32[]{:S(2)}, u32[]{:S(2)}) %collective-permute-start) | collective-permute-done | bytes 28704 | tf_op jit(solution)/shard_map/ppermute | solution.py:818
  6.4 0.2 strip.1
  6.6 3.2 %collective-permute-start.3 = (f32[592,128]{1,0:T(8,128)S(1)}, f32[592,128]{1,0:T(8,128)S(1)}, u32[]{:S(2)}, u32[]{:S(2)}) collective-permute-start(f32[592,128]{1,0:T(8,128)S(1)} %get-tuple-element.48), channel_id=1, source_target_pairs={{0,16},{16,0},{32,48},{48,32},{64,80},{80,64},{96,112},{112,96},{1... | collective-permute-start | bytes 909320 | tf_op jit(solution)/shard_map/ppermute | solution.py:783
  9.8 4.0 %collective-permute-start.4 = (f32[592,128]{1,0:T(8,128)S(1)}, f32[592,128]{1,0:T(8,128)S(1)}, u32[]{:S(2)}, u32[]{:S(2)}) collective-permute-start(f32[592,128]{1,0:T(8,128)S(1)} %get-tuple-element.49), channel_id=1, source_target_pairs={{0,112},{16,32},{32,16},{48,64},{64,48},{80,96},{96,80},{112,0},{1... | collective-permute-start | bytes 909320 | tf_op jit(solution)/shard_map/ppermute | solution.py:783
  13.8 0.0 collective-permute-start.1
  13.8 3.1 %collective-permute-start.2 = (f32[336,128]{1,0:T(8,128)S(1)}, f32[336,128]{1,0:T(8,128)S(1)}, u32[]{:S(2)}, u32[]{:S(2)}) collective-permute-start(f32[336,128]{1,0:T(8,128)S(1)} %get-tuple-element.45), channel_id=1, source_target_pairs={{0,14},{2,4},{4,2},{6,8},{8,6},{10,12},{12,10},{14,0},{1,15},{3,5}... | collective-permute-start | bytes 516104 | tf_op jit(solution)/shard_map/ppermute | solution.py:783
  16.9 0.0 collective-permute-done.1.got0.y0
  16.9 3.1 %collective-permute-done.2.got1.y1 = f32[336,128]{1,0:T(8,128)S(1)} collective-permute-done((f32[336,128]{1,0:T(8,128)S(1)}, f32[336,128]{1,0:T(8,128)S(1)}, u32[]{:S(2)}, u32[]{:S(2)}) %collective-permute-start.2) | collective-permute-done | bytes 172064 | tf_op jit(solution)/shard_map/ppermute | solution.py:783
  20.0 0.4 edge.1
  20.4 1.0 %collective-permute-start.5 = (f32[160,128]{1,0:T(8,128)S(1)}, f32[160,128]{1,0:T(8,128)S(1)}, u32[]{:S(2)}, u32[]{:S(2)}) collective-permute-start(f32[160,128]{1,0:T(8,128)S(1)} %get-tuple-element.50), channel_id=1, source_target_pairs={{0,16},{16,0},{32,48},{48,32},{64,80},{80,64},{96,112},{112,96},{1... | collective-permute-start | bytes 245768 | tf_op jit(solution)/shard_map/ppermute | solution.py:783
  21.4 2.5 %collective-permute-start.6 = (f32[160,128]{1,0:T(8,128)S(1)}, f32[160,128]{1,0:T(8,128)S(1)}, u32[]{:S(2)}, u32[]{:S(2)}) collective-permute-start(f32[160,128]{1,0:T(8,128)S(1)} %get-tuple-element.51), channel_id=1, source_target_pairs={{0,112},{16,32},{32,16},{48,64},{64,48},{80,96},{96,80},{112,0},{1... | collective-permute-start | bytes 245768 | tf_op jit(solution)/shard_map/ppermute | solution.py:783
  23.8 1.2 %inner.1 = (f32[27,32,128]{2,1,0:T(8,128)S(1)}, f32[27,32,128]{2,1,0:T(8,128)S(1)}, f32[4,32,128]{2,1,0:T(8,128)S(1)}, f32[27,32,128]{2,1,0:T(8,128)S(1)}) custom-call(f32[27,144,128]{2,1,0:T(8,128)S(1)} %get-tuple-element.38.tx, f32[27,144,128]{2,1,0:T(8,128)S(1)} %get-tuple-element.39.ax, f32[1,144,128]{2,1,0:T(8,128)S(1)} %get-tuple-element.40.sx, ...), custom_call_target="tpu_custom_call" | custom-call | bytes 6000000 | tf_op jit(solution)/shard_map/inner/pallas_call | solution.py:827
  25.0 1.9 %collective-permute-done.5.e0 = f32[160,128]{1,0:T(8,128)S(1)} collective-permute-done((f32[160,128]{1,0:T(8,128)S(1)}, f32[160,128]{1,0:T(8,128)S(1)}, u32[]{:S(2)}, u32[]{:S(2)}) %collective-permute-start.5) | collective-permute-done | bytes 81952 | tf_op jit(solution)/shard_map/ppermute | solution.py:783
  26.9 2.6 %collective-permute-done.6.e1 = f32[160,128]{1,0:T(8,128)S(1)} collective-permute-done((f32[160,128]{1,0:T(8,128)S(1)}, f32[160,128]{1,0:T(8,128)S(1)}, u32[]{:S(2)}, u32[]{:S(2)}) %collective-permute-start.6) | collective-permute-done | bytes 81952 | tf_op jit(solution)/shard_map/ppermute | solution.py:783
  29.5 0.0 collective-permute-done.3.x0
  29.5 0.0 collective-permute-done.4.x1
  29.5 4.8 %middle.1 = (f32[27,144,128]{2,1,0:T(8,128)S(1)}, f32[27,8,128]{2,1,0:T(8,128)S(1)}, f32[27,144,128]{2,1,0:T(8,128)S(1)}, f32[4,144,128]{2,1,0:T(8,128)S(1)}, f3...) custom-call(f32[27,144,128]{2,1,0:T(8,128)S(1)} %get-tuple-element.3, ...), custom_call_target="tpu_custom_call" | custom-call | tf_op jit(solution)/shard_map/middle/pallas_call | solution.py:835
  34.3 0.1 collective-permute-start.7
  34.4 3.1 %collective-permute-start.8 = (f32[440,128]{1,0:T(8,128)S(1)}, f32[440,128]{1,0:T(8,128)S(1)}, u32[]{:S(2)}, u32[]{:S(2)}) collective-permute-start(f32[440,128]{1,0:T(8,128)S(1)} %get-tuple-element.67), channel_id=1, source_target_pairs={{0,14},{2,4},{4,2},{6,8},{8,6},{10,12},{12,10},{14,0},{1,15},{3,5}... | collective-permute-start | bytes 675848 | tf_op jit(solution)/shard_map/ppermute | solution.py:783
  37.5 0.7 %collective-permute-start.9 = (f32[432,128]{1,0:T(8,128)S(1)}, f32[432,128]{1,0:T(8,128)S(1)}, u32[]{:S(2)}, u32[]{:S(2)}) collective-permute-start(f32[432,128]{1,0:T(8,128)S(1)} %get-tuple-element.68), channel_id=1, source_target_pairs={{0,16},{16,0},{32,48},{48,32},{64,80},{80,64},{96,112},{112,96},{1... | collective-permute-start | bytes 663560 | tf_op jit(solution)/shard_map/ppermute | solution.py:783
  38.1 2.8 %collective-permute-start.10 = (f32[432,128]{1,0:T(8,128)S(1)}, f32[432,128]{1,0:T(8,128)S(1)}, u32[]{:S(2)}, u32[]{:S(2)}) collective-permute-start(f32[432,128]{1,0:T(8,128)S(1)} %get-tuple-element.69), channel_id=1, source_target_pairs={{0,112},{16,32},{32,16},{48,64},{64,48},{80,96},{96,80},{112,0},{1... | collective-permute-start | bytes 663560 | tf_op jit(solution)/shard_map/ppermute | solution.py:783
  40.9 0.0 collective-permute-done.7.got0.y0
  40.9 0.2 collective-permute-done.8.got1.y1
  41.1 0.3 edge2.1
  41.4 2.1 %collective-permute-start.11 = (f32[128,128]{1,0:T(8,128)S(1)}, f32[128,128]{1,0:T(8,128)S(1)}, u32[]{:S(2)}, u32[]{:S(2)}) collective-permute-start(f32[128,128]{1,0:T(8,128)S(1)} %get-tuple-element.70), channel_id=1, source_target_pairs={{0,16},{16,0},{32,48},{48,32},{64,80},{80,64},{96,112},{112,96},{1... | collective-permute-start | bytes 196616 | tf_op jit(solution)/shard_map/ppermute | solution.py:783
  43.5 2.0 %collective-permute-start.12 = (f32[128,128]{1,0:T(8,128)S(1)}, f32[128,128]{1,0:T(8,128)S(1)}, u32[]{:S(2)}, u32[]{:S(2)}) collective-permute-start(f32[128,128]{1,0:T(8,128)S(1)} %get-tuple-element.71), channel_id=1, source_target_pairs={{0,112},{16,32},{32,16},{48,64},{64,48},{80,96},{96,80},{112,0},{1... | collective-permute-start | bytes 196616 | tf_op jit(solution)/shard_map/ppermute | solution.py:783
  45.6 0.8 %inner2.1 = (f32[27,32,128]{2,1,0:T(8,128)S(1)}, f32[1,32,128]{2,1,0:T(8,128)S(1)}) custom-call(f32[27,144,128]{2,1,0:T(8,128)S(1)} %get-tuple-element.56.a2, f32[27,8,128]{2,1,0:T(8,128)S(1)} %get-tuple-element.57.tm.a2m, f32[27,144,128]{2,1,0:T(8,128)S(1)} %get-tuple-element.58.f1, f32[4,144,128]{2,1,0:T(8,128)S(1)} %get-tuple-element.59.u_own, ...), custom_call_target="tpu_custom_call" | custom-call | bytes 6000000 | tf_op jit(solution)/shard_map/inner2/pallas_call | solution.py:848
  46.4 1.0 %collective-permute-done.9.x0 = f32[432,128]{1,0:T(8,128)S(1)} collective-permute-done((f32[432,128]{1,0:T(8,128)S(1)}, f32[432,128]{1,0:T(8,128)S(1)}, u32[]{:S(2)}, u32[]{:S(2)}) %collective-permute-start.9) | collective-permute-done | bytes 221216 | tf_op jit(solution)/shard_map/ppermute | solution.py:783
  47.3 3.7 %collective-permute-done.10.x1 = f32[432,128]{1,0:T(8,128)S(1)} collective-permute-done((f32[432,128]{1,0:T(8,128)S(1)}, f32[432,128]{1,0:T(8,128)S(1)}, u32[]{:S(2)}, u32[]{:S(2)}) %collective-permute-start.10) | collective-permute-done | bytes 221216 | tf_op jit(solution)/shard_map/ppermute | solution.py:783
  51.0 0.9 %collective-permute-done.11.e0 = f32[128,128]{1,0:T(8,128)S(1)} collective-permute-done((f32[128,128]{1,0:T(8,128)S(1)}, f32[128,128]{1,0:T(8,128)S(1)}, u32[]{:S(2)}, u32[]{:S(2)}) %collective-permute-start.11) | collective-permute-done | bytes 65568 | tf_op jit(solution)/shard_map/ppermute | solution.py:783
  51.9 0.5 collective-permute-done.12.e1
  52.4 4.8 %last.1 = (f32[27,4,8,256]{3,2,1,0:T(8,128)}, f32[4,8,256]{2,1,0:T(8,128)}) custom-call(f32[27,144,128]{2,1,0:T(8,128)S(1)} %get-tuple-element.56.a2, f32[27,8,128]{2,1,0:T(8,128)S(1)} %get-tuple-element.57.tm.a2m, f32[27,4,8,256]{3,2,1,0:T(8,128)S(1)} %copy-done, s32[4,8,256]{2,1,0:T(8,128)S(1)} %copy-done.2, f32[27,144,128]{2,1,0:T(8,128)S(1)} %get-tuple-element.58.f1, ...), custom_call_target="tpu_custom_call" | custom-call | tf_op jit(solution)/shard_map/last/pallas_call | solution.py:851
  (1 shorter events, 0.0 us)
Async XLA Ops:
  0.6 0.8 %copy-start.2 = (s32[4,8,256]{2,1,0:T(8,128)S(1)}, s32[4,8,256]{2,1,0:T(8,128)}, u32[]{:S(2)}) copy-start(s32[4,8,256]{2,1,0:T(8,128)} %mask.5) | copy-start | bytes 98308
  0.6 1.2 %copy-start = (f32[27,4,8,256]{3,2,1,0:T(8,128)S(1)}, f32[27,4,8,256]{3,2,1,0:T(8,128)}, u32[]{:S(2)}) copy-start(f32[27,4,8,256]{3,2,1,0:T(8,128)} %pops.5) | copy-start | bytes 2654212
  0.7 1.4 %copy-start.1 = (f32[27,4,8,256]{3,2,1,0:T(8,128)S(1)}, f32[27,4,8,256]{3,2,1,0:T(8,128)}, u32[]{:S(2)}) copy-start(f32[27,4,8,256]{3,2,1,0:T(8,128)} %cot.3) | copy-start | bytes 2654212
  0.7 1.4 %copy-start.3 = (f32[4,8,256]{2,1,0:T(8,128)S(1)}, f32[4,8,256]{2,1,0:T(8,128)}, u32[]{:S(2)}) copy-start(f32[4,8,256]{2,1,0:T(8,128)} %block.3) | copy-start | bytes 98308
  2.4 4.0 %collective-permute-start = (f32[56,128]{1,0:T(8,128)S(1)}, f32[56,128]{1,0:T(8,128)S(1)}, u32[]{:S(2)}, u32[]{:S(2)}) collective-permute-start(f32[56,128]{1,0:T(8,128)S(1)} %cut.1.after), channel_id=1, source_target_pairs={{0,1},{1,0},{2,3},{3,2},{4,5},{5,4},{6,7},{7,6},{8,9},{9,8},{10,11... | collective-permute-start | bytes 86024 | tf_op jit(solution)/shard_map/ppermute | solution.py:818
  6.6 22.9 %collective-permute-start.3 = (f32[592,128]{1,0:T(8,128)S(1)}, f32[592,128]{1,0:T(8,128)S(1)}, u32[]{:S(2)}, u32[]{:S(2)}) collective-permute-start(f32[592,128]{1,0:T(8,128)S(1)} %get-tuple-element.48), channel_id=1, source_target_pairs={{0,16},{16,0},{32,48},{48,32},{64,80},{80,64},{96,112},{112,96},{1... | collective-permute-start | bytes 909320 | tf_op jit(solution)/shard_map/ppermute | solution.py:783
  9.8 19.7 %collective-permute-start.4 = (f32[592,128]{1,0:T(8,128)S(1)}, f32[592,128]{1,0:T(8,128)S(1)}, u32[]{:S(2)}, u32[]{:S(2)}) collective-permute-start(f32[592,128]{1,0:T(8,128)S(1)} %get-tuple-element.49), channel_id=1, source_target_pairs={{0,112},{16,32},{32,16},{48,64},{64,48},{80,96},{96,80},{112,0},{1... | collective-permute-start | bytes 909320 | tf_op jit(solution)/shard_map/ppermute | solution.py:783
  13.8 3.1 %collective-permute-start.1 = (f32[336,128]{1,0:T(8,128)S(1)}, f32[336,128]{1,0:T(8,128)S(1)}, u32[]{:S(2)}, u32[]{:S(2)}) collective-permute-start(f32[336,128]{1,0:T(8,128)S(1)} %get-tuple-element.44), channel_id=1, source_target_pairs={{0,2},{2,0},{4,6},{6,4},{8,10},{10,8},{12,14},{14,12},{1,3},{3,1},... | collective-permute-start | bytes 516104 | tf_op jit(solution)/shard_map/ppermute | solution.py:783
  13.8 6.2 %collective-permute-start.2 = (f32[336,128]{1,0:T(8,128)S(1)}, f32[336,128]{1,0:T(8,128)S(1)}, u32[]{:S(2)}, u32[]{:S(2)}) collective-permute-start(f32[336,128]{1,0:T(8,128)S(1)} %get-tuple-element.45), channel_id=1, source_target_pairs={{0,14},{2,4},{4,2},{6,8},{8,6},{10,12},{12,10},{14,0},{1,15},{3,5}... | collective-permute-start | bytes 516104 | tf_op jit(solution)/shard_map/ppermute | solution.py:783
  20.4 6.6 %collective-permute-start.5 = (f32[160,128]{1,0:T(8,128)S(1)}, f32[160,128]{1,0:T(8,128)S(1)}, u32[]{:S(2)}, u32[]{:S(2)}) collective-permute-start(f32[160,128]{1,0:T(8,128)S(1)} %get-tuple-element.50), channel_id=1, source_target_pairs={{0,16},{16,0},{32,48},{48,32},{64,80},{80,64},{96,112},{112,96},{1... | collective-permute-start | bytes 245768 | tf_op jit(solution)/shard_map/ppermute | solution.py:783
  21.4 8.2 %collective-permute-start.6 = (f32[160,128]{1,0:T(8,128)S(1)}, f32[160,128]{1,0:T(8,128)S(1)}, u32[]{:S(2)}, u32[]{:S(2)}) collective-permute-start(f32[160,128]{1,0:T(8,128)S(1)} %get-tuple-element.51), channel_id=1, source_target_pairs={{0,112},{16,32},{32,16},{48,64},{64,48},{80,96},{96,80},{112,0},{1... | collective-permute-start | bytes 245768 | tf_op jit(solution)/shard_map/ppermute | solution.py:783
  34.3 6.6 %collective-permute-start.7 = (f32[440,128]{1,0:T(8,128)S(1)}, f32[440,128]{1,0:T(8,128)S(1)}, u32[]{:S(2)}, u32[]{:S(2)}) collective-permute-start(f32[440,128]{1,0:T(8,128)S(1)} %get-tuple-element.66), channel_id=1, source_target_pairs={{0,2},{2,0},{4,6},{6,4},{8,10},{10,8},{12,14},{14,12},{1,3},{3,1},... | collective-permute-start | bytes 675848 | tf_op jit(solution)/shard_map/ppermute | solution.py:783
  34.4 6.7 %collective-permute-start.8 = (f32[440,128]{1,0:T(8,128)S(1)}, f32[440,128]{1,0:T(8,128)S(1)}, u32[]{:S(2)}, u32[]{:S(2)}) collective-permute-start(f32[440,128]{1,0:T(8,128)S(1)} %get-tuple-element.67), channel_id=1, source_target_pairs={{0,14},{2,4},{4,2},{6,8},{8,6},{10,12},{12,10},{14,0},{1,15},{3,5}... | collective-permute-start | bytes 675848 | tf_op jit(solution)/shard_map/ppermute | solution.py:783
  37.5 9.9 %collective-permute-start.9 = (f32[432,128]{1,0:T(8,128)S(1)}, f32[432,128]{1,0:T(8,128)S(1)}, u32[]{:S(2)}, u32[]{:S(2)}) collective-permute-start(f32[432,128]{1,0:T(8,128)S(1)} %get-tuple-element.68), channel_id=1, source_target_pairs={{0,16},{16,0},{32,48},{48,32},{64,80},{80,64},{96,112},{112,96},{1... | collective-permute-start | bytes 663560 | tf_op jit(solution)/shard_map/ppermute | solution.py:783
  38.1 12.9 %collective-permute-start.10 = (f32[432,128]{1,0:T(8,128)S(1)}, f32[432,128]{1,0:T(8,128)S(1)}, u32[]{:S(2)}, u32[]{:S(2)}) collective-permute-start(f32[432,128]{1,0:T(8,128)S(1)} %get-tuple-element.69), channel_id=1, source_target_pairs={{0,112},{16,32},{32,16},{48,64},{64,48},{80,96},{96,80},{112,0},{1... | collective-permute-start | bytes 663560 | tf_op jit(solution)/shard_map/ppermute | solution.py:783
  41.4 10.5 %collective-permute-start.11 = (f32[128,128]{1,0:T(8,128)S(1)}, f32[128,128]{1,0:T(8,128)S(1)}, u32[]{:S(2)}, u32[]{:S(2)}) collective-permute-start(f32[128,128]{1,0:T(8,128)S(1)} %get-tuple-element.70), channel_id=1, source_target_pairs={{0,16},{16,0},{32,48},{48,32},{64,80},{80,64},{96,112},{112,96},{1... | collective-permute-start | bytes 196616 | tf_op jit(solution)/shard_map/ppermute | solution.py:783
  43.5 8.9 %collective-permute-start.12 = (f32[128,128]{1,0:T(8,128)S(1)}, f32[128,128]{1,0:T(8,128)S(1)}, u32[]{:S(2)}, u32[]{:S(2)}) collective-permute-start(f32[128,128]{1,0:T(8,128)S(1)} %get-tuple-element.71), channel_id=1, source_target_pairs={{0,112},{16,32},{32,16},{48,64},{64,48},{80,96},{96,80},{112,0},{1... | collective-permute-start | bytes 196616 | tf_op jit(solution)/shard_map/ppermute | solution.py:783
